TPU v7x, 256 devices: a whole 4x4x8 slice. The times are simulated.
256 devices in a mesh: cell: 16 (over y, z_lo), mem: 8 (over x, core), dp: 2 (over z_hi).
Axes of the slice: x: 4, y: 4, z: 8 (z_hi: 2, z_lo: 4; z = z_hi * 4 + z_lo), core: 2. Of those that a mesh axis runs over, the one named last changes fastest.
Arguments:
- ensemble: bfloat16 [256, 524288], P('mem', 'cell'), may hold values from -6 to 6
- data_anom: bfloat16 [256, 4096], P('mem', ('cell', 'dp')), may hold values from -6 to 6
- weighted_innov: bfloat16 [256, 4096], P('mem', ('cell', 'dp')), may hold values from -12 to 12
- profiles: bfloat16 [64, 128], replicated, may hold values from 0.049804688 to 1
- seg_data: int32 [128, 4096], P(('cell', 'dp')), may hold values from -1 to 4095, as said below
- seg_profile: int32 [128, 4096], P(('cell', 'dp')), may hold values from 0 to 63
Outputs:
- updated: bfloat16 [256, 524288], P('mem', ('cell', 'dp'))
Inputs may be any that keep to these rules, and one draw needn't show every extreme that they name: `seg_data`: A slot holds -1 (empty) or a datum of its own data group: rows g * 4 to (g + 1) * 4 - 1 hold data 128 * g to 128 * (g + 1) - 1.
All inputs are finite; a program needn't handle non-finite values.
Results may differ from a plain program's by a relative error of at most 0.003.
Values may be sent and summed in bfloat16 or wider, within the bound.
No kernel may reach another device: no remote copies, remote signals or barrier semaphores. Data moves between devices by JAX's collectives and lax.ppermute only.
A program may use at most 128 MiB of HBM per device.

v0:
```python
import jax
import jax.numpy as jnp
from jax import lax
from jax.sharding import PartitionSpec as P

M = 256


def local(ensemble, data_anom, weighted_innov, profiles, seg_data, seg_profile):
    n_cell = lax.axis_size("cell")
    n_dp = lax.axis_size("dp")
    members_dev, cells_dev = ensemble.shape
    data_dev = data_anom.shape[1]
    slot_count = seg_data.shape[0]
    blocks_dev = seg_data.shape[1] // n_cell
    table_len, block_len = profiles.shape
    group_index = lax.axis_index("cell") * n_dp + lax.axis_index("dp")
    local_ids = seg_data.reshape(slot_count, n_cell, blocks_dev) - group_index * data_dev
    picker = (local_ids[None] == jnp.arange(data_dev, dtype=jnp.int32)[:, None, None, None]).astype(
        jnp.bfloat16
    )
    stacked = jnp.stack([data_anom, weighted_innov])
    columns = jnp.einsum(
        "nmd,dkqb->nmqkb", stacked, picker, preferred_element_type=jnp.float32
    ).astype(jnp.bfloat16)
    columns = columns.reshape(2 * members_dev, n_cell, slot_count, blocks_dev)
    prof_local = seg_profile.reshape(slot_count, n_cell, blocks_dev)
    chooser = (
        prof_local[None] == jnp.arange(table_len, dtype=jnp.int32)[:, None, None, None]
    ).astype(jnp.bfloat16)
    rows_sent = jnp.einsum(
        "ti,tkqb->iqkb", profiles, chooser, preferred_element_type=jnp.float32
    ).astype(jnp.bfloat16)
    got_cols, profile_rows = (
        lax.all_to_all(columns, "cell", split_axis=1, concat_axis=1, tiled=True),
        lax.all_to_all(rows_sent, "cell", split_axis=1, concat_axis=1, tiled=True),
    )
    anom_cols = got_cols[:members_dev]
    innov_cols = got_cols[members_dev:]
    state_blocks = ensemble.reshape(members_dev, blocks_dev, block_len)
    partial_prod = jnp.einsum(
        "mbi,mqkb->iqkb", state_blocks, anom_cols, preferred_element_type=jnp.float32
    )
    inner_prod = lax.psum(partial_prod, "mem")
    coefficient = (profile_rows.astype(jnp.float32) * inner_prod / (M - 1)).astype(jnp.bfloat16)
    correction = jnp.einsum(
        "iqkb,mqkb->mbi", coefficient, innov_cols, preferred_element_type=jnp.float32
    )
    correction = correction.reshape(members_dev, cells_dev)
    reduced = lax.psum_scatter(correction, "dp", scatter_dimension=1, tiled=True)
    half_len = cells_dev // n_dp
    own_state = lax.dynamic_slice_in_dim(ensemble, lax.axis_index("dp") * half_len, half_len, 1)
    return (own_state.astype(jnp.float32) + reduced).astype(jnp.bfloat16)


def solution(mesh):
    placed = (
        P("mem", "cell"),
        P("mem", ("cell", "dp")),
        P("mem", ("cell", "dp")),
        P(),
        P(("cell", "dp"), None),
        P(("cell", "dp"), None),
    )
    return jax.shard_map(
        local, mesh=mesh, in_specs=placed, out_specs=P("mem", ("cell", "dp")), check_vma=False
    )
```

profile of v0, /device:TPU:1, one launch (start us, length us, event | category | flops | bytes accessed | tf_op | source)
XLA Modules:
  0.0 333.9 jit_solution(6484901291576700012)
XLA Ops:
  6.5 0.0 copy-start
  6.5 0.9 broadcast_subtract_fusion
  7.4 2.7 fusion.11
  10.1 0.0 copy-start.4
  10.1 1.6 copy.10
  11.7 9.2 %all-to-all-start = ((bf16[64,16,4,256]{3,0,2,1:T(8,128)(2,1)}), bf16[64,16,4,256]{3,0,2,1:T(8,128)(2,1)S(1)}, u32[]{:S(2)}, u32[]{:S(2)}) async-start(bf16[64,16,4,256]{3,0,2,1:T(8,128)(2,1)} %copy.10), calls=%async_computation | async-start | bytes 4194304 | tf_op jit(solution)/shard_map/all_to_all | solution.py:35
  20.9 0.0 copy-done.4
  20.9 0.2 copy.12
  21.2 0.0 copy-done
  21.2 3.8 %convert_bitcast_fusion = bf16[128,16,4,256]{0,1,2,3:T(8,128)(2,1)S(1)} fusion(s32[4,16,256]{1,0,2:T(4,128)S(1)} %copy.12, bf16[64,128]{1,0:T(8,128)(2,1)S(1)} %copy-done), kind=kOutput, calls=%fused_computation.10 | convolution fusion | flops 271581184 | bytes 4276224 | tf_op jit(solution)/shard_map/ti,tkqb->iqkb/dot_general | solution.py:31
  25.0 3.9 %copy.13 = bf16[128,16,4,256]{0,2,3,1:T(4,128)(2,1)} copy(bf16[128,16,4,256]{0,1,2,3:T(8,128)(2,1)S(1)} %convert_bitcast_fusion) | data formatting | bytes 8388608 | tf_op jit(solution)/shard_map/convert_element_type | solution.py:33
  28.8 41.9 %all-to-all-done = bf16[64,16,4,256]{3,0,2,1:T(8,128)(2,1)S(1)} async-done(((bf16[64,16,4,256]{3,0,2,1:T(8,128)(2,1)}), bf16[64,16,4,256]{3,0,2,1:T(8,128)(2,1)S(1)}, u32[]{:S(2)}, u32[]{:S(2)}) %all-to-all-start) | async-done | bytes 2097184 | tf_op jit(solution)/shard_map/all_to_all | solution.py:35
  70.7 0.0 copy-start.1
  70.7 4.5 %all-to-all-start.1 = ((bf16[128,16,4,256]{0,2,3,1:T(4,128)(2,1)}), bf16[128,16,4,256]{0,2,3,1:T(4,128)(2,1)}, u32[]{:S(2)}, u32[]{:S(2)}) async-start(bf16[128,16,4,256]{0,2,3,1:T(4,128)(2,1)} %copy.13), calls=%async_computation.1 | async-start | bytes 8388608 | tf_op jit(solution)/shard_map/all_to_all | solution.py:36
  75.2 0.0 all-reduce.2.cloned.1.call-start
  75.3 0.0 copy-done.1
  75.3 0.0 copy-start.2
  75.3 2.2 copy.29
  77.5 0.0 copy-done.2
  77.6 1.1 fusion.19
  78.7 7.3 %copy.25 = bf16[32,16,4,256]{0,1,2,3:T(8,128)(2,1)} copy(bf16[32,16,4,256]{3,0,2,1:T(8,128)(2,1)} %get-tuple-element.5) | data formatting | bytes 2097152
  86.0 7.1 %convolution_bitcast_fusion = f32[128,16,4,256]{0,1,2,3:T(8,128)} fusion(bf16[32,16,4,256]{0,1,2,3:T(8,128)(2,1)} %copy.25, bf16[32,256,128,1]{2,1,0,3:T(8,128)(2,1)S(1)} %bitcast.48), kind=kOutput, calls=%fused_computation.13 | convolution fusion | flops 134217728 | bytes 11534336 | tf_op jit(solution)/shard_map/mbi,mqkb->iqkb/dot_general | solution.py:41
  93.1 0.0 all-reduce.2.cloned.1.call-update
  93.1 0.2 reduce-scatter.2.cloned.1.call-start
  93.3 6.5 %copy.24 = bf16[32,16,4,256]{0,1,2,3:T(8,128)(2,1)} copy(bf16[32,16,4,256]{3,0,2,1:T(8,128)(2,1)S(1)} %get-tuple-element.6) | data formatting | bytes 2097152
  99.8 72.3 %all-to-all-done.1 = bf16[128,16,4,256]{0,2,3,1:T(4,128)(2,1)} async-done(((bf16[128,16,4,256]{0,2,3,1:T(4,128)(2,1)}), bf16[128,16,4,256]{0,2,3,1:T(4,128)(2,1)}, u32[]{:S(2)}, u32[]{:S(2)}) %all-to-all-start.1) | async-done | bytes 4194336 | tf_op jit(solution)/shard_map/all_to_all | solution.py:36
  172.1 31.0 %all-reduce.2.cloned.1.call-done = f32[128,16,4,256]{0,1,2,3:T(8,128)} async-done(((f32[128,16,4,256]{0,1,2,3:T(8,128)}), f32[128,16,4,256]{0,1,2,3:T(8,128)}) %all-reduce.2.cloned.1.call-update) | async-done | bytes 8388624 | tf_op jit(solution)/shard_map/psum | solution.py:44
  203.1 9.1 %fusion.9 = f32[256,4,8,128]{3,2,1,0:T(8,128)S(1)} fusion(bf16[32,16,4,256]{0,1,2,3:T(8,128)(2,1)} %copy.24, f32[128,16,4,256]{0,1,2,3:T(8,128)} %all-reduce.2.cloned.1.call-done, bf16[128,16,4,256]{0,2,3,1:T(4,128)(2,1)} %all-to-all-done.1), kind=kOutput, calls=%fused_computation.14 | convolution fusion | flops 142606336 | bytes 17825792 | tf_op jit(solution)/shard_map/iqkb,mqkb->mbi/dot_general | solution.py:46
  212.2 2.2 copy.41
  214.5 0.0 copy-start.3
  214.5 0.0 reduce-scatter.2.cloned.1.call-update
  214.5 109.9 %reduce-scatter.2.cloned.1.call-done = f32[32,16384]{1,0:T(8,128)} async-done(((f32[32,32768]{1,0:T(8,128)}), f32[32,16384]{1,0:T(8,128)}) %reduce-scatter.2.cloned.1.call-update) | async-done | bytes 2097168 | tf_op jit(solution)/shard_map/reduce_scatter | solution.py:50
  324.3 0.0 copy-done.3
  324.3 2.7 add_convert_fusion
  (2 shorter events, 0.0 us)
Async XLA Ops:
  6.5 14.6 %copy-start = (bf16[64,128]{1,0:T(8,128)(2,1)S(1)}, bf16[64,128]{1,0:T(8,128)(2,1)}, u32[]{:S(2)}) copy-start(bf16[64,128]{1,0:T(8,128)(2,1)} %param.9) | copy-start | bytes 49156
  10.1 10.8 %copy-start.4 = (s32[4,4096]{1,0:T(4,128)S(1)}, s32[4,4096]{1,0:T(4,128)}, u32[]{:S(2)}) copy-start(s32[4,4096]{1,0:T(4,128)} %param.11) | copy-start | bytes 196612
  11.7 59.0 %all-to-all-start = ((bf16[64,16,4,256]{3,0,2,1:T(8,128)(2,1)}), bf16[64,16,4,256]{3,0,2,1:T(8,128)(2,1)S(1)}, u32[]{:S(2)}, u32[]{:S(2)}) async-start(bf16[64,16,4,256]{3,0,2,1:T(8,128)(2,1)} %copy.10), calls=%async_computation | async-start | bytes 4194304 | tf_op jit(solution)/shard_map/all_to_all | solution.py:35
  70.7 4.6 %copy-start.1 = (bf16[64,16,4,256]{3,0,2,1:T(8,128)(2,1)}, bf16[64,16,4,256]{3,0,2,1:T(8,128)(2,1)S(1)}, u32[]{:S(2)}) copy-start(bf16[64,16,4,256]{3,0,2,1:T(8,128)(2,1)S(1)} %all-to-all-done) | copy-start | bytes 6291460
  70.7 101.4 %all-to-all-start.1 = ((bf16[128,16,4,256]{0,2,3,1:T(4,128)(2,1)}), bf16[128,16,4,256]{0,2,3,1:T(4,128)(2,1)}, u32[]{:S(2)}, u32[]{:S(2)}) async-start(bf16[128,16,4,256]{0,2,3,1:T(4,128)(2,1)} %copy.13), calls=%async_computation.1 | async-start | bytes 8388608 | tf_op jit(solution)/shard_map/all_to_all | solution.py:36
  75.2 127.9 %all-reduce.2.cloned.1.call-start = ((), (), s32[]{:S(2)}) async-start(), calls=%async_computation.3 | async-start | bytes 16777216 | tf_op jit(solution)/shard_map/psum | solution.py:44
  75.3 2.2 copy-start.2
  93.1 231.2 %reduce-scatter.2.cloned.1.call-start = ((), (), s32[]{:S(2)}) async-start(), calls=%async_computation.4 | async-start | bytes 6291456 | tf_op jit(solution)/shard_map/reduce_scatter | solution.py:50
  214.5 109.9 %copy-start.3 = (bf16[32,32768]{1,0:T(8,128)(2,1)S(1)}, bf16[32,32768]{1,0:T(8,128)(2,1)}, u32[]{:S(2)}) copy-start(bf16[32,32768]{1,0:T(8,128)(2,1)} %param.6) | copy-start | bytes 6291460
Sparse Core Ops, SparseCore 0:
  93.2 109.8 all-reduce.1
  214.6 109.6 reduce-scatter.1
where the time goes:
time: 334 us
  waiting for transfers between devices  255 us (76%)
  local copies, waits for them, and re-layouts  25.1 us (8%)
  matrix products  22.7 us (7%)
  starting transfers between devices  14 us (4%)
  between operations  13.5 us (4%)
  other arithmetic  3.6 us (1%)
    reduce_scatter x1, waiting for transfers between devices, local(): lax.psum_scatter(correction, 'dp', scatter_dimension=1, tiled=True)  110 us
    all_to_all x1, waiting for transfers between devices, local(): lax.all_to_all(rows_sent, 'cell', split_axis=1, concat_axis=1, tiled=True)  72.3 us
    all_to_all x1, waiting for transfers between devices, local(): lax.all_to_all(columns, 'cell', split_axis=1, concat_axis=1, tiled=True)  41.9 us
    psum x1, waiting for transfers between devices, local(): inner_prod = lax.psum(partial_prod, 'mem')  31 us
    unnamed x15, local copies, waits for them, and re-layouts  16 us
    all_to_all x1, starting transfers between devices, local(): lax.all_to_all(columns, 'cell', split_axis=1, concat_axis=1, tiled=True)  9.18 us
    dot_general x1, matrix products, local(): jnp.einsum('iqkb,mqkb->mbi', coefficient, innov_cols, preferred_element_t...  9.08 us
    dot_general x1, matrix products, local(): jnp.einsum('mbi,mqkb->iqkb', state_blocks, anom_cols, preferred_element_t...  7.12 us
  transfers between devices with their start and end apart: 4, of which 4 were waited for; matrix products, arithmetic and copies ran while one was open for 10% of the time, Pallas kernels for 0%

commit v1 on v0

v1 whole, which is shorter than its diff:
```python
import jax
import jax.numpy as jnp
from jax import lax
from jax.experimental import pallas as pl
from jax.experimental.pallas import tpu as pltpu
from jax.sharding import PartitionSpec as P

M = 256
EMPTY = 512
X = 4
DN_NT = (((1,), (1,)), ((), ()))
DN_TN = (((0,), (0,)), ((), ()))


def update_kernel(*refs):
    data = (refs[0:4], refs[4:8])
    near_ref, far_ref, ids_ref, prof_ids_ref, table_ref, out_near, out_far, cols = refs[8:]
    n_group, two_m, data_dev = refs[0].shape
    mem_dev = two_m // 2
    half = X * mem_dev
    n_block = near_ref.shape[1] // 128
    n_slot = prof_ids_ref.shape[0]

    lanes = lax.broadcasted_iota(jnp.int32, (128, 2 * data_dev), 1).astype(jnp.float32)
    for pair in range(n_group // 2):
        picker = jnp.where(lanes == ids_ref[:, pair : pair + 1], 1.0, 0.0).astype(jnp.bfloat16)
        for side in range(2):
            values = jnp.concatenate(
                [
                    jnp.concatenate(
                        [data[side][s][2 * pair + g, a * mem_dev : (a + 1) * mem_dev, :] for a in range(2) for s in range(X)],
                        axis=0,
                    )
                    for g in range(2)
                ],
                axis=1,
            )
            picked = lax.dot_general(picker, values, DN_NT, preferred_element_type=jnp.float32)
            picked = picked.reshape(n_block, 8, 2 * half)
            for a in range(2):
                cols[a, :, pair * 8 : (pair + 1) * 8, side * half : (side + 1) * half] = picked[:, :, a * half : (a + 1) * half]

    table = table_ref[...]
    rows = lax.broadcasted_iota(jnp.int32, (n_slot, table.shape[0]), 1).astype(jnp.float32)
    for b in range(n_block):
        spot = pl.ds(b * 128, 128)
        state = jnp.concatenate([near_ref[:, spot], far_ref[:, spot]], axis=0)
        anom = cols[0, b].astype(jnp.bfloat16)
        innov = cols[1, b].astype(jnp.bfloat16)
        inner = jnp.dot(anom, state, preferred_element_type=jnp.float32)
        chooser = jnp.where(rows == prof_ids_ref[:, b : b + 1], 1.0, 0.0).astype(jnp.bfloat16)
        weight = jnp.dot(chooser, table, preferred_element_type=jnp.float32)
        coef = (weight * inner / (M - 1)).astype(jnp.bfloat16)
        corr = lax.dot_general(innov, coef, DN_TN, preferred_element_type=jnp.float32)
        new = (state.astype(jnp.float32) + corr).astype(jnp.bfloat16)
        out_near[:, spot] = new[:half]
        out_far[:, spot] = new[half:]


def run_update(data, near, far, ids, prof_ids, table):
    half, width = near.shape
    n_block = width // 128
    n_slot = prof_ids.shape[0]
    whole = pl.BlockSpec(memory_space=pltpu.VMEM)
    return pl.pallas_call(
        update_kernel,
        out_shape=[jax.ShapeDtypeStruct(near.shape, jnp.bfloat16)] * 2,
        in_specs=[whole] * 13,
        out_specs=[whole] * 2,
        scratch_shapes=[pltpu.VMEM((2, n_block, n_slot, 2 * half), jnp.float32)],
        compiler_params=pltpu.CompilerParams(vmem_limit_bytes=40 * 1024 * 1024),
        cost_estimate=pl.CostEstimate(flops=800_000_000, bytes_accessed=6_500_000, transcendentals=0),
        name="update",
    )(*data, near, far, ids, prof_ids, table)


def x_shift(s):
    return [(x * 2 + c, ((x + s) % X) * 2 + c) for x in range(X) for c in range(2)]


CORE_SWAP = [(i, i ^ 1) for i in range(2 * X)]
SHIFTS = (1, 3, 2)


def local(ensemble, data_anom, weighted_innov, profiles, seg_data, seg_profile):
    n_cell = lax.axis_size("cell")
    n_dp = lax.axis_size("dp")
    n_mem = lax.axis_size("mem")
    me_cell, me_dp, me_mem = (lax.axis_index(n) for n in ("cell", "dp", "mem"))
    me_x, me_core = me_mem // 2, me_mem % 2
    mem_dev, cells_dev = ensemble.shape
    data_dev = data_anom.shape[1]
    per_group, blocks = seg_data.shape
    n_group = n_cell * n_dp
    own_blocks = blocks // (n_group * n_mem)
    half_cells = cells_dev // n_dp
    x_cells = half_cells // X
    own_cells = x_cells // 2

    def mine(seg):
        seg = seg.reshape(per_group, n_group, n_mem * own_blocks)
        return lax.dynamic_slice_in_dim(seg, me_mem * own_blocks, own_blocks, 2)

    pair_ids = jnp.where(seg_data >= 0, seg_data - me_cell * (n_dp * data_dev), EMPTY)
    seg = jnp.concatenate([mine(pair_ids), mine(seg_profile)], axis=0).astype(jnp.bfloat16)
    seg = jnp.pad(seg.transpose(1, 0, 2), ((0, 0), (0, 0), (0, data_dev - own_blocks)))
    own_data = jnp.concatenate([data_anom, weighted_innov], axis=0)
    sent = jnp.concatenate([jnp.broadcast_to(own_data[None], (n_group,) + own_data.shape), seg], axis=1)

    got = lax.all_to_all(sent, ("cell", "dp"), 0, 0, tiled=True)

    def state_for(s):
        x_to = (me_x + s) % X
        return lax.dynamic_slice_in_dim(ensemble, me_dp * half_cells + x_to * x_cells, x_cells, 1)

    pieces = [state_for(0)] + [None] * 3
    for s in SHIFTS:
        pieces[s] = lax.ppermute(state_for(s), "mem", x_shift(s))
    state = jnp.concatenate(pieces, axis=0)
    near = lax.dynamic_slice_in_dim(state, me_core * own_cells, own_cells, 1)
    far = lax.ppermute(
        lax.dynamic_slice_in_dim(state, (1 - me_core) * own_cells, own_cells, 1), "mem", CORE_SWAP
    )

    data_near = [got[:, : 2 * mem_dev]] + [None] * 3
    for s in SHIFTS:
        data_near[s] = lax.ppermute(data_near[0], "mem", x_shift(s))
    data_far = [lax.ppermute(d, "mem", CORE_SWAP) for d in data_near]

    got_seg = got[:, 2 * mem_dev :, :own_blocks].astype(jnp.float32)
    ids = got_seg[:, :per_group].reshape(n_group // 2, 2 * per_group, own_blocks).transpose(2, 1, 0)
    ids = ids.reshape(own_blocks * 2 * per_group, n_group // 2)
    prof_ids = got_seg[:, per_group:].reshape(n_group * per_group, own_blocks)

    new_near, new_far = run_update(data_near + data_far, near, far, ids, prof_ids, profiles)

    back_far = lax.ppermute(new_far, "mem", CORE_SWAP)
    first = me_core == 0
    new = jnp.concatenate([jnp.where(first, new_near, back_far), jnp.where(first, back_far, new_near)], axis=1)
    out = jnp.zeros((mem_dev, half_cells), jnp.bfloat16)
    for s in (0,) + SHIFTS:
        piece = new[s * mem_dev : (s + 1) * mem_dev]
        if s:
            piece = lax.ppermute(piece, "mem", x_shift(X - s))
        out = lax.dynamic_update_slice_in_dim(out, piece, ((me_x + s) % X) * x_cells, 1)
    return out


def solution(mesh):
    placed = (
        P("mem", "cell"),
        P("mem", ("cell", "dp")),
        P("mem", ("cell", "dp")),
        P(),
        P(("cell", "dp"), None),
        P(("cell", "dp"), None),
    )
    return jax.shard_map(
        local, mesh=mesh, in_specs=placed, out_specs=P("mem", ("cell", "dp")), check_vma=False
    )
```

time: 334 us -> 90.6 us (0.27)
  waiting for transfers between devices: 255 us -> 29.8 us
  starting transfers between devices: 14 us -> 41.6 us
  matrix products: 22.7 us -> 0 us
  local copies, waits for them, and re-layouts: 25.1 us -> 4.79 us
  between operations: 13.5 us -> 0.26 us
  Pallas kernels: 0 us -> 6.65 us
    reduce_scatter x1 -> x0, waiting for transfers between devices: 110 us -> none  [local(): lax.psum_scatter(correction, 'dp', scatter_dimension=1, tiled=True)]
    all_to_all x2 -> x1, waiting for transfers between devices: 114 us -> 11.2 us  [local(): got = lax.all_to_all(sent, ('cell', 'dp'), 0, 0, tiled=True)]
    psum x1 -> x0, waiting for transfers between devices: 31 us -> none  [local(): inner_prod = lax.psum(partial_prod, 'mem')]
    ppermute x0 -> x15, starting transfers between devices: none -> 29.6 us  [the longest x4 11.8 us: local(): data_far = [lax.ppermute(d, 'mem', CORE_SWAP) for d in data_near]]
    dot_general x4 -> x0, matrix products: 22.7 us -> none  [the longest x1 9.08 us: local(): jnp.einsum('iqkb,mqkb->mbi', coefficient, innov_cols, preferred_element_t...]
    ppermute x0 -> x15, waiting for transfers between devices: none -> 18.6 us  [the longest x3 11.5 us: local(): piece = lax.ppermute(piece, 'mem', x_shift(X - s))]
    unnamed x15 -> x12, local copies, waits for them, and re-layouts: 16 us -> 1.85 us
    pallas_call x0 -> x1, Pallas kernels: none -> 6.65 us  [run_update(): pl.pallas_call(update_kernel, out_shape=[jax.ShapeDtypeStruct(near.shape,...]
  transfers between devices with their start and end apart: 4 -> 16, of which waited for: 4 -> 7; matrix products, arithmetic and copies ran while one was open for 10% -> 4% of each run, Pallas kernels for 0% -> 0%
where the time goes in v1:
time: 90.6 us; the launch traced here: 88.8 us
  starting transfers between devices  41.6 us (46%)
  waiting for transfers between devices  29.8 us (33%)
  Pallas kernels  6.65 us (7%)
  other arithmetic  5.73 us (6%)
  local copies, waits for them, and re-layouts  4.79 us (5%)
    all_to_all x1, starting transfers between devices, local(): got = lax.all_to_all(sent, ('cell', 'dp'), 0, 0, tiled=True)  12 us
    ppermute x4, starting transfers between devices, local(): data_far = [lax.ppermute(d, 'mem', CORE_SWAP) for d in data_near]  11.8 us
    ppermute x3, waiting for transfers between devices, local(): piece = lax.ppermute(piece, 'mem', x_shift(X - s))  11.5 us
    all_to_all x1, waiting for transfers between devices, local(): got = lax.all_to_all(sent, ('cell', 'dp'), 0, 0, tiled=True)  11.2 us
    pallas_call x1, Pallas kernels, run_update(): pl.pallas_call(update_kernel, out_shape=[jax.ShapeDtypeStruct(near.shape,...  6.65 us
    ppermute x3, starting transfers between devices, local(): data_near[s] = lax.ppermute(data_near[0], 'mem', x_shift(s))  4.89 us
    ppermute x3, starting transfers between devices, local(): pieces[s] = lax.ppermute(state_for(s), 'mem', x_shift(s))  4.81 us
    ppermute x3, waiting for transfers between devices, local(): data_near[s] = lax.ppermute(data_near[0], 'mem', x_shift(s))  4.74 us
  transfers between devices with their start and end apart: 16, of which 7 were waited for; matrix products, arithmetic and copies ran while one was open for 4% of the time, Pallas kernels for 0%

profile of v1, /device:TPU:1, one launch (start us, length us, event | category | flops | bytes accessed | tf_op | source)
XLA Modules:
  0.0 88.8 jit_solution(18199130560659496111)
XLA Ops:
  0.0 1.0 %select_bitcast_fusion = s32[4,32,128]{2,0,1:T(4,128)S(1)} fusion(s32[4,4096]{1,0:T(4,128)} %param.10, s32[]{:T(128)S(6)} %mul.35), kind=kLoop, calls=%fused_computation.21 | loop fusion | flops 49152 | bytes 131076 | tf_op jit(solution)/shard_map/reshape | solution.py:101
  1.0 1.0 %dynamic-slice_convert_fusion = (bf16[4,32,16]{2,0,1:T(4,128)(2,1)S(1)}, bf16[4,32,16]{2,0,1:T(4,128)(2,1)S(1)}) fusion(s32[4,32,128]{2,0,1:T(4,128)} %bitcast.13, s32[]{:T(128)S(6)} %select_n.88, s32[4,32,128]{2,0,1:T(4,128)S(1)} %select_bitcast_fusion), kind=kLoop, calls=%fused_computation.19 | loop fusion | flops 4096 | bytes 24580 | tf_op jit(solution)/shard_map/convert.1
  2.1 0.7 pad_maximum_fusion.2
  2.8 0.1 broadcast_in_dim.14
  2.9 0.9 fusion.1
  3.8 12.0 %all-to-all-start = ((bf16[32,72,128]{2,1,0:T(8,128)(2,1)}), bf16[32,72,128]{2,1,0:T(8,128)(2,1)S(1)}, u32[]{:S(2)}, u32[]{:S(2)}) async-start(bf16[32,72,128]{2,1,0:T(8,128)(2,1)} %fusion.1), calls=%async_computation | async-start | bytes 1179648 | tf_op jit(solution)/shard_map/all_to_all | solution.py:110
  15.9 0.9 %constant_dynamic-slice_fusion.5 = (bf16[32,4096]{1,0:T(8,128)(2,1)S(1)}, bf16[32,4096]{1,0:T(8,128)(2,1)}, bf16[32,4096]{1,0:T(8,128)(2,1)}, bf16[32,4096]{1,0:T(8,128)(2,1)}) fusion(bf16[32,32768]{1,0:T(8,128)(2,1)S(1)} %copy-done.5, s32[]{:T(128)S(6)} %select_n.91, s32[]{:T(128)S(6)} %select_n.93, s32[]{:T(128)S(6)} %select_n.97, s32[]{:T(128)S(6)} %select_n.95), kind=kLoop, calls=%fused_computation.31 | loop fusion | bytes 2097168 | tf_op jit(solution)/shard_map/dynamic_slice | solution.py:114
  16.8 1.2 %collective-permute-start.7 = (bf16[32,4096]{1,0:T(8,128)(2,1)}, bf16[32,4096]{1,0:T(8,128)(2,1)S(1)}, u32[]{:S(2)}, u32[]{:S(2)}) collective-permute-start(bf16[32,4096]{1,0:T(8,128)(2,1)} %get-tuple-element.10), channel_id=1, source_target_pairs={{0,4},{2,6},{4,8},{6,10},{8,12},{10,14},{12,0},{14,2},{1,5},{3,7},... | collective-permute-start | bytes 786440 | tf_op jit(solution)/shard_map/ppermute | solution.py:118
  18.0 2.5 %collective-permute-start.8 = (bf16[32,4096]{1,0:T(8,128)(2,1)}, bf16[32,4096]{1,0:T(8,128)(2,1)}, u32[]{:S(2)}, u32[]{:S(2)}) collective-permute-start(bf16[32,4096]{1,0:T(8,128)(2,1)} %get-tuple-element.12), channel_id=1, source_target_pairs={{0,8},{2,10},{4,12},{6,14},{8,0},{10,2},{12,4},{14,6},{1,9},{3,11}... | collective-permute-start | bytes 786440 | tf_op jit(solution)/shard_map/ppermute | solution.py:118
  20.5 1.2 %collective-permute-start.9 = (bf16[32,4096]{1,0:T(8,128)(2,1)}, bf16[32,4096]{1,0:T(8,128)(2,1)}, u32[]{:S(2)}, u32[]{:S(2)}) collective-permute-start(bf16[32,4096]{1,0:T(8,128)(2,1)} %get-tuple-element.11), channel_id=1, source_target_pairs={{0,12},{2,14},{4,0},{6,2},{8,4},{10,6},{12,8},{14,10},{1,13},{3,15... | collective-permute-start | bytes 786440 | tf_op jit(solution)/shard_map/ppermute | solution.py:118
  21.6 11.2 %all-to-all-done = bf16[32,72,128]{2,1,0:T(8,128)(2,1)S(1)} async-done(((bf16[32,72,128]{2,1,0:T(8,128)(2,1)}), bf16[32,72,128]{2,1,0:T(8,128)(2,1)S(1)}, u32[]{:S(2)}, u32[]{:S(2)}) %all-to-all-start) | async-done | bytes 589856 | tf_op jit(solution)/shard_map/all_to_all | solution.py:110
  32.8 0.1 slice.32.refs_0_
  32.9 1.3 %collective-permute-start = (bf16[32,64,128]{2,1,0:T(8,128)(2,1)S(1)}, bf16[32,64,128]{2,1,0:T(8,128)(2,1)S(1)}, u32[]{:S(2)}, u32[]{:S(2)}) collective-permute-start(bf16[32,64,128]{2,1,0:T(8,128)(2,1)S(1)} %slice.32.refs_0_), channel_id=1, source_target_pairs={{0,4},{2,6},{4,8},{6,10},{8,12},{10,14},{12,0},{14,2},{1,5},{3,7},... | collective-permute-start | bytes 1572872 | tf_op jit(solution)/shard_map/ppermute | solution.py:127
  34.2 2.5 %collective-permute-start.1 = (bf16[32,64,128]{2,1,0:T(8,128)(2,1)S(1)}, bf16[32,64,128]{2,1,0:T(8,128)(2,1)S(1)}, u32[]{:S(2)}, u32[]{:S(2)}) collective-permute-start(bf16[32,64,128]{2,1,0:T(8,128)(2,1)S(1)} %slice.32.refs_0_), channel_id=1, source_target_pairs={{0,8},{2,10},{4,12},{6,14},{8,0},{10,2},{12,4},{14,6},{1,9},{3,11}... | collective-permute-start | bytes 1572872 | tf_op jit(solution)/shard_map/ppermute | solution.py:127
  36.6 1.2 %collective-permute-start.2 = (bf16[32,64,128]{2,1,0:T(8,128)(2,1)S(1)}, bf16[32,64,128]{2,1,0:T(8,128)(2,1)S(1)}, u32[]{:S(2)}, u32[]{:S(2)}) collective-permute-start(bf16[32,64,128]{2,1,0:T(8,128)(2,1)S(1)} %slice.32.refs_0_), channel_id=1, source_target_pairs={{0,12},{2,14},{4,0},{6,2},{8,4},{10,6},{12,8},{14,10},{1,13},{3,15... | collective-permute-start | bytes 1572872 | tf_op jit(solution)/shard_map/ppermute | solution.py:127
  37.8 0.0 collective-permute-done.8
  37.8 0.0 collective-permute-done.9
  37.8 0.0 copy-start.2
  37.8 1.1 %pad_maximum_fusion = bf16[128,4096]{1,0:T(8,128)(2,1)S(1)} fusion(bf16[32,4096]{1,0:T(8,128)(2,1)} %collective-permute-done.9, bf16[32,4096]{1,0:T(8,128)(2,1)} %collective-permute-done.8, bf16[32,4096]{1,0:T(8,128)(2,1)S(1)} %collective-permute-done.7, bf16[32,4096]{1,0:T(8,128)(2,1)S(1)} %get-tuple-element.9), kind=kLoop, calls=%fused_computation.8 | loop fusion | flops 4194304 | bytes 2097152 | tf_op jit(solution)/shard_map/concatenate | solution.py:119
  38.9 0.9 %constant_dynamic-slice_fusion = (bf16[128,2048]{1,0:T(8,128)(2,1)}, bf16[128,2048]{1,0:T(8,128)(2,1)S(1)}) fusion(bf16[128,4096]{1,0:T(8,128)(2,1)S(1)} %pad_maximum_fusion, s32[]{:T(128)S(6)} %select_n.99, s32[]{:T(128)S(6)} %select_n.98), kind=kLoop, calls=%fused_computation.26 | loop fusion | bytes 2097160 | tf_op jit(solution)/shard_map/dynamic_slice | solution.py:122
  39.8 4.4 %collective-permute-start.10 = (bf16[128,2048]{1,0:T(8,128)(2,1)}, bf16[128,2048]{1,0:T(8,128)(2,1)S(1)}, u32[]{:S(2)}, u32[]{:S(2)}) collective-permute-start(bf16[128,2048]{1,0:T(8,128)(2,1)} %get-tuple-element.19), channel_id=1, source_target_pairs={{0,2},{2,0},{4,6},{6,4},{8,10},{10,8},{12,14},{14,12},{1,3},{3,1},... | collective-permute-start | bytes 1572872 | tf_op jit(solution)/shard_map/ppermute | solution.py:121
  44.2 0.0 collective-permute-done.refs_1_
  44.2 7.4 %collective-permute-start.4 = (bf16[32,64,128]{2,1,0:T(8,128)(2,1)S(1)}, bf16[32,64,128]{2,1,0:T(8,128)(2,1)}, u32[]{:S(2)}, u32[]{:S(2)}) collective-permute-start(bf16[32,64,128]{2,1,0:T(8,128)(2,1)S(1)} %collective-permute-done.refs_1_), channel_id=1, source_target_pairs={{0,2},{2,0},{4,6},{6,4},{8,10},{10,8},{12,14},{14,12},{1,3},{3,1},... | collective-permute-start | bytes 1572872 | tf_op jit(solution)/shard_map/ppermute | solution.py:128
  51.6 4.7 %collective-permute-done.1.refs_2_ = bf16[32,64,128]{2,1,0:T(8,128)(2,1)S(1)} collective-permute-done((bf16[32,64,128]{2,1,0:T(8,128)(2,1)S(1)}, bf16[32,64,128]{2,1,0:T(8,128)(2,1)S(1)}, u32[]{:S(2)}, u32[]{:S(2)}) %collective-permute-start.1) | collective-permute-done | bytes 524320 | tf_op jit(solution)/shard_map/ppermute | solution.py:127
  56.3 4.4 %collective-permute-start.5 = (bf16[32,64,128]{2,1,0:T(8,128)(2,1)S(1)}, bf16[32,64,128]{2,1,0:T(8,128)(2,1)}, u32[]{:S(2)}, u32[]{:S(2)}) collective-permute-start(bf16[32,64,128]{2,1,0:T(8,128)(2,1)S(1)} %collective-permute-done.1.refs_2_), channel_id=1, source_target_pairs={{0,2},{2,0},{4,6},{6,4},{8,10},{10,8},{12,14},{14,12},{1,3},{3,1},... | collective-permute-start | bytes 1572872 | tf_op jit(solution)/shard_map/ppermute | solution.py:128
  60.7 0.0 collective-permute-start.6
  60.7 0.8 slice_convert_fusion
  61.6 0.1 copy.7
  61.7 0.0 collective-permute-done.10.refs_9_
  61.7 0.0 copy-start
  61.8 0.8 copy-done
  62.5 0.0 collective-permute-done.3.refs_4_
  62.5 0.6 collective-permute-done.6.refs_7_
  63.2 1.0 %copy-done.1 = bf16[128,2048]{1,0:T(8,128)(2,1)S(1)} copy-done((bf16[128,2048]{1,0:T(8,128)(2,1)S(1)}, bf16[128,2048]{1,0:T(8,128)(2,1)}, u32[]{:S(2)}) %copy-start.1) | copy-done | bytes 524312
  64.2 6.7 %update.1 = (bf16[128,2048]{1,0:T(8,128)(2,1)S(1)}, bf16[128,2048]{1,0:T(8,128)(2,1)}) custom-call(bf16[32,64,128]{2,1,0:T(8,128)(2,1)S(1)} %slice.32.refs_0_, bf16[32,64,128]{2,1,0:T(8,128)(2,1)S(1)} %collective-permute-done.refs_1_, bf16[32,64,128]{2,1,0:T(8,128)(2,1)S(1)} %collective-permute-done.1.refs_2_, ...), custom_call_target="tpu_custom_call" | custom-call | flops 800000000 | bytes 6500000 | tf_op jit(solution)/shard_map/update/pallas_call | solution.py:65
  70.9 0.4 collective-permute-start.11
  71.2 1.8 %collective-permute-done.11 = bf16[128,2048]{1,0:T(8,128)(2,1)S(1)} collective-permute-done((bf16[128,2048]{1,0:T(8,128)(2,1)}, bf16[128,2048]{1,0:T(8,128)(2,1)S(1)}, u32[]{:S(2)}, u32[]{:S(2)}) %collective-permute-start.11) | collective-permute-done | bytes 524320 | tf_op jit(solution)/shard_map/ppermute | solution.py:137
  73.0 0.1 broadcast_select_fusion
  73.1 0.1 broadcast_in_dim.13
  73.1 0.1 pad_maximum_fusion.1
  73.2 1.5 %collective-permute-start.12 = (bf16[32,4096]{1,0:T(8,128)(2,1)S(1)}, bf16[32,4096]{1,0:T(8,128)(2,1)S(1)}, u32[]{:S(2)}, u32[]{:S(2)}) collective-permute-start(bf16[32,4096]{1,0:T(8,128)(2,1)S(1)} %get-tuple-element.15), channel_id=1, source_target_pairs={{0,12},{2,14},{4,0},{6,2},{8,4},{10,6},{12,8},{14,10},{1,13},{3,15... | collective-permute-start | bytes 786440 | tf_op jit(solution)/shard_map/ppermute | solution.py:144
  74.7 0.1 collective-permute-start.13
  74.8 1.8 %collective-permute-start.14 = (bf16[32,4096]{1,0:T(8,128)(2,1)S(1)}, bf16[32,4096]{1,0:T(8,128)(2,1)S(1)}, u32[]{:S(2)}, u32[]{:S(2)}) collective-permute-start(bf16[32,4096]{1,0:T(8,128)(2,1)S(1)} %get-tuple-element.13), channel_id=1, source_target_pairs={{0,8},{2,10},{4,12},{6,14},{8,0},{10,2},{12,4},{14,6},{1,9},{3,11}... | collective-permute-start | bytes 786440 | tf_op jit(solution)/shard_map/ppermute | solution.py:144
  76.6 4.3 %collective-permute-done.12 = bf16[32,4096]{1,0:T(8,128)(2,1)S(1)} collective-permute-done((bf16[32,4096]{1,0:T(8,128)(2,1)S(1)}, bf16[32,4096]{1,0:T(8,128)(2,1)S(1)}, u32[]{:S(2)}, u32[]{:S(2)}) %collective-permute-start.12) | collective-permute-done | bytes 262176 | tf_op jit(solution)/shard_map/ppermute | solution.py:144
  80.9 3.2 %collective-permute-done.13 = bf16[32,4096]{1,0:T(8,128)(2,1)S(1)} collective-permute-done((bf16[32,4096]{1,0:T(8,128)(2,1)S(1)}, bf16[32,4096]{1,0:T(8,128)(2,1)S(1)}, u32[]{:S(2)}, u32[]{:S(2)}) %collective-permute-start.13) | collective-permute-done | bytes 262176 | tf_op jit(solution)/shard_map/ppermute | solution.py:144
  84.1 0.0 copy-start.4
  84.1 4.0 %collective-permute-done.14 = bf16[32,4096]{1,0:T(8,128)(2,1)S(1)} collective-permute-done((bf16[32,4096]{1,0:T(8,128)(2,1)S(1)}, bf16[32,4096]{1,0:T(8,128)(2,1)S(1)}, u32[]{:S(2)}, u32[]{:S(2)}) %collective-permute-start.14) | collective-permute-done | bytes 262176 | tf_op jit(solution)/shard_map/ppermute | solution.py:144
  88.1 0.7 constant_dynamic-update-slice_fusion
  (16 shorter events, 0.1 us)
Async XLA Ops:
  0.0 15.9 %copy-start.5 = (bf16[32,32768]{1,0:T(8,128)(2,1)S(1)}, bf16[32,32768]{1,0:T(8,128)(2,1)}, u32[]{:S(2)}) copy-start(bf16[32,32768]{1,0:T(8,128)(2,1)} %param.6) | copy-start | bytes 6291460
  3.8 29.1 %all-to-all-start = ((bf16[32,72,128]{2,1,0:T(8,128)(2,1)}), bf16[32,72,128]{2,1,0:T(8,128)(2,1)S(1)}, u32[]{:S(2)}, u32[]{:S(2)}) async-start(bf16[32,72,128]{2,1,0:T(8,128)(2,1)} %fusion.1), calls=%async_computation | async-start | bytes 1179648 | tf_op jit(solution)/shard_map/all_to_all | solution.py:110
  16.8 19.8 %collective-permute-start.7 = (bf16[32,4096]{1,0:T(8,128)(2,1)}, bf16[32,4096]{1,0:T(8,128)(2,1)S(1)}, u32[]{:S(2)}, u32[]{:S(2)}) collective-permute-start(bf16[32,4096]{1,0:T(8,128)(2,1)} %get-tuple-element.10), channel_id=1, source_target_pairs={{0,4},{2,6},{4,8},{6,10},{8,12},{10,14},{12,0},{14,2},{1,5},{3,7},... | collective-permute-start | bytes 786440 | tf_op jit(solution)/shard_map/ppermute | solution.py:118
  18.0 19.7 %collective-permute-start.8 = (bf16[32,4096]{1,0:T(8,128)(2,1)}, bf16[32,4096]{1,0:T(8,128)(2,1)}, u32[]{:S(2)}, u32[]{:S(2)}) collective-permute-start(bf16[32,4096]{1,0:T(8,128)(2,1)} %get-tuple-element.12), channel_id=1, source_target_pairs={{0,8},{2,10},{4,12},{6,14},{8,0},{10,2},{12,4},{14,6},{1,9},{3,11}... | collective-permute-start | bytes 786440 | tf_op jit(solution)/shard_map/ppermute | solution.py:118
  20.5 17.3 %collective-permute-start.9 = (bf16[32,4096]{1,0:T(8,128)(2,1)}, bf16[32,4096]{1,0:T(8,128)(2,1)}, u32[]{:S(2)}, u32[]{:S(2)}) collective-permute-start(bf16[32,4096]{1,0:T(8,128)(2,1)} %get-tuple-element.11), channel_id=1, source_target_pairs={{0,12},{2,14},{4,0},{6,2},{8,4},{10,6},{12,8},{14,10},{1,13},{3,15... | collective-permute-start | bytes 786440 | tf_op jit(solution)/shard_map/ppermute | solution.py:118
  32.8 5.0 %copy-start.3 = (bf16[32,72,128]{2,1,0:T(8,128)(2,1)}, bf16[32,72,128]{2,1,0:T(8,128)(2,1)S(1)}, u32[]{:S(2)}) copy-start(bf16[32,72,128]{2,1,0:T(8,128)(2,1)S(1)} %all-to-all-done) | copy-start | bytes 1769476
  32.9 11.3 %collective-permute-start = (bf16[32,64,128]{2,1,0:T(8,128)(2,1)S(1)}, bf16[32,64,128]{2,1,0:T(8,128)(2,1)S(1)}, u32[]{:S(2)}, u32[]{:S(2)}) collective-permute-start(bf16[32,64,128]{2,1,0:T(8,128)(2,1)S(1)} %slice.32.refs_0_), channel_id=1, source_target_pairs={{0,4},{2,6},{4,8},{6,10},{8,12},{10,14},{12,0},{14,2},{1,5},{3,7},... | collective-permute-start | bytes 1572872 | tf_op jit(solution)/shard_map/ppermute | solution.py:127
  34.2 22.1 %collective-permute-start.1 = (bf16[32,64,128]{2,1,0:T(8,128)(2,1)S(1)}, bf16[32,64,128]{2,1,0:T(8,128)(2,1)S(1)}, u32[]{:S(2)}, u32[]{:S(2)}) collective-permute-start(bf16[32,64,128]{2,1,0:T(8,128)(2,1)S(1)} %slice.32.refs_0_), channel_id=1, source_target_pairs={{0,8},{2,10},{4,12},{6,14},{8,0},{10,2},{12,4},{14,6},{1,9},{3,11}... | collective-permute-start | bytes 1572872 | tf_op jit(solution)/shard_map/ppermute | solution.py:127
  36.6 24.1 %collective-permute-start.2 = (bf16[32,64,128]{2,1,0:T(8,128)(2,1)S(1)}, bf16[32,64,128]{2,1,0:T(8,128)(2,1)S(1)}, u32[]{:S(2)}, u32[]{:S(2)}) collective-permute-start(bf16[32,64,128]{2,1,0:T(8,128)(2,1)S(1)} %slice.32.refs_0_), channel_id=1, source_target_pairs={{0,12},{2,14},{4,0},{6,2},{8,4},{10,6},{12,8},{14,10},{1,13},{3,15... | collective-permute-start | bytes 1572872 | tf_op jit(solution)/shard_map/ppermute | solution.py:127
  37.8 25.4 %copy-start.2 = (bf16[64,128]{1,0:T(8,128)(2,1)S(1)}, bf16[64,128]{1,0:T(8,128)(2,1)}, u32[]{:S(2)}) copy-start(bf16[64,128]{1,0:T(8,128)(2,1)} %refs_12_.1) | copy-start | bytes 49156
  39.8 21.9 %collective-permute-start.10 = (bf16[128,2048]{1,0:T(8,128)(2,1)}, bf16[128,2048]{1,0:T(8,128)(2,1)S(1)}, u32[]{:S(2)}, u32[]{:S(2)}) collective-permute-start(bf16[128,2048]{1,0:T(8,128)(2,1)} %get-tuple-element.19), channel_id=1, source_target_pairs={{0,2},{2,0},{4,6},{6,4},{8,10},{10,8},{12,14},{14,12},{1,3},{3,1},... | collective-permute-start | bytes 1572872 | tf_op jit(solution)/shard_map/ppermute | solution.py:121
  44.2 18.4 %collective-permute-start.3 = (bf16[32,64,128]{2,1,0:T(8,128)(2,1)S(1)}, bf16[32,64,128]{2,1,0:T(8,128)(2,1)}, u32[]{:S(2)}, u32[]{:S(2)}) collective-permute-start(bf16[32,64,128]{2,1,0:T(8,128)(2,1)S(1)} %slice.32.refs_0_), channel_id=1, source_target_pairs={{0,2},{2,0},{4,6},{6,4},{8,10},{10,8},{12,14},{14,12},{1,3},{3,1},... | collective-permute-start | bytes 1572872 | tf_op jit(solution)/shard_map/ppermute | solution.py:128
  44.2 18.4 %collective-permute-start.4 = (bf16[32,64,128]{2,1,0:T(8,128)(2,1)S(1)}, bf16[32,64,128]{2,1,0:T(8,128)(2,1)}, u32[]{:S(2)}, u32[]{:S(2)}) collective-permute-start(bf16[32,64,128]{2,1,0:T(8,128)(2,1)S(1)} %collective-permute-done.refs_1_), channel_id=1, source_target_pairs={{0,2},{2,0},{4,6},{6,4},{8,10},{10,8},{12,14},{14,12},{1,3},{3,1},... | collective-permute-start | bytes 1572872 | tf_op jit(solution)/shard_map/ppermute | solution.py:128
  56.3 6.2 %collective-permute-start.5 = (bf16[32,64,128]{2,1,0:T(8,128)(2,1)S(1)}, bf16[32,64,128]{2,1,0:T(8,128)(2,1)}, u32[]{:S(2)}, u32[]{:S(2)}) collective-permute-start(bf16[32,64,128]{2,1,0:T(8,128)(2,1)S(1)} %collective-permute-done.1.refs_2_), channel_id=1, source_target_pairs={{0,2},{2,0},{4,6},{6,4},{8,10},{10,8},{12,14},{14,12},{1,3},{3,1},... | collective-permute-start | bytes 1572872 | tf_op jit(solution)/shard_map/ppermute | solution.py:128
  60.7 2.4 %collective-permute-start.6 = (bf16[32,64,128]{2,1,0:T(8,128)(2,1)S(1)}, bf16[32,64,128]{2,1,0:T(8,128)(2,1)}, u32[]{:S(2)}, u32[]{:S(2)}) collective-permute-start(bf16[32,64,128]{2,1,0:T(8,128)(2,1)S(1)} %collective-permute-done.2.refs_3_), channel_id=1, source_target_pairs={{0,2},{2,0},{4,6},{6,4},{8,10},{10,8},{12,14},{14,12},{1,3},{3,1},... | collective-permute-start | bytes 1572872 | tf_op jit(solution)/shard_map/ppermute | solution.py:128
  61.7 0.8 copy-start
  63.2 1.0 %copy-start.1 = (bf16[128,2048]{1,0:T(8,128)(2,1)S(1)}, bf16[128,2048]{1,0:T(8,128)(2,1)}, u32[]{:S(2)}) copy-start(bf16[128,2048]{1,0:T(8,128)(2,1)} %copy-done) | copy-start | bytes 1572868
  70.9 2.1 %collective-permute-start.11 = (bf16[128,2048]{1,0:T(8,128)(2,1)}, bf16[128,2048]{1,0:T(8,128)(2,1)S(1)}, u32[]{:S(2)}, u32[]{:S(2)}) collective-permute-start(bf16[128,2048]{1,0:T(8,128)(2,1)} %get-tuple-element.8), channel_id=1, source_target_pairs={{0,2},{2,0},{4,6},{6,4},{8,10},{10,8},{12,14},{14,12},{1,3},{3,1},... | collective-permute-start | bytes 1572872 | tf_op jit(solution)/shard_map/ppermute | solution.py:137
  73.2 7.6 %collective-permute-start.12 = (bf16[32,4096]{1,0:T(8,128)(2,1)S(1)}, bf16[32,4096]{1,0:T(8,128)(2,1)S(1)}, u32[]{:S(2)}, u32[]{:S(2)}) collective-permute-start(bf16[32,4096]{1,0:T(8,128)(2,1)S(1)} %get-tuple-element.15), channel_id=1, source_target_pairs={{0,12},{2,14},{4,0},{6,2},{8,4},{10,6},{12,8},{14,10},{1,13},{3,15... | collective-permute-start | bytes 786440 | tf_op jit(solution)/shard_map/ppermute | solution.py:144
  74.7 9.4 %collective-permute-start.13 = (bf16[32,4096]{1,0:T(8,128)(2,1)S(1)}, bf16[32,4096]{1,0:T(8,128)(2,1)S(1)}, u32[]{:S(2)}, u32[]{:S(2)}) collective-permute-start(bf16[32,4096]{1,0:T(8,128)(2,1)S(1)} %get-tuple-element.16), channel_id=1, source_target_pairs={{0,4},{2,6},{4,8},{6,10},{8,12},{10,14},{12,0},{14,2},{1,5},{3,7},... | collective-permute-start | bytes 786440 | tf_op jit(solution)/shard_map/ppermute | solution.py:144
  74.8 13.3 %collective-permute-start.14 = (bf16[32,4096]{1,0:T(8,128)(2,1)S(1)}, bf16[32,4096]{1,0:T(8,128)(2,1)S(1)}, u32[]{:S(2)}, u32[]{:S(2)}) collective-permute-start(bf16[32,4096]{1,0:T(8,128)(2,1)S(1)} %get-tuple-element.13), channel_id=1, source_target_pairs={{0,8},{2,10},{4,12},{6,14},{8,0},{10,2},{12,4},{14,6},{1,9},{3,11}... | collective-permute-start | bytes 786440 | tf_op jit(solution)/shard_map/ppermute | solution.py:144
  84.1 4.0 %copy-start.4 = (bf16[32,16384]{1,0:T(8,128)(2,1)}, bf16[32,16384]{1,0:T(8,128)(2,1)S(1)}, u32[]{:S(2)}) copy-start(bf16[32,16384]{1,0:T(8,128)(2,1)S(1)} %constant_dynamic-update-slice_fusion.1) | copy-start | bytes 3145732

commit v2 on v1

--- a/solution.py
+++ b/solution.py
@@ -7,28 +7,29 @@
 
 M = 256
 EMPTY = 512
-X = 4
+X, Y, Z = 4, 4, 8
 DN_NT = (((1,), (1,)), ((), ()))
 DN_TN = (((0,), (0,)), ((), ()))
 
 
 def update_kernel(*refs):
-    data = (refs[0:4], refs[4:8])
-    near_ref, far_ref, ids_ref, prof_ids_ref, table_ref, out_near, out_far, cols = refs[8:]
-    n_group, two_m, data_dev = refs[0].shape
-    mem_dev = two_m // 2
+    anom_data, innov_data = (refs[0:4], refs[4:8]), (refs[8:12], refs[12:16])
+    near_ref, far_ref, ids_ref, prof_ids_ref, table_ref, out_near, out_far, cols = refs[16:]
+    n_y, n_z, mem_dev, data_dev = refs[0].shape
     half = X * mem_dev
     n_block = near_ref.shape[1] // 128
     n_slot = prof_ids_ref.shape[0]
 
     lanes = lax.broadcasted_iota(jnp.int32, (128, 2 * data_dev), 1).astype(jnp.float32)
-    for pair in range(n_group // 2):
+    for pair in range(n_y * n_z // 2):
+        t, q = pair // (n_z // 2), pair % (n_z // 2)
         picker = jnp.where(lanes == ids_ref[:, pair : pair + 1], 1.0, 0.0).astype(jnp.bfloat16)
         for side in range(2):
             values = jnp.concatenate(
                 [
                     jnp.concatenate(
-                        [data[side][s][2 * pair + g, a * mem_dev : (a + 1) * mem_dev, :] for a in range(2) for s in range(X)],
+                        [anom_data[side][s][t, 2 * q + g] for s in range(X)]
+                        + [innov_data[side][t][s, 2 * q + g] for s in range(X)],
                         axis=0,
                     )
                     for g in range(2)
@@ -65,7 +66,7 @@
     return pl.pallas_call(
         update_kernel,
         out_shape=[jax.ShapeDtypeStruct(near.shape, jnp.bfloat16)] * 2,
-        in_specs=[whole] * 13,
+        in_specs=[whole] * 21,
         out_specs=[whole] * 2,
         scratch_shapes=[pltpu.VMEM((2, n_block, n_slot, 2 * half), jnp.float32)],
         compiler_params=pltpu.CompilerParams(vmem_limit_bytes=40 * 1024 * 1024),
@@ -78,36 +79,61 @@
     return [(x * 2 + c, ((x + s) % X) * 2 + c) for x in range(X) for c in range(2)]
 
 
+def line(y, z):
+    return (y * 4 + z % 4) * 2 + z // 4
+
+
+def y_shift(s):
+    return [(line(y, z), line((y + s) % Y, z)) for y in range(Y) for z in range(Z)]
+
+
+Z_RUNS = [[line(y, z) for z in range(Z)] for y in range(Y)]
 CORE_SWAP = [(i, i ^ 1) for i in range(2 * X)]
 SHIFTS = (1, 3, 2)
+PLANE = ("cell", "dp")
+
+
+def shifted(piece, axis, shift):
+    out = [piece] + [None] * 3
+    for s in SHIFTS:
+        out[s] = lax.ppermute(piece, axis, shift(s))
+    return out
 
 
 def local(ensemble, data_anom, weighted_innov, profiles, seg_data, seg_profile):
-    n_cell = lax.axis_size("cell")
-    n_dp = lax.axis_size("dp")
+    n_group = lax.axis_size("cell") * lax.axis_size("dp")
     n_mem = lax.axis_size("mem")
     me_cell, me_dp, me_mem = (lax.axis_index(n) for n in ("cell", "dp", "mem"))
     me_x, me_core = me_mem // 2, me_mem % 2
+    me_y, me_zlo = me_cell // 4, me_cell % 4
     mem_dev, cells_dev = ensemble.shape
     data_dev = data_anom.shape[1]
     per_group, blocks = seg_data.shape
-    n_group = n_cell * n_dp
     own_blocks = blocks // (n_group * n_mem)
-    half_cells = cells_dev // n_dp
+    half_cells = cells_dev // 2
     x_cells = half_cells // X
     own_cells = x_cells // 2
+
+    group = me_cell * 2 + me_dp
+    pair_ids = jnp.where(seg_data >= 0, seg_data - group * data_dev + (me_zlo % 2) * data_dev, EMPTY)
 
     def mine(seg):
         seg = seg.reshape(per_group, n_group, n_mem * own_blocks)
         return lax.dynamic_slice_in_dim(seg, me_mem * own_blocks, own_blocks, 2)
 
-    pair_ids = jnp.where(seg_data >= 0, seg_data - me_cell * (n_dp * data_dev), EMPTY)
-    seg = jnp.concatenate([mine(pair_ids), mine(seg_profile)], axis=0).astype(jnp.bfloat16)
-    seg = jnp.pad(seg.transpose(1, 0, 2), ((0, 0), (0, 0), (0, data_dev - own_blocks)))
-    own_data = jnp.concatenate([data_anom, weighted_innov], axis=0)
-    sent = jnp.concatenate([jnp.broadcast_to(own_data[None], (n_group,) + own_data.shape), seg], axis=1)
-
-    got = lax.all_to_all(sent, ("cell", "dp"), 0, 0, tiled=True)
+    seg = jnp.stack([mine(pair_ids), mine(seg_profile)]).astype(jnp.bfloat16)
+    seg = seg.reshape(2, per_group, Y, Z // 2, 2, own_blocks).transpose(4, 3, 2, 0, 1, 5)
+    seg = seg.reshape(Z, Y, 2 * per_group * own_blocks)
+    seg = jnp.pad(seg, ((0, 0), (0, 8 - Y), (0, 0)))
+    sent = jnp.concatenate(
+        [
+            jnp.broadcast_to(data_anom[None], (Z,) + data_anom.shape),
+            seg,
+            jnp.broadcast_to(weighted_innov[None], (Z,) + weighted_innov.shape),
+        ],
+        axis=1,
+    )
+    got = lax.all_to_all(sent, PLANE, 0, 0, tiled=True, axis_index_groups=Z_RUNS)
 
     def state_for(s):
         x_to = (me_x + s) % X
@@ -122,23 +148,27 @@
         lax.dynamic_slice_in_dim(state, (1 - me_core) * own_cells, own_cells, 1), "mem", CORE_SWAP
     )
 
-    data_near = [got[:, : 2 * mem_dev]] + [None] * 3
-    for s in SHIFTS:
-        data_near[s] = lax.ppermute(data_near[0], "mem", x_shift(s))
-    data_far = [lax.ppermute(d, "mem", CORE_SWAP) for d in data_near]
+    anom_mid = shifted(got[:, : mem_dev + 8], PLANE, y_shift)
+    innov_mid = shifted(got[:, mem_dev + 8 :], "mem", x_shift)
+    anom_near = shifted(jnp.stack([p[:, :mem_dev] for p in anom_mid]), "mem", x_shift)
+    innov_near = shifted(jnp.stack(innov_mid), PLANE, y_shift)
+    anom_far = [lax.ppermute(p, "mem", CORE_SWAP) for p in anom_near]
+    innov_far = [lax.ppermute(p, "mem", CORE_SWAP) for p in innov_near]
 
-    got_seg = got[:, 2 * mem_dev :, :own_blocks].astype(jnp.float32)
-    ids = got_seg[:, :per_group].reshape(n_group // 2, 2 * per_group, own_blocks).transpose(2, 1, 0)
+    got_seg = jnp.stack([lax.dynamic_slice_in_dim(p, mem_dev + me_y, 1, 1) for p in anom_mid])
+    got_seg = got_seg.astype(jnp.float32).reshape(n_group, 2, per_group, own_blocks)
+    ids = got_seg[:, 0].reshape(n_group // 2, 2 * per_group, own_blocks).transpose(2, 1, 0)
     ids = ids.reshape(own_blocks * 2 * per_group, n_group // 2)
-    prof_ids = got_seg[:, per_group:].reshape(n_group * per_group, own_blocks)
+    prof_ids = got_seg[:, 1].reshape(n_group * per_group, own_blocks)
 
-    new_near, new_far = run_update(data_near + data_far, near, far, ids, prof_ids, profiles)
+    data = anom_near + anom_far + innov_near + innov_far
+    new_near, new_far = run_update(data, near, far, ids, prof_ids, profiles)
 
     back_far = lax.ppermute(new_far, "mem", CORE_SWAP)
     first = me_core == 0
     new = jnp.concatenate([jnp.where(first, new_near, back_far), jnp.where(first, back_far, new_near)], axis=1)
     out = jnp.zeros((mem_dev, half_cells), jnp.bfloat16)
-    for s in (0,) + SHIFTS:
+    for s in (0, 2, 1, 3):
         piece = new[s * mem_dev : (s + 1) * mem_dev]
         if s:
             piece = lax.ppermute(piece, "mem", x_shift(X - s))

time: 90.6 us -> 101 us (1.11)
  local copies, waits for them, and re-layouts: 4.79 us -> 15.4 us
  starting transfers between devices: 41.6 us -> 51.7 us
  waiting for transfers between devices: 29.8 us -> 24.1 us
  other arithmetic: 5.73 us -> 2.06 us
    ppermute x7 -> x20, starting transfers between devices: 16.7 us -> 29.9 us  [the longest x12 18.6 us: shifted(): out[s] = lax.ppermute(piece, axis, shift(s))]
    all_to_all x1, waiting for transfers between devices: 11.2 us -> 1.75 us  [local(): lax.all_to_all(sent, PLANE, 0, 0, tiled=True, axis_index_groups=Z_RUNS)]
    unnamed x12 -> x30, local copies, waits for them, and re-layouts: 1.85 us -> 6.1 us
    ppermute x3, waiting for transfers between devices: 0.01 us -> 3.7 us  [local(): pieces[s] = lax.ppermute(state_for(s), 'mem', x_shift(s))]
    all_to_all x1, starting transfers between devices: 12 us -> 9.01 us  [local(): lax.all_to_all(sent, PLANE, 0, 0, tiled=True, axis_index_groups=Z_RUNS)]
    ppermute x1, starting transfers between devices: 4.35 us -> 2.25 us  [local(): lax.ppermute(lax.dynamic_slice_in_dim(state, (1 - me_core) * own_cells, o...]
    ppermute x3, starting transfers between devices: 3.32 us -> 5.17 us  [local(): piece = lax.ppermute(piece, 'mem', x_shift(X - s))]
    dynamic_slice x0 -> x4, local copies, waits for them, and re-layouts: none -> 1.49 us  [local(): lax.dynamic_slice_in_dim(p, mem_dev + me_y, 1, 1)]
  transfers between devices with their start and end apart: 16 -> 29, of which waited for: 7 -> 8; matrix products, arithmetic and copies ran while one was open for 4% -> 7% of each run, Pallas kernels for 0% -> 0%
where the time goes in v2:
time: 101 us; the launch traced here: 100 us
  starting transfers between devices  51.7 us (51%)
  waiting for transfers between devices  24.1 us (24%)
  local copies, waits for them, and re-layouts  15.4 us (15%)
  Pallas kernels  6.4 us (6%)
  other arithmetic  2.06 us (2%)
    ppermute x12, starting transfers between devices, shifted(): out[s] = lax.ppermute(piece, axis, shift(s))  18.6 us
    ppermute x3, waiting for transfers between devices, local(): piece = lax.ppermute(piece, 'mem', x_shift(X - s))  10.9 us
    ppermute x4, starting transfers between devices, local(): innov_far = [lax.ppermute(p, 'mem', CORE_SWAP) for p in innov_near]  10.2 us
    all_to_all x1, starting transfers between devices, local(): lax.all_to_all(sent, PLANE, 0, 0, tiled=True, axis_index_groups=Z_RUNS)  9.01 us
    pallas_call x1, Pallas kernels, run_update(): pl.pallas_call(update_kernel, out_shape=[jax.ShapeDtypeStruct(near.shape,...  6.4 us
    unnamed x30, local copies, waits for them, and re-layouts  6.1 us
    ppermute x12, waiting for transfers between devices, shifted(): out[s] = lax.ppermute(piece, axis, shift(s))  6.02 us
    ppermute x3, starting transfers between devices, local(): piece = lax.ppermute(piece, 'mem', x_shift(X - s))  5.17 us
  transfers between devices with their start and end apart: 29, of which 8 were waited for; matrix products, arithmetic and copies ran while one was open for 7% of the time, Pallas kernels for 0%

profile of v2, /device:TPU:1, one launch (start us, length us, event | category | flops | bytes accessed | tf_op | source)
XLA Modules:
  0.0 100.0 jit_solution(3153633092705170300)
XLA Ops:
  0.0 0.9 select_bitcast_fusion
  0.9 0.8 copy.22
  2.1 0.7 broadcast_in_dim.20
  2.8 0.7 broadcast_in_dim.22
  3.5 0.7 fusion.7
  4.2 9.0 %all-to-all-start = ((bf16[8,72,128]{2,1,0:T(8,128)(2,1)}), bf16[8,72,128]{2,1,0:T(8,128)(2,1)S(1)}, u32[]{:S(2)}, u32[]{:S(2)}) async-start(bf16[8,72,128]{2,1,0:T(8,128)(2,1)} %fusion.7), calls=%async_computation | async-start | bytes 294912 | tf_op jit(solution)/shard_map/all_to_all | solution.py:136
  13.2 1.3 %constant_dynamic-slice_fusion.9 = (bf16[32,4096]{1,0:T(8,128)(2,1)S(1)}, bf16[32,4096]{1,0:T(8,128)(2,1)S(1)}, bf16[32,4096]{1,0:T(8,128)(2,1)S(1)}, bf16[32,4096]{1,0:T(8,128)(2,1)S(1)}) fusion(bf16[32,32768]{1,0:T(8,128)(2,1)} %param.6, s32[]{:T(128)S(6)} %select_n.110, s32[]{:T(128)S(6)} %select_n.112, s32[]{:T(128)S(6)} %select_n.116, s32[]{:T(128)S(6)} %select_n.114), kind=kLoop, calls=%fused_computation.45 | loop fusion | bytes 2097168 | tf_op jit(solution)/shard_map/dynamic_slice | solution.py:140
  14.5 1.3 %collective-permute-start.20 = (bf16[32,4096]{1,0:T(8,128)(2,1)S(1)}, bf16[32,4096]{1,0:T(8,128)(2,1)S(1)}, u32[]{:S(2)}, u32[]{:S(2)}) collective-permute-start(bf16[32,4096]{1,0:T(8,128)(2,1)S(1)} %get-tuple-element.10), channel_id=1, source_target_pairs={{0,4},{2,6},{4,8},{6,10},{8,12},{10,14},{12,0},{14,2},{1,5},{3,7},... | collective-permute-start | bytes 786440 | tf_op jit(solution)/shard_map/ppermute | solution.py:144
  15.8 2.5 %collective-permute-start.21 = (bf16[32,4096]{1,0:T(8,128)(2,1)S(1)}, bf16[32,4096]{1,0:T(8,128)(2,1)S(1)}, u32[]{:S(2)}, u32[]{:S(2)}) collective-permute-start(bf16[32,4096]{1,0:T(8,128)(2,1)S(1)} %get-tuple-element.12), channel_id=1, source_target_pairs={{0,8},{2,10},{4,12},{6,14},{8,0},{10,2},{12,4},{14,6},{1,9},{3,11}... | collective-permute-start | bytes 786440 | tf_op jit(solution)/shard_map/ppermute | solution.py:144
  18.2 1.2 %collective-permute-start.22 = (bf16[32,4096]{1,0:T(8,128)(2,1)S(1)}, bf16[32,4096]{1,0:T(8,128)(2,1)S(1)}, u32[]{:S(2)}, u32[]{:S(2)}) collective-permute-start(bf16[32,4096]{1,0:T(8,128)(2,1)S(1)} %get-tuple-element.11), channel_id=1, source_target_pairs={{0,12},{2,14},{4,0},{6,2},{8,4},{10,6},{12,8},{14,10},{1,13},{3,15... | collective-permute-start | bytes 786440 | tf_op jit(solution)/shard_map/ppermute | solution.py:144
  19.4 1.7 %all-to-all-done = bf16[8,72,128]{2,1,0:T(8,128)(2,1)S(1)} async-done(((bf16[8,72,128]{2,1,0:T(8,128)(2,1)}), bf16[8,72,128]{2,1,0:T(8,128)(2,1)S(1)}, u32[]{:S(2)}, u32[]{:S(2)}) %all-to-all-start) | async-done | bytes 147488 | tf_op jit(solution)/shard_map/all_to_all | solution.py:136
  21.2 2.6 %collective-permute-start.12 = (bf16[8,32,128]{2,1,0:T(8,128)(2,1)S(1)}, bf16[8,32,128]{2,1,0:T(8,128)(2,1)S(1)}, u32[]{:S(2)}, u32[]{:S(2)}) collective-permute-start(bf16[8,32,128]{2,1,0:T(8,128)(2,1)S(1)} %get-tuple-element.22), channel_id=1, source_target_pairs={{0,12},{2,14},{4,0},{6,2},{8,4},{10,6},{12,8},{14,10},{1,13},{3,15... | collective-permute-start | bytes 196616 | tf_op jit(solution)/shard_map/ppermute | solution.py:99
  23.7 1.8 %collective-permute-start.11 = (bf16[8,32,128]{2,1,0:T(8,128)(2,1)S(1)}, bf16[8,32,128]{2,1,0:T(8,128)(2,1)S(1)}, u32[]{:S(2)}, u32[]{:S(2)}) collective-permute-start(bf16[8,32,128]{2,1,0:T(8,128)(2,1)S(1)} %get-tuple-element.22), channel_id=1, source_target_pairs={{0,8},{2,10},{4,12},{6,14},{8,0},{10,2},{12,4},{14,6},{1,9},{3,11}... | collective-permute-start | bytes 196616 | tf_op jit(solution)/shard_map/ppermute | solution.py:99
  25.6 3.7 %collective-permute-done.21 = bf16[32,4096]{1,0:T(8,128)(2,1)S(1)} collective-permute-done((bf16[32,4096]{1,0:T(8,128)(2,1)S(1)}, bf16[32,4096]{1,0:T(8,128)(2,1)S(1)}, u32[]{:S(2)}, u32[]{:S(2)}) %collective-permute-start.21) | collective-permute-done | bytes 262176 | tf_op jit(solution)/shard_map/ppermute | solution.py:144
  29.3 2.7 %collective-permute-start.2 = (bf16[8,40,128]{2,1,0:T(8,128)(2,1)S(1)}, bf16[8,40,128]{2,1,0:T(8,128)(2,1)S(1)}, u32[]{:S(2)}, u32[]{:S(2)}) collective-permute-start(bf16[8,40,128]{2,1,0:T(8,128)(2,1)S(1)} %slice.50), channel_id=1, source_target_pairs={{0,192},{16,208},{32,224},{48,240},{1,193},{17,209},{33,225},{49,2... | collective-permute-start | bytes 245768 | tf_op jit(solution)/shard_map/ppermute | solution.py:99
  32.4 0.8 collective-permute-start
  33.2 1.7 %collective-permute-start.13 = (bf16[4,8,32,128]{3,2,1,0:T(8,128)(2,1)S(1)}, bf16[4,8,32,128]{3,2,1,0:T(8,128)(2,1)S(1)}, u32[]{:S(2)}, u32[]{:S(2)}) collective-permute-start(bf16[4,8,32,128]{3,2,1,0:T(8,128)(2,1)S(1)} %pad_maximum_fusion.3.refs_8_), channel_id=1, source_target_pairs={{0,64},{16,80},{32,96},{48,112},{1,65},{17,81},{33,97},{49,113},{6... | collective-permute-start | bytes 786440 | tf_op jit(solution)/shard_map/ppermute | solution.py:99
  34.9 1.6 %collective-permute-start.14 = (bf16[4,8,32,128]{3,2,1,0:T(8,128)(2,1)S(1)}, bf16[4,8,32,128]{3,2,1,0:T(8,128)(2,1)S(1)}, u32[]{:S(2)}, u32[]{:S(2)}) collective-permute-start(bf16[4,8,32,128]{3,2,1,0:T(8,128)(2,1)S(1)} %pad_maximum_fusion.3.refs_8_), channel_id=1, source_target_pairs={{0,128},{16,144},{32,160},{48,176},{1,129},{17,145},{33,161},{49,1... | collective-permute-start | bytes 786440 | tf_op jit(solution)/shard_map/ppermute | solution.py:99
  36.5 0.9 collective-permute-start.15
  37.5 7.8 %collective-permute-start.16 = (bf16[4,8,32,128]{3,2,1,0:T(8,128)(2,1)S(1)}, bf16[4,8,32,128]{3,2,1,0:T(8,128)(2,1)S(1)}, u32[]{:S(2)}, u32[]{:S(2)}) collective-permute-start(bf16[4,8,32,128]{3,2,1,0:T(8,128)(2,1)S(1)} %pad_maximum_fusion.3.refs_8_), channel_id=1, source_target_pairs={{0,2},{2,0},{4,6},{6,4},{8,10},{10,8},{12,14},{14,12},{1,3},{3,1},... | collective-permute-start | bytes 786440 | tf_op jit(solution)/shard_map/ppermute | solution.py:156
  45.4 0.9 constant_dynamic-slice_fusion.4
  46.3 2.2 %collective-permute-start.23 = (bf16[128,2048]{1,0:T(8,128)(2,1)}, bf16[128,2048]{1,0:T(8,128)(2,1)S(1)}, u32[]{:S(2)}, u32[]{:S(2)}) collective-permute-start(bf16[128,2048]{1,0:T(8,128)(2,1)} %get-tuple-element.19), channel_id=1, source_target_pairs={{0,2},{2,0},{4,6},{6,4},{8,10},{10,8},{12,14},{14,12},{1,3},{3,1},... | collective-permute-start | bytes 1572872 | tf_op jit(solution)/shard_map/ppermute | solution.py:147
  48.6 1.0 %collective-permute-start.4 = (bf16[4,8,32,128]{3,2,1,0:T(8,128)(2,1)S(1)}, bf16[4,8,32,128]{3,2,1,0:T(8,128)(2,1)S(1)}, u32[]{:S(2)}, u32[]{:S(2)}) collective-permute-start(bf16[4,8,32,128]{3,2,1,0:T(8,128)(2,1)S(1)} %pad_maximum_fusion.2.refs_0_), channel_id=1, source_target_pairs={{0,8},{2,10},{4,12},{6,14},{8,0},{10,2},{12,4},{14,6},{1,9},{3,11}... | collective-permute-start | bytes 786440 | tf_op jit(solution)/shard_map/ppermute | solution.py:99
  49.6 5.1 %collective-permute-start.5 = (bf16[4,8,32,128]{3,2,1,0:T(8,128)(2,1)S(1)}, bf16[4,8,32,128]{3,2,1,0:T(8,128)(2,1)S(1)}, u32[]{:S(2)}, u32[]{:S(2)}) collective-permute-start(bf16[4,8,32,128]{3,2,1,0:T(8,128)(2,1)S(1)} %pad_maximum_fusion.2.refs_0_), channel_id=1, source_target_pairs={{0,12},{2,14},{4,0},{6,2},{8,4},{10,6},{12,8},{14,10},{1,13},{3,15... | collective-permute-start | bytes 786440 | tf_op jit(solution)/shard_map/ppermute | solution.py:99
  54.7 0.6 collective-permute-start.6
  55.3 4.8 %collective-permute-done.3.refs_1_ = bf16[4,8,32,128]{3,2,1,0:T(8,128)(2,1)S(1)} collective-permute-done((bf16[4,8,32,128]{3,2,1,0:T(8,128)(2,1)S(1)}, bf16[4,8,32,128]{3,2,1,0:T(8,128)(2,1)S(1)}, u32[]{:S(2)}, u32[]{:S(2)}) %collective-permute-start.3) | collective-permute-done | bytes 262176 | tf_op jit(solution)/shard_map/ppermute | solution.py:99
  60.1 0.8 collective-permute-start.17
  61.0 0.7 constant_dynamic-slice_fusion.1
  61.7 0.7 constant_dynamic-slice_fusion.2
  62.6 1.2 %collective-permute-done.5.refs_3_ = bf16[4,8,32,128]{3,2,1,0:T(8,128)(2,1)S(1)} collective-permute-done((bf16[4,8,32,128]{3,2,1,0:T(8,128)(2,1)S(1)}, bf16[4,8,32,128]{3,2,1,0:T(8,128)(2,1)S(1)}, u32[]{:S(2)}, u32[]{:S(2)}) %collective-permute-start.5) | collective-permute-done | bytes 262176 | tf_op jit(solution)/shard_map/ppermute | solution.py:99
  63.7 1.5 %collective-permute-start.19 = (bf16[4,8,32,128]{3,2,1,0:T(8,128)(2,1)S(1)}, bf16[4,8,32,128]{3,2,1,0:T(8,128)(2,1)}, u32[]{:S(2)}, u32[]{:S(2)}) collective-permute-start(bf16[4,8,32,128]{3,2,1,0:T(8,128)(2,1)S(1)} %collective-permute-done.15.refs_11_), channel_id=1, source_target_pairs={{0,2},{2,0},{4,6},{6,4},{8,10},{10,8},{12,14},{14,12},{1,3},{3,1},... | collective-permute-start | bytes 786440 | tf_op jit(solution)/shard_map/ppermute | solution.py:156
  65.2 0.7 copy-done.4
  66.5 0.7 copy-done.6
  67.2 0.8 reshape.46
  68.0 1.5 %fusion.8 = (f32[32,1,4,16]{3,2,1,0:T(4,128)S(1)}, f32[32,1,4,16]{3,2,1,0:T(4,128)}) fusion(f32[32,2,4,16]{3,2,1,0:T(4,128)} %reshape.46), kind=kLoop, calls=%fused_computation.51 | loop fusion | bytes 32768 | tf_op jit(solution)/shard_map/slice | solution.py:162
  69.5 0.9 copy.9
  70.5 0.9 copy-done.1
  71.5 0.9 copy-done.3
  72.4 0.9 copy-done.5
  73.4 0.9 copy-done.7
  74.3 6.4 %update.1 = (bf16[128,2048]{1,0:T(8,128)(2,1)S(1)}, bf16[128,2048]{1,0:T(8,128)(2,1)}) custom-call(bf16[4,8,32,128]{3,2,1,0:T(8,128)(2,1)S(1)} %pad_maximum_fusion.2.refs_0_, bf16[4,8,32,128]{3,2,1,0:T(8,128)(2,1)S(1)} %collective-permute-done.3.refs_1_, bf16[4,8,32,128]{3,2,1,0:T(8,128)(2,1)S(1)} %copy-done.1, bf16[4,8,32,128]{3,2,1,0:T(8,128)(2,1)S(1)} %copy-done.3, ...), custom_call_target="tpu_custom_call" | custom-call | flops 800000000 | bytes 6500000 | tf_op jit(solution)/shard_map/update/pallas_call | solution.py:66
  81.2 1.7 %collective-permute-done.24 = bf16[128,2048]{1,0:T(8,128)(2,1)S(1)} collective-permute-done((bf16[128,2048]{1,0:T(8,128)(2,1)}, bf16[128,2048]{1,0:T(8,128)(2,1)S(1)}, u32[]{:S(2)}, u32[]{:S(2)}) %collective-permute-start.24) | collective-permute-done | bytes 524320 | tf_op jit(solution)/shard_map/ppermute | solution.py:167
  83.2 3.7 %collective-permute-start.25 = (bf16[32,4096]{1,0:T(8,128)(2,1)S(1)}, bf16[32,4096]{1,0:T(8,128)(2,1)S(1)}, u32[]{:S(2)}, u32[]{:S(2)}) collective-permute-start(bf16[32,4096]{1,0:T(8,128)(2,1)S(1)} %get-tuple-element.15), channel_id=1, source_target_pairs={{0,8},{2,10},{4,12},{6,14},{8,0},{10,2},{12,4},{14,6},{1,9},{3,11}... | collective-permute-start | bytes 786440 | tf_op jit(solution)/shard_map/ppermute | solution.py:174
  87.4 0.9 collective-permute-start.27
  88.3 5.0 %collective-permute-done.25 = bf16[32,4096]{1,0:T(8,128)(2,1)S(1)} collective-permute-done((bf16[32,4096]{1,0:T(8,128)(2,1)S(1)}, bf16[32,4096]{1,0:T(8,128)(2,1)S(1)}, u32[]{:S(2)}, u32[]{:S(2)}) %collective-permute-start.25) | collective-permute-done | bytes 262176 | tf_op jit(solution)/shard_map/ppermute | solution.py:174
  93.3 4.6 %collective-permute-done.26 = bf16[32,4096]{1,0:T(8,128)(2,1)S(1)} collective-permute-done((bf16[32,4096]{1,0:T(8,128)(2,1)S(1)}, bf16[32,4096]{1,0:T(8,128)(2,1)S(1)}, u32[]{:S(2)}, u32[]{:S(2)}) %collective-permute-start.26) | collective-permute-done | bytes 262176 | tf_op jit(solution)/shard_map/ppermute | solution.py:174
  98.0 1.3 %collective-permute-done.27 = bf16[32,4096]{1,0:T(8,128)(2,1)S(1)} collective-permute-done((bf16[32,4096]{1,0:T(8,128)(2,1)S(1)}, bf16[32,4096]{1,0:T(8,128)(2,1)S(1)}, u32[]{:S(2)}, u32[]{:S(2)}) %collective-permute-start.27) | collective-permute-done | bytes 262176 | tf_op jit(solution)/shard_map/ppermute | solution.py:174
  99.3 0.7 constant_dynamic-update-slice_fusion
  (73 shorter events, 3.0 us)
Async XLA Ops:
  4.2 16.9 %all-to-all-start = ((bf16[8,72,128]{2,1,0:T(8,128)(2,1)}), bf16[8,72,128]{2,1,0:T(8,128)(2,1)S(1)}, u32[]{:S(2)}, u32[]{:S(2)}) async-start(bf16[8,72,128]{2,1,0:T(8,128)(2,1)} %fusion.7), calls=%async_computation | async-start | bytes 294912 | tf_op jit(solution)/shard_map/all_to_all | solution.py:136
  14.5 9.2 %collective-permute-start.20 = (bf16[32,4096]{1,0:T(8,128)(2,1)S(1)}, bf16[32,4096]{1,0:T(8,128)(2,1)S(1)}, u32[]{:S(2)}, u32[]{:S(2)}) collective-permute-start(bf16[32,4096]{1,0:T(8,128)(2,1)S(1)} %get-tuple-element.10), channel_id=1, source_target_pairs={{0,4},{2,6},{4,8},{6,10},{8,12},{10,14},{12,0},{14,2},{1,5},{3,7},... | collective-permute-start | bytes 786440 | tf_op jit(solution)/shard_map/ppermute | solution.py:144
  15.8 13.5 %collective-permute-start.21 = (bf16[32,4096]{1,0:T(8,128)(2,1)S(1)}, bf16[32,4096]{1,0:T(8,128)(2,1)S(1)}, u32[]{:S(2)}, u32[]{:S(2)}) collective-permute-start(bf16[32,4096]{1,0:T(8,128)(2,1)S(1)} %get-tuple-element.12), channel_id=1, source_target_pairs={{0,8},{2,10},{4,12},{6,14},{8,0},{10,2},{12,4},{14,6},{1,9},{3,11}... | collective-permute-start | bytes 786440 | tf_op jit(solution)/shard_map/ppermute | solution.py:144
  18.2 13.8 %collective-permute-start.22 = (bf16[32,4096]{1,0:T(8,128)(2,1)S(1)}, bf16[32,4096]{1,0:T(8,128)(2,1)S(1)}, u32[]{:S(2)}, u32[]{:S(2)}) collective-permute-start(bf16[32,4096]{1,0:T(8,128)(2,1)S(1)} %get-tuple-element.11), channel_id=1, source_target_pairs={{0,12},{2,14},{4,0},{6,2},{8,4},{10,6},{12,8},{14,10},{1,13},{3,15... | collective-permute-start | bytes 786440 | tf_op jit(solution)/shard_map/ppermute | solution.py:144
  21.2 11.3 %collective-permute-start.12 = (bf16[8,32,128]{2,1,0:T(8,128)(2,1)S(1)}, bf16[8,32,128]{2,1,0:T(8,128)(2,1)S(1)}, u32[]{:S(2)}, u32[]{:S(2)}) collective-permute-start(bf16[8,32,128]{2,1,0:T(8,128)(2,1)S(1)} %get-tuple-element.22), channel_id=1, source_target_pairs={{0,12},{2,14},{4,0},{6,2},{8,4},{10,6},{12,8},{14,10},{1,13},{3,15... | collective-permute-start | bytes 196616 | tf_op jit(solution)/shard_map/ppermute | solution.py:99
  23.7 9.5 %collective-permute-start.10 = (bf16[8,32,128]{2,1,0:T(8,128)(2,1)S(1)}, bf16[8,32,128]{2,1,0:T(8,128)(2,1)S(1)}, u32[]{:S(2)}, u32[]{:S(2)}) collective-permute-start(bf16[8,32,128]{2,1,0:T(8,128)(2,1)S(1)} %get-tuple-element.22), channel_id=1, source_target_pairs={{0,4},{2,6},{4,8},{6,10},{8,12},{10,14},{12,0},{14,2},{1,5},{3,7},... | collective-permute-start | bytes 196616 | tf_op jit(solution)/shard_map/ppermute | solution.py:99
  23.7 9.5 %collective-permute-start.11 = (bf16[8,32,128]{2,1,0:T(8,128)(2,1)S(1)}, bf16[8,32,128]{2,1,0:T(8,128)(2,1)S(1)}, u32[]{:S(2)}, u32[]{:S(2)}) collective-permute-start(bf16[8,32,128]{2,1,0:T(8,128)(2,1)S(1)} %get-tuple-element.22), channel_id=1, source_target_pairs={{0,8},{2,10},{4,12},{6,14},{8,0},{10,2},{12,4},{14,6},{1,9},{3,11}... | collective-permute-start | bytes 196616 | tf_op jit(solution)/shard_map/ppermute | solution.py:99
  29.3 7.2 %collective-permute-start.2 = (bf16[8,40,128]{2,1,0:T(8,128)(2,1)S(1)}, bf16[8,40,128]{2,1,0:T(8,128)(2,1)S(1)}, u32[]{:S(2)}, u32[]{:S(2)}) collective-permute-start(bf16[8,40,128]{2,1,0:T(8,128)(2,1)S(1)} %slice.50), channel_id=1, source_target_pairs={{0,192},{16,208},{32,224},{48,240},{1,193},{17,209},{33,225},{49,2... | collective-permute-start | bytes 245768 | tf_op jit(solution)/shard_map/ppermute | solution.py:99
  32.0 5.5 %collective-permute-start.1 = (bf16[8,40,128]{2,1,0:T(8,128)(2,1)S(1)}, bf16[8,40,128]{2,1,0:T(8,128)(2,1)S(1)}, u32[]{:S(2)}, u32[]{:S(2)}) collective-permute-start(bf16[8,40,128]{2,1,0:T(8,128)(2,1)S(1)} %slice.50), channel_id=1, source_target_pairs={{0,128},{16,144},{32,160},{48,176},{1,129},{17,145},{33,161},{49,1... | collective-permute-start | bytes 245768 | tf_op jit(solution)/shard_map/ppermute | solution.py:99
  32.4 12.8 %collective-permute-start = (bf16[8,40,128]{2,1,0:T(8,128)(2,1)S(1)}, bf16[8,40,128]{2,1,0:T(8,128)(2,1)S(1)}, u32[]{:S(2)}, u32[]{:S(2)}) collective-permute-start(bf16[8,40,128]{2,1,0:T(8,128)(2,1)S(1)} %slice.50), channel_id=1, source_target_pairs={{0,64},{16,80},{32,96},{48,112},{1,65},{17,81},{33,97},{49,113},{6... | collective-permute-start | bytes 245768 | tf_op jit(solution)/shard_map/ppermute | solution.py:99
  33.2 37.3 %copy-start.8 = (bf16[64,128]{1,0:T(8,128)(2,1)S(1)}, bf16[64,128]{1,0:T(8,128)(2,1)}, u32[]{:S(2)}) copy-start(bf16[64,128]{1,0:T(8,128)(2,1)} %refs_20_.1) | copy-start | bytes 49156
  33.2 13.0 %collective-permute-start.13 = (bf16[4,8,32,128]{3,2,1,0:T(8,128)(2,1)S(1)}, bf16[4,8,32,128]{3,2,1,0:T(8,128)(2,1)S(1)}, u32[]{:S(2)}, u32[]{:S(2)}) collective-permute-start(bf16[4,8,32,128]{3,2,1,0:T(8,128)(2,1)S(1)} %pad_maximum_fusion.3.refs_8_), channel_id=1, source_target_pairs={{0,64},{16,80},{32,96},{48,112},{1,65},{17,81},{33,97},{49,113},{6... | collective-permute-start | bytes 786440 | tf_op jit(solution)/shard_map/ppermute | solution.py:99
  34.9 13.6 %collective-permute-start.14 = (bf16[4,8,32,128]{3,2,1,0:T(8,128)(2,1)S(1)}, bf16[4,8,32,128]{3,2,1,0:T(8,128)(2,1)S(1)}, u32[]{:S(2)}, u32[]{:S(2)}) collective-permute-start(bf16[4,8,32,128]{3,2,1,0:T(8,128)(2,1)S(1)} %pad_maximum_fusion.3.refs_8_), channel_id=1, source_target_pairs={{0,128},{16,144},{32,160},{48,176},{1,129},{17,145},{33,161},{49,1... | collective-permute-start | bytes 786440 | tf_op jit(solution)/shard_map/ppermute | solution.py:99
  36.5 13.1 %collective-permute-start.15 = (bf16[4,8,32,128]{3,2,1,0:T(8,128)(2,1)S(1)}, bf16[4,8,32,128]{3,2,1,0:T(8,128)(2,1)S(1)}, u32[]{:S(2)}, u32[]{:S(2)}) collective-permute-start(bf16[4,8,32,128]{3,2,1,0:T(8,128)(2,1)S(1)} %pad_maximum_fusion.3.refs_8_), channel_id=1, source_target_pairs={{0,192},{16,208},{32,224},{48,240},{1,193},{17,209},{33,225},{49,2... | collective-permute-start | bytes 786440 | tf_op jit(solution)/shard_map/ppermute | solution.py:99
  37.4 11.1 %copy-start.10 = (bf16[8,40,128]{2,1,0:T(8,128)(2,1)}, bf16[8,40,128]{2,1,0:T(8,128)(2,1)S(1)}, u32[]{:S(2)}) copy-start(bf16[8,40,128]{2,1,0:T(8,128)(2,1)S(1)} %collective-permute-done.1) | copy-start | bytes 245764
  37.5 17.3 %collective-permute-start.16 = (bf16[4,8,32,128]{3,2,1,0:T(8,128)(2,1)S(1)}, bf16[4,8,32,128]{3,2,1,0:T(8,128)(2,1)S(1)}, u32[]{:S(2)}, u32[]{:S(2)}) collective-permute-start(bf16[4,8,32,128]{3,2,1,0:T(8,128)(2,1)S(1)} %pad_maximum_fusion.3.refs_8_), channel_id=1, source_target_pairs={{0,2},{2,0},{4,6},{6,4},{8,10},{10,8},{12,14},{14,12},{1,3},{3,1},... | collective-permute-start | bytes 786440 | tf_op jit(solution)/shard_map/ppermute | solution.py:156
  45.3 3.3 %copy-start.11 = (bf16[8,40,128]{2,1,0:T(8,128)(2,1)}, bf16[8,40,128]{2,1,0:T(8,128)(2,1)S(1)}, u32[]{:S(2)}) copy-start(bf16[8,40,128]{2,1,0:T(8,128)(2,1)S(1)} %collective-permute-done) | copy-start | bytes 245764
  45.3 14.8 %collective-permute-start.3 = (bf16[4,8,32,128]{3,2,1,0:T(8,128)(2,1)S(1)}, bf16[4,8,32,128]{3,2,1,0:T(8,128)(2,1)S(1)}, u32[]{:S(2)}, u32[]{:S(2)}) collective-permute-start(bf16[4,8,32,128]{3,2,1,0:T(8,128)(2,1)S(1)} %pad_maximum_fusion.2.refs_0_), channel_id=1, source_target_pairs={{0,4},{2,6},{4,8},{6,10},{8,12},{10,14},{12,0},{14,2},{1,5},{3,7},... | collective-permute-start | bytes 786440 | tf_op jit(solution)/shard_map/ppermute | solution.py:99
  46.3 19.7 %collective-permute-start.23 = (bf16[128,2048]{1,0:T(8,128)(2,1)}, bf16[128,2048]{1,0:T(8,128)(2,1)S(1)}, u32[]{:S(2)}, u32[]{:S(2)}) collective-permute-start(bf16[128,2048]{1,0:T(8,128)(2,1)} %get-tuple-element.19), channel_id=1, source_target_pairs={{0,2},{2,0},{4,6},{6,4},{8,10},{10,8},{12,14},{14,12},{1,3},{3,1},... | collective-permute-start | bytes 1572872 | tf_op jit(solution)/shard_map/ppermute | solution.py:147
  48.6 13.9 %collective-permute-start.4 = (bf16[4,8,32,128]{3,2,1,0:T(8,128)(2,1)S(1)}, bf16[4,8,32,128]{3,2,1,0:T(8,128)(2,1)S(1)}, u32[]{:S(2)}, u32[]{:S(2)}) collective-permute-start(bf16[4,8,32,128]{3,2,1,0:T(8,128)(2,1)S(1)} %pad_maximum_fusion.2.refs_0_), channel_id=1, source_target_pairs={{0,8},{2,10},{4,12},{6,14},{8,0},{10,2},{12,4},{14,6},{1,9},{3,11}... | collective-permute-start | bytes 786440 | tf_op jit(solution)/shard_map/ppermute | solution.py:99
  49.6 14.1 %collective-permute-start.5 = (bf16[4,8,32,128]{3,2,1,0:T(8,128)(2,1)S(1)}, bf16[4,8,32,128]{3,2,1,0:T(8,128)(2,1)S(1)}, u32[]{:S(2)}, u32[]{:S(2)}) collective-permute-start(bf16[4,8,32,128]{3,2,1,0:T(8,128)(2,1)S(1)} %pad_maximum_fusion.2.refs_0_), channel_id=1, source_target_pairs={{0,12},{2,14},{4,0},{6,2},{8,4},{10,6},{12,8},{14,10},{1,13},{3,15... | collective-permute-start | bytes 786440 | tf_op jit(solution)/shard_map/ppermute | solution.py:99
  54.7 10.5 %collective-permute-start.6 = (bf16[4,8,32,128]{3,2,1,0:T(8,128)(2,1)S(1)}, bf16[4,8,32,128]{3,2,1,0:T(8,128)(2,1)S(1)}, u32[]{:S(2)}, u32[]{:S(2)}) collective-permute-start(bf16[4,8,32,128]{3,2,1,0:T(8,128)(2,1)S(1)} %pad_maximum_fusion.2.refs_0_), channel_id=1, source_target_pairs={{0,2},{2,0},{4,6},{6,4},{8,10},{10,8},{12,14},{14,12},{1,3},{3,1},... | collective-permute-start | bytes 786440 | tf_op jit(solution)/shard_map/ppermute | solution.py:155
  60.1 6.3 %collective-permute-start.17 = (bf16[4,8,32,128]{3,2,1,0:T(8,128)(2,1)S(1)}, bf16[4,8,32,128]{3,2,1,0:T(8,128)(2,1)S(1)}, u32[]{:S(2)}, u32[]{:S(2)}) collective-permute-start(bf16[4,8,32,128]{3,2,1,0:T(8,128)(2,1)S(1)} %collective-permute-done.13.refs_9_), channel_id=1, source_target_pairs={{0,2},{2,0},{4,6},{6,4},{8,10},{10,8},{12,14},{14,12},{1,3},{3,1},... | collective-permute-start | bytes 786440 | tf_op jit(solution)/shard_map/ppermute | solution.py:156
  62.5 8.0 %copy-start = (bf16[4,8,32,128]{3,2,1,0:T(8,128)(2,1)}, bf16[4,8,32,128]{3,2,1,0:T(8,128)(2,1)S(1)}, u32[]{:S(2)}) copy-start(bf16[4,8,32,128]{3,2,1,0:T(8,128)(2,1)S(1)} %collective-permute-done.4.refs_2_) | copy-start | bytes 786436
  62.5 8.0 %collective-permute-start.18 = (bf16[4,8,32,128]{3,2,1,0:T(8,128)(2,1)S(1)}, bf16[4,8,32,128]{3,2,1,0:T(8,128)(2,1)}, u32[]{:S(2)}, u32[]{:S(2)}) collective-permute-start(bf16[4,8,32,128]{3,2,1,0:T(8,128)(2,1)S(1)} %collective-permute-done.14.refs_10_), channel_id=1, source_target_pairs={{0,2},{2,0},{4,6},{6,4},{8,10},{10,8},{12,14},{14,12},{1,3},{3,1},... | collective-permute-start | bytes 786440 | tf_op jit(solution)/shard_map/ppermute | solution.py:156
  63.7 6.8 %copy-start.2 = (bf16[4,8,32,128]{3,2,1,0:T(8,128)(2,1)}, bf16[4,8,32,128]{3,2,1,0:T(8,128)(2,1)S(1)}, u32[]{:S(2)}) copy-start(bf16[4,8,32,128]{3,2,1,0:T(8,128)(2,1)S(1)} %collective-permute-done.5.refs_3_) | copy-start | bytes 786436
  63.7 6.7 %collective-permute-start.19 = (bf16[4,8,32,128]{3,2,1,0:T(8,128)(2,1)S(1)}, bf16[4,8,32,128]{3,2,1,0:T(8,128)(2,1)}, u32[]{:S(2)}, u32[]{:S(2)}) collective-permute-start(bf16[4,8,32,128]{3,2,1,0:T(8,128)(2,1)S(1)} %collective-permute-done.15.refs_11_), channel_id=1, source_target_pairs={{0,2},{2,0},{4,6},{6,4},{8,10},{10,8},{12,14},{14,12},{1,3},{3,1},... | collective-permute-start | bytes 786440 | tf_op jit(solution)/shard_map/ppermute | solution.py:156
  65.2 0.7 copy-start.4
  65.9 4.5 %collective-permute-start.7 = (bf16[4,8,32,128]{3,2,1,0:T(8,128)(2,1)S(1)}, bf16[4,8,32,128]{3,2,1,0:T(8,128)(2,1)}, u32[]{:S(2)}, u32[]{:S(2)}) collective-permute-start(bf16[4,8,32,128]{3,2,1,0:T(8,128)(2,1)S(1)} %collective-permute-done.3.refs_1_), channel_id=1, source_target_pairs={{0,2},{2,0},{4,6},{6,4},{8,10},{10,8},{12,14},{14,12},{1,3},{3,1},... | collective-permute-start | bytes 786440 | tf_op jit(solution)/shard_map/ppermute | solution.py:155
  66.0 4.5 %collective-permute-start.8 = (bf16[4,8,32,128]{3,2,1,0:T(8,128)(2,1)S(1)}, bf16[4,8,32,128]{3,2,1,0:T(8,128)(2,1)}, u32[]{:S(2)}, u32[]{:S(2)}) collective-permute-start(bf16[4,8,32,128]{3,2,1,0:T(8,128)(2,1)S(1)} %collective-permute-done.4.refs_2_), channel_id=1, source_target_pairs={{0,2},{2,0},{4,6},{6,4},{8,10},{10,8},{12,14},{14,12},{1,3},{3,1},... | collective-permute-start | bytes 786440 | tf_op jit(solution)/shard_map/ppermute | solution.py:155
  66.4 0.7 copy-start.6
  67.2 3.3 %collective-permute-start.9 = (bf16[4,8,32,128]{3,2,1,0:T(8,128)(2,1)S(1)}, bf16[4,8,32,128]{3,2,1,0:T(8,128)(2,1)}, u32[]{:S(2)}, u32[]{:S(2)}) collective-permute-start(bf16[4,8,32,128]{3,2,1,0:T(8,128)(2,1)S(1)} %collective-permute-done.5.refs_3_), channel_id=1, source_target_pairs={{0,2},{2,0},{4,6},{6,4},{8,10},{10,8},{12,14},{14,12},{1,3},{3,1},... | collective-permute-start | bytes 786440 | tf_op jit(solution)/shard_map/ppermute | solution.py:155
  70.5 1.0 copy-start.1
  71.5 0.9 copy-start.3
  72.4 0.9 copy-start.5
  73.4 0.9 copy-start.7
  80.7 2.2 %collective-permute-start.24 = (bf16[128,2048]{1,0:T(8,128)(2,1)}, bf16[128,2048]{1,0:T(8,128)(2,1)S(1)}, u32[]{:S(2)}, u32[]{:S(2)}) collective-permute-start(bf16[128,2048]{1,0:T(8,128)(2,1)} %get-tuple-element.8), channel_id=1, source_target_pairs={{0,2},{2,0},{4,6},{6,4},{8,10},{10,8},{12,14},{14,12},{1,3},{3,1},... | collective-permute-start | bytes 1572872 | tf_op jit(solution)/shard_map/ppermute | solution.py:167
  83.2 10.1 %collective-permute-start.25 = (bf16[32,4096]{1,0:T(8,128)(2,1)S(1)}, bf16[32,4096]{1,0:T(8,128)(2,1)S(1)}, u32[]{:S(2)}, u32[]{:S(2)}) collective-permute-start(bf16[32,4096]{1,0:T(8,128)(2,1)S(1)} %get-tuple-element.15), channel_id=1, source_target_pairs={{0,8},{2,10},{4,12},{6,14},{8,0},{10,2},{12,4},{14,6},{1,9},{3,11}... | collective-permute-start | bytes 786440 | tf_op jit(solution)/shard_map/ppermute | solution.py:174
  86.9 11.1 %collective-permute-start.26 = (bf16[32,4096]{1,0:T(8,128)(2,1)S(1)}, bf16[32,4096]{1,0:T(8,128)(2,1)S(1)}, u32[]{:S(2)}, u32[]{:S(2)}) collective-permute-start(bf16[32,4096]{1,0:T(8,128)(2,1)S(1)} %get-tuple-element.16), channel_id=1, source_target_pairs={{0,12},{2,14},{4,0},{6,2},{8,4},{10,6},{12,8},{14,10},{1,13},{3,15... | collective-permute-start | bytes 786440 | tf_op jit(solution)/shard_map/ppermute | solution.py:174
  87.4 11.9 %collective-permute-start.27 = (bf16[32,4096]{1,0:T(8,128)(2,1)S(1)}, bf16[32,4096]{1,0:T(8,128)(2,1)S(1)}, u32[]{:S(2)}, u32[]{:S(2)}) collective-permute-start(bf16[32,4096]{1,0:T(8,128)(2,1)S(1)} %get-tuple-element.13), channel_id=1, source_target_pairs={{0,4},{2,6},{4,8},{6,10},{8,12},{10,14},{12,0},{14,2},{1,5},{3,7},... | collective-permute-start | bytes 786440 | tf_op jit(solution)/shard_map/ppermute | solution.py:174
  98.0 1.3 %copy-start.9 = (bf16[32,16384]{1,0:T(8,128)(2,1)}, bf16[32,16384]{1,0:T(8,128)(2,1)S(1)}, u32[]{:S(2)}) copy-start(bf16[32,16384]{1,0:T(8,128)(2,1)S(1)} %constant_dynamic-update-slice_fusion.1) | copy-start | bytes 3145732

commit v3 on v1

v3 whole, which is shorter than its diff:
```python
import jax
import jax.numpy as jnp
from jax import lax
from jax.experimental import pallas as pl
from jax.experimental.pallas import tpu as pltpu
from jax.sharding import PartitionSpec as P

M = 256
EMPTY = 512
X, Y, Z = 4, 4, 8
LIST_ROWS = 16
DN_NT = (((1,), (1,)), ((), ()))
DN_TN = (((0,), (0,)), ((), ()))


def update_kernel(*refs):
    n_side = Y + 1
    n_data = 2 * n_side
    data_hbm, (near_hbm, far_hbm, table_ref) = refs[:n_data], refs[n_data : n_data + 3]
    out_near, out_far, data, state, cols, weights, sems, state_sems = refs[n_data + 3 :]
    data_rows = data.shape[3] - LIST_ROWS
    mem_dev = data_rows // (2 * X)
    data_dev = data.shape[4]
    half = X * mem_dev
    n_block = near_hbm.shape[1] // 128

    loads = {}
    for t in range(n_side):
        for side in range(2):
            if t < 2:
                dst = data.at[side, t]
            elif t < 4:
                dst = data.at[side, 2, pl.ds((t - 2) * (Z // 2), Z // 2)]
            else:
                dst = data.at[side, 3]
            loads[side, t] = pltpu.make_async_copy(data_hbm[side * n_side + t], dst, sems.at[side, t])
            loads[side, t].start()
    state_loads = [pltpu.make_async_copy(src, state.at[i], state_sems.at[i]) for i, src in enumerate((near_hbm, far_hbm))]
    for load in state_loads:
        load.start()
    for load in loads.values():
        load.wait()

    me_cell = lax.axis_index("cell")
    me_row = lax.axis_index("dp") * Y + lax.div(me_cell, 4)
    list_rows = lax.broadcasted_iota(jnp.int32, (LIST_ROWS, 128), 0)
    lists = []
    for g in range(2):
        for pair in range(Y * Z // 2):
            t, j = pair // (Z // 2), 2 * (pair % (Z // 2)) + g
            rows = data[0, t, j, data_rows : data_rows + LIST_ROWS].astype(jnp.float32)
            lists.append(jnp.sum(jnp.where(list_rows == me_row, rows, 0.0), axis=0, keepdims=True))
    lists = jnp.concatenate(lists + [jnp.zeros((128 - Y * Z, 128), jnp.float32)], axis=0).T
    later = pltpu.roll(lists, 128 - 2 * Z, 1)
    is_first = lax.rem(lax.broadcasted_iota(jnp.int32, (128, 128), 0), 8) < 4
    ids = jnp.where(is_first, lists, pltpu.roll(later, 4, 0) + data_dev)
    prof_ids = jnp.where(is_first, pltpu.roll(lists, 124, 0), later)

    table = table_ref[...]
    lanes = lax.broadcasted_iota(jnp.int32, (128, 2 * data_dev), 1).astype(jnp.float32)
    prof_lanes = lax.broadcasted_iota(jnp.int32, (128, table.shape[0]), 1).astype(jnp.float32)
    for pair in range(Y * Z // 2):
        t, q = pair // (Z // 2), pair % (Z // 2)
        place = slice(pair * 8, (pair + 1) * 8)
        chooser = jnp.where(prof_lanes == prof_ids[:, pair : pair + 1], 1.0, 0.0).astype(jnp.bfloat16)
        weight = jnp.dot(chooser, table, preferred_element_type=jnp.float32)
        weights[:, place] = weight.reshape(n_block, 8, 128)
        picker = jnp.where(lanes == ids[:, pair : pair + 1], 1.0, 0.0).astype(jnp.bfloat16)
        for side in range(2):
            values = jnp.concatenate(
                [
                    jnp.concatenate(
                        [
                            data[side, t, 2 * q + g, (2 * s + a) * mem_dev : (2 * s + a + 1) * mem_dev]
                            for a in range(2)
                            for s in range(X)
                        ],
                        axis=0,
                    )
                    for g in range(2)
                ],
                axis=1,
            )
            picked = lax.dot_general(picker, values, DN_NT, preferred_element_type=jnp.float32)
            picked = picked.reshape(n_block, 8, 2 * half)
            for a in range(2):
                cols[a, :, place, side * half : (side + 1) * half] = picked[:, :, a * half : (a + 1) * half]

    for load in state_loads:
        load.wait()
    for b in range(n_block):
        spot = pl.ds(b * 128, 128)
        own = jnp.concatenate([state[0, :, spot], state[1, :, spot]], axis=0)
        anom = cols[0, b].astype(jnp.bfloat16)
        innov = cols[1, b].astype(jnp.bfloat16)
        inner = jnp.dot(anom, own, preferred_element_type=jnp.float32)
        coef = (weights[b] * inner / (M - 1)).astype(jnp.bfloat16)
        corr = lax.dot_general(innov, coef, DN_TN, preferred_element_type=jnp.float32)
        new = (own.astype(jnp.float32) + corr).astype(jnp.bfloat16)
        out_near[:, spot] = new[:half]
        out_far[:, spot] = new[half:]


def run_update(data, near, far, table):
    half, width = near.shape
    n_block = width // 128
    n_slot = Y * Z * 4
    any_space = pl.BlockSpec(memory_space=pl.ANY)
    whole = pl.BlockSpec(memory_space=pltpu.VMEM)
    return pl.pallas_call(
        update_kernel,
        out_shape=[jax.ShapeDtypeStruct(near.shape, jnp.bfloat16)] * 2,
        in_specs=[any_space] * (len(data) + 2) + [whole],
        out_specs=[whole] * 2,
        scratch_shapes=[
            pltpu.VMEM((2, Y) + data[0].shape, jnp.bfloat16),
            pltpu.VMEM((2,) + near.shape, jnp.bfloat16),
            pltpu.VMEM((2, n_block, n_slot, 2 * half), jnp.float32),
            pltpu.VMEM((n_block, n_slot, 128), jnp.float32),
            pltpu.SemaphoreType.DMA((2, Y + 1)),
            pltpu.SemaphoreType.DMA((2,)),
        ],
        compiler_params=pltpu.CompilerParams(vmem_limit_bytes=24 * 1024 * 1024),
        cost_estimate=pl.CostEstimate(flops=800_000_000, bytes_accessed=6_500_000, transcendentals=0),
        name="update",
    )(*data, near, far, table)


def line(y, z):
    return (y * 4 + z % 4) * 2 + z // 4


X_SHIFT = [[(x * 2 + c, ((x + s) % X) * 2 + c) for x in range(X) for c in range(2)] for s in range(X)]
Y_SHIFT = [[(line(y, z), line((y + s) % Y, z)) for y in range(Y) for z in range(Z)] for s in range(Y)]
Z_SHIFT = [[(line(y, z), line(y, (z + s) % Z)) for y in range(Y) for z in range(Z)] for s in range(Z)]
CORE_SWAP = [(i, i ^ 1) for i in range(2 * X)]


def to_x(piece, s):
    return lax.ppermute(piece, "mem", X_SHIFT[s % X])


def to_y(piece, s):
    return lax.ppermute(piece, ("cell", "dp"), Y_SHIFT[s % Y])


def to_z(piece, s):
    return lax.ppermute(piece, ("cell", "dp"), Z_SHIFT[s % Z])


def swap(piece):
    return lax.ppermute(piece, "mem", CORE_SWAP)


def after(piece, other):
    return lax.optimization_barrier((piece, other))[0]


def local(ensemble, data_anom, weighted_innov, profiles, seg_data, seg_profile):
    n_group = lax.axis_size("cell") * lax.axis_size("dp")
    n_mem = lax.axis_size("mem")
    me_cell, me_dp, me_mem = (lax.axis_index(n) for n in ("cell", "dp", "mem"))
    me_x, me_core = me_mem // 2, me_mem % 2
    mem_dev, cells_dev = ensemble.shape
    data_dev = data_anom.shape[1]
    per_group, blocks = seg_data.shape
    own_blocks = blocks // (n_group * n_mem)
    half_cells = cells_dev // 2
    x_cells = half_cells // X
    own_cells = x_cells // 2

    own = lax.optimization_barrier(jnp.concatenate([data_anom, weighted_innov], axis=0))
    by_x = [own] + [None] * 3
    for s in (2, 1, 3):
        by_x[s] = to_x(own, s)

    def mine(seg):
        seg = seg.reshape(per_group, n_group, n_mem * own_blocks)
        return lax.dynamic_slice_in_dim(seg, me_mem * own_blocks, own_blocks, 2)

    group = me_cell * 2 + me_dp
    local_ids = jnp.where(seg_data >= 0, seg_data - group * data_dev, EMPTY)
    lists = jnp.stack([mine(local_ids), mine(seg_profile)]).astype(jnp.bfloat16)
    lists = lists.reshape(2, per_group, Y, Z, own_blocks).transpose(3, 2, 4, 0, 1)
    lists = lists.reshape(n_group, own_blocks * 2 * per_group)
    lists = jnp.pad(lists, ((0, LIST_ROWS - 8), (0, 0)))

    unit = jnp.concatenate(by_x + [lists], axis=0)
    data_rows = 2 * mem_dev * X
    by_z = [unit] + [None] * (Z - 1)
    for s in (4, 3, 5, 2, 6, 1, 7):
        by_z[s] = to_z(unit, s)
    first_row = data_rows + (me_cell % 4) * 8
    unit = jnp.stack(
        [
            jnp.concatenate([p[:data_rows], lax.dynamic_slice_in_dim(p, first_row, LIST_ROWS, 0)], axis=0)
            for p in by_z
        ]
    )

    up, down = to_y(unit, 1), to_y(unit, -1)
    up2, down2 = to_y(up[: Z // 2], 1), to_y(down[Z // 2 :], -1)
    data_near = [unit, up, up2, down2, down]
    data_far = [swap(d) for d in data_near]

    def state_for(s):
        x_to = (me_x + s) % X
        return lax.dynamic_slice_in_dim(ensemble, me_dp * half_cells + x_to * x_cells, x_cells, 1)

    pieces = [state_for(0)] + [None] * 3
    last = by_x[2]
    for s in (2, 1, 3):
        pieces[s] = last = to_x(after(state_for(s), last), s)
    state = jnp.concatenate(pieces, axis=0)
    near = lax.dynamic_slice_in_dim(state, me_core * own_cells, own_cells, 1)
    far = swap(lax.dynamic_slice_in_dim(state, (1 - me_core) * own_cells, own_cells, 1))

    new_near, new_far = run_update(data_near + data_far, near, far, profiles)

    back_far = swap(new_far)
    first = me_core == 0
    new = jnp.concatenate([jnp.where(first, new_near, back_far), jnp.where(first, back_far, new_near)], axis=1)
    out = jnp.zeros((mem_dev, half_cells), jnp.bfloat16)
    for s in (0, 2, 1, 3):
        piece = new[s * mem_dev : (s + 1) * mem_dev]
        if s:
            piece = to_x(piece, -s)
        out = lax.dynamic_update_slice_in_dim(out, piece, ((me_x + s) % X) * x_cells, 1)
    return out


def solution(mesh):
    placed = (
        P("mem", "cell"),
        P("mem", ("cell", "dp")),
        P("mem", ("cell", "dp")),
        P(),
        P(("cell", "dp"), None),
        P(("cell", "dp"), None),
    )
    return jax.shard_map(
        local, mesh=mesh, in_specs=placed, out_specs=P("mem", ("cell", "dp")), check_vma=False
    )
```

time: 90.6 us -> 85.9 us (0.948); the launches traced: 88.8 us -> 85.3 us
  waiting for transfers between devices: 29.8 us -> 34.7 us
  other arithmetic: 5.73 us -> 2.03 us
  Pallas kernels: 6.65 us -> 3.67 us
  starting transfers between devices: 41.6 us -> 40.6 us
    ppermute x15 -> x27, waiting for transfers between devices: 18.6 us -> 34.7 us  [the longest x9 20.1 us: to_x(): return lax.ppermute(piece, 'mem', X_SHIFT[s % X])]
    all_to_all x1 -> x0, starting transfers between devices: 12 us -> none  [local(): got = lax.all_to_all(sent, ('cell', 'dp'), 0, 0, tiled=True)]
    all_to_all x1 -> x0, waiting for transfers between devices: 11.2 us -> none  [local(): got = lax.all_to_all(sent, ('cell', 'dp'), 0, 0, tiled=True)]
    ppermute x15 -> x27, starting transfers between devices: 29.6 us -> 40.6 us  [the longest x7 16.7 us: to_z(): return lax.ppermute(piece, ('cell', 'dp'), Z_SHIFT[s % Z])]
    pallas_call x1, Pallas kernels: 6.65 us -> 3.67 us  [run_update(): pl.pallas_call(update_kernel, out_shape=[jax.ShapeDtypeStruct(near.shape,...]
    concatenate x1, other arithmetic: 1.1 us -> 0.08 us  [local(): state = jnp.concatenate(pieces, axis=0)]
    reshape x1 -> x0, other arithmetic: 1.01 us -> none  [mine(): seg = seg.reshape(per_group, n_group, n_mem * own_blocks)]
    unnamed x0 -> x7, other arithmetic: none -> 0.94 us
  transfers between devices with their start and end apart: 16 -> 27, of which waited for: 7 -> 13; matrix products, arithmetic and copies ran while one was open for 4% -> 5% of each run, Pallas kernels for 0% -> 0%
where the time goes in v3:
time: 85.9 us; the launch traced here: 85.3 us
  starting transfers between devices  40.6 us (47%)
  waiting for transfers between devices  34.7 us (40%)
  local copies, waits for them, and re-layouts  4.05 us (5%)
  Pallas kernels  3.67 us (4%)
  other arithmetic  2.03 us (2%)
    ppermute x9, waiting for transfers between devices, to_x(): return lax.ppermute(piece, 'mem', X_SHIFT[s % X])  20.1 us
    ppermute x7, starting transfers between devices, to_z(): return lax.ppermute(piece, ('cell', 'dp'), Z_SHIFT[s % Z])  16.7 us
    ppermute x7, starting transfers between devices, swap(): return lax.ppermute(piece, 'mem', CORE_SWAP)  9.15 us
    ppermute x9, starting transfers between devices, to_x(): return lax.ppermute(piece, 'mem', X_SHIFT[s % X])  9.04 us
    ppermute x7, waiting for transfers between devices, to_z(): return lax.ppermute(piece, ('cell', 'dp'), Z_SHIFT[s % Z])  8.85 us
    ppermute x4, starting transfers between devices, to_y(): return lax.ppermute(piece, ('cell', 'dp'), Y_SHIFT[s % Y])  5.71 us
    pallas_call x1, Pallas kernels, run_update(): pl.pallas_call(update_kernel, out_shape=[jax.ShapeDtypeStruct(near.shape,...  3.67 us
    ppermute x7, waiting for transfers between devices, swap(): return lax.ppermute(piece, 'mem', CORE_SWAP)  3.13 us
  transfers between devices with their start and end apart: 27, of which 13 were waited for; matrix products, arithmetic and copies ran while one was open for 5% of the time, Pallas kernels for 0%

profile of v3, /device:TPU:1, one launch (start us, length us, event | category | flops | bytes accessed | tf_op | source)
XLA Modules:
  0.0 85.3 jit_solution(1070453394102520665)
XLA Ops:
  0.0 0.7 pad_maximum_fusion.2
  0.7 3.6 %collective-permute-start.1 = (bf16[64,128]{1,0:T(8,128)(2,1)S(1)}, bf16[64,128]{1,0:T(8,128)(2,1)S(1)}, u32[]{:S(2)}, u32[]{:S(2)}) collective-permute-start(bf16[64,128]{1,0:T(8,128)(2,1)S(1)} %pad_maximum_fusion.2), channel_id=1, source_target_pairs={{0,8},{2,10},{4,12},{6,14},{8,0},{10,2},{12,4},{14,6},{1,9},{3,11}... | collective-permute-start | bytes 49160 | tf_op jit(solution)/shard_map/ppermute | solution.py:140
  4.3 0.3 collective-permute-start
  4.6 2.4 %collective-permute-start.2 = (bf16[64,128]{1,0:T(8,128)(2,1)S(1)}, bf16[64,128]{1,0:T(8,128)(2,1)S(1)}, u32[]{:S(2)}, u32[]{:S(2)}) collective-permute-start(bf16[64,128]{1,0:T(8,128)(2,1)S(1)} %pad_maximum_fusion.2), channel_id=1, source_target_pairs={{0,12},{2,14},{4,0},{6,2},{8,4},{10,6},{12,8},{14,10},{1,13},{3,15... | collective-permute-start | bytes 49160 | tf_op jit(solution)/shard_map/ppermute | solution.py:140
  7.0 0.9 %select_bitcast_fusion = s32[1,4,32,128]{3,1,2,0:T(4,128)S(1)} fusion(s32[4,4096]{1,0:T(4,128)} %param.10, s32[]{:T(128)S(6)} %mul.42), kind=kLoop, calls=%fused_computation.34 | loop fusion | flops 49152 | bytes 131076
  7.8 0.8 copy.12
  8.7 0.1 fusion.11
  8.8 1.3 %constant_dynamic-slice_fusion.5 = (bf16[32,4096]{1,0:T(8,128)(2,1)S(1)}, bf16[32,4096]{1,0:T(8,128)(2,1)S(1)}, bf16[32,4096]{1,0:T(8,128)(2,1)S(1)}, bf16[32,4096]{1,0:T(8,128)(2,1)S(1)}) fusion(bf16[32,32768]{1,0:T(8,128)(2,1)} %param.6, s32[]{:T(128)S(6)} %select_n.107, s32[]{:T(128)S(6)} %select_n.109, s32[]{:T(128)S(6)} %select_n.113, s32[]{:T(128)S(6)} %select_n.111), kind=kLoop, calls=%fused_computation.56 | loop fusion | bytes 2097168 | tf_op jit(solution)/shard_map/dynamic_slice | solution.py:208
  10.1 0.5 copy.7
  10.6 0.3 reshape.18
  11.0 1.7 %collective-permute-start.3 = (bf16[296,128]{1,0:T(8,128)(2,1)S(1)}, bf16[296,128]{1,0:T(8,128)(2,1)S(1)}, u32[]{:S(2)}, u32[]{:S(2)}) collective-permute-start(bf16[296,128]{1,0:T(8,128)(2,1)S(1)} %constant_dynamic-update-slice_fusion), channel_id=1, source_target_pairs={{0,16},{16,32},{32,48},{48,1},{1,17},{17,33},{33,49},{49,0},{64,80... | collective-permute-start | bytes 227336 | tf_op jit(solution)/shard_map/ppermute | solution.py:148
  12.7 3.0 %collective-permute-start.4 = (bf16[296,128]{1,0:T(8,128)(2,1)S(1)}, bf16[296,128]{1,0:T(8,128)(2,1)S(1)}, u32[]{:S(2)}, u32[]{:S(2)}) collective-permute-start(bf16[296,128]{1,0:T(8,128)(2,1)S(1)} %constant_dynamic-update-slice_fusion), channel_id=1, source_target_pairs={{0,32},{16,48},{32,1},{48,17},{1,33},{17,49},{33,0},{49,16},{64,96... | collective-permute-start | bytes 227336 | tf_op jit(solution)/shard_map/ppermute | solution.py:148
  15.7 3.8 %collective-permute-start.5 = (bf16[296,128]{1,0:T(8,128)(2,1)S(1)}, bf16[296,128]{1,0:T(8,128)(2,1)S(1)}, u32[]{:S(2)}, u32[]{:S(2)}) collective-permute-start(bf16[296,128]{1,0:T(8,128)(2,1)S(1)} %constant_dynamic-update-slice_fusion), channel_id=1, source_target_pairs={{0,48},{16,1},{32,17},{48,33},{1,49},{17,0},{33,16},{49,32},{64,11... | collective-permute-start | bytes 227336 | tf_op jit(solution)/shard_map/ppermute | solution.py:148
  19.5 0.5 collective-permute-start.6
  20.0 4.5 %collective-permute-start.7 = (bf16[296,128]{1,0:T(8,128)(2,1)S(1)}, bf16[296,128]{1,0:T(8,128)(2,1)S(1)}, u32[]{:S(2)}, u32[]{:S(2)}) collective-permute-start(bf16[296,128]{1,0:T(8,128)(2,1)S(1)} %constant_dynamic-update-slice_fusion), channel_id=1, source_target_pairs={{0,17},{16,33},{32,49},{48,0},{1,16},{17,32},{33,48},{49,1},{64,81... | collective-permute-start | bytes 227336 | tf_op jit(solution)/shard_map/ppermute | solution.py:148
  24.5 2.5 %collective-permute-start.8 = (bf16[296,128]{1,0:T(8,128)(2,1)S(1)}, bf16[296,128]{1,0:T(8,128)(2,1)S(1)}, u32[]{:S(2)}, u32[]{:S(2)}) collective-permute-start(bf16[296,128]{1,0:T(8,128)(2,1)S(1)} %constant_dynamic-update-slice_fusion), channel_id=1, source_target_pairs={{0,33},{16,49},{32,0},{48,16},{1,32},{17,48},{33,1},{49,17},{64,97... | collective-permute-start | bytes 227336 | tf_op jit(solution)/shard_map/ppermute | solution.py:148
  26.9 0.8 collective-permute-start.9
  27.8 0.1 collective-permute-start.19
  27.9 0.4 collective-permute-done.6
  28.3 0.7 collective-permute-done.7
  29.0 7.1 %collective-permute-done.8 = bf16[296,128]{1,0:T(8,128)(2,1)S(1)} collective-permute-done((bf16[296,128]{1,0:T(8,128)(2,1)S(1)}, bf16[296,128]{1,0:T(8,128)(2,1)S(1)}, u32[]{:S(2)}, u32[]{:S(2)}) %collective-permute-start.8) | collective-permute-done | bytes 75808 | tf_op jit(solution)/shard_map/ppermute | solution.py:148
  36.1 0.7 collective-permute-done.9
  36.9 1.4 %collective-permute-start.10 = (bf16[8,272,128]{2,1,0:T(8,128)(2,1)S(1)}, bf16[8,272,128]{2,1,0:T(8,128)(2,1)S(1)}, u32[]{:S(2)}, u32[]{:S(2)}) collective-permute-start(bf16[8,272,128]{2,1,0:T(8,128)(2,1)S(1)} %fusion.10.refs_0_), channel_id=1, source_target_pairs={{0,64},{16,80},{32,96},{48,112},{1,65},{17,81},{33,97},{49,113},{6... | collective-permute-start | bytes 1671176 | tf_op jit(solution)/shard_map/ppermute | solution.py:144
  38.3 1.5 %collective-permute-start.12 = (bf16[8,272,128]{2,1,0:T(8,128)(2,1)S(1)}, bf16[8,272,128]{2,1,0:T(8,128)(2,1)S(1)}, u32[]{:S(2)}, u32[]{:S(2)}) collective-permute-start(bf16[8,272,128]{2,1,0:T(8,128)(2,1)S(1)} %fusion.10.refs_0_), channel_id=1, source_target_pairs={{0,192},{16,208},{32,224},{48,240},{1,193},{17,209},{33,225},{49,2... | collective-permute-start | bytes 1671176 | tf_op jit(solution)/shard_map/ppermute | solution.py:144
  39.8 7.4 %collective-permute-done.20 = bf16[32,4096]{1,0:T(8,128)(2,1)S(1)} collective-permute-done((bf16[32,4096]{1,0:T(8,128)(2,1)S(1)}, bf16[32,4096]{1,0:T(8,128)(2,1)S(1)}, u32[]{:S(2)}, u32[]{:S(2)}) %collective-permute-start.20) | collective-permute-done | bytes 262176 | tf_op jit(solution)/shard_map/ppermute | solution.py:140
  47.2 2.5 %collective-permute-start.14 = (bf16[8,272,128]{2,1,0:T(8,128)(2,1)S(1)}, bf16[8,272,128]{2,1,0:T(8,128)(2,1)S(1)}, u32[]{:S(2)}, u32[]{:S(2)}) collective-permute-start(bf16[8,272,128]{2,1,0:T(8,128)(2,1)S(1)} %fusion.10.refs_0_), channel_id=1, source_target_pairs={{0,2},{2,0},{4,6},{6,4},{8,10},{10,8},{12,14},{14,12},{1,3},{3,1},... | collective-permute-start | bytes 1671176 | tf_op jit(solution)/shard_map/ppermute | solution.py:152
  49.8 1.5 %collective-permute-done.10.refs_1_ = bf16[8,272,128]{2,1,0:T(8,128)(2,1)S(1)} collective-permute-done((bf16[8,272,128]{2,1,0:T(8,128)(2,1)S(1)}, bf16[8,272,128]{2,1,0:T(8,128)(2,1)S(1)}, u32[]{:S(2)}, u32[]{:S(2)}) %collective-permute-start.10) | collective-permute-done | bytes 557088 | tf_op jit(solution)/shard_map/ppermute | solution.py:144
  51.3 0.1 collective-permute-start.11
  51.4 2.7 %collective-permute-start.13 = (bf16[4,272,128]{2,1,0:T(8,128)(2,1)S(1)}, bf16[4,272,128]{2,1,0:T(8,128)(2,1)S(1)}, u32[]{:S(2)}, u32[]{:S(2)}) collective-permute-start(bf16[4,272,128]{2,1,0:T(8,128)(2,1)S(1)} %slice.62), channel_id=1, source_target_pairs={{0,192},{16,208},{32,224},{48,240},{1,193},{17,209},{33,225},{49,2... | collective-permute-start | bytes 835592 | tf_op jit(solution)/shard_map/ppermute | solution.py:144
  54.1 2.6 %collective-permute-start.15 = (bf16[8,272,128]{2,1,0:T(8,128)(2,1)S(1)}, bf16[8,272,128]{2,1,0:T(8,128)(2,1)S(1)}, u32[]{:S(2)}, u32[]{:S(2)}) collective-permute-start(bf16[8,272,128]{2,1,0:T(8,128)(2,1)S(1)} %collective-permute-done.10.refs_1_), channel_id=1, source_target_pairs={{0,2},{2,0},{4,6},{6,4},{8,10},{10,8},{12,14},{14,12},{1,3},{3,1},... | collective-permute-start | bytes 1671176 | tf_op jit(solution)/shard_map/ppermute | solution.py:152
  56.8 0.1 pad_maximum_fusion
  56.8 0.1 constant_dynamic-slice_fusion
  57.0 0.6 collective-permute-start.22
  57.6 1.1 %collective-permute-done.11.refs_2_ = bf16[4,272,128]{2,1,0:T(8,128)(2,1)S(1)} collective-permute-done((bf16[4,272,128]{2,1,0:T(8,128)(2,1)S(1)}, bf16[4,272,128]{2,1,0:T(8,128)(2,1)S(1)}, u32[]{:S(2)}, u32[]{:S(2)}) %collective-permute-start.11) | collective-permute-done | bytes 278560 | tf_op jit(solution)/shard_map/ppermute | solution.py:144
  58.7 3.0 %collective-permute-start.16 = (bf16[4,272,128]{2,1,0:T(8,128)(2,1)S(1)}, bf16[4,272,128]{2,1,0:T(8,128)(2,1)S(1)}, u32[]{:S(2)}, u32[]{:S(2)}) collective-permute-start(bf16[4,272,128]{2,1,0:T(8,128)(2,1)S(1)} %collective-permute-done.11.refs_2_), channel_id=1, source_target_pairs={{0,2},{2,0},{4,6},{6,4},{8,10},{10,8},{12,14},{14,12},{1,3},{3,1},... | collective-permute-start | bytes 835592 | tf_op jit(solution)/shard_map/ppermute | solution.py:152
  61.6 1.2 %collective-permute-done.16.refs_7_ = bf16[4,272,128]{2,1,0:T(8,128)(2,1)S(1)} collective-permute-done((bf16[4,272,128]{2,1,0:T(8,128)(2,1)S(1)}, bf16[4,272,128]{2,1,0:T(8,128)(2,1)S(1)}, u32[]{:S(2)}, u32[]{:S(2)}) %collective-permute-start.16) | collective-permute-done | bytes 278560 | tf_op jit(solution)/shard_map/ppermute | solution.py:152
  62.8 0.4 collective-permute-done.17.refs_8_
  63.2 3.7 %update.1 = (bf16[128,2048]{1,0:T(8,128)(2,1)S(1)}, bf16[128,2048]{1,0:T(8,128)(2,1)S(1)}) custom-call(bf16[8,272,128]{2,1,0:T(8,128)(2,1)S(1)} %fusion.10.refs_0_, bf16[8,272,128]{2,1,0:T(8,128)(2,1)S(1)} %collective-permute-done.10.refs_1_, bf16[4,272,128]{2,1,0:T(8,128)(2,1)S(1)} %collective-permute-done.11.refs_2_, ...), custom_call_target="tpu_custom_call" | custom-call | flops 800000000 | bytes 6500000 | tf_op jit(solution)/shard_map/update/pallas_call | solution.py:110
  66.9 0.5 collective-permute-start.23
  67.4 1.5 %collective-permute-done.23 = bf16[128,2048]{1,0:T(8,128)(2,1)S(1)} collective-permute-done((bf16[128,2048]{1,0:T(8,128)(2,1)S(1)}, bf16[128,2048]{1,0:T(8,128)(2,1)S(1)}, u32[]{:S(2)}, u32[]{:S(2)}) %collective-permute-start.23) | collective-permute-done | bytes 524320 | tf_op jit(solution)/shard_map/ppermute | solution.py:152
  68.9 0.1 broadcast_select_fusion
  69.1 0.1 pad_maximum_fusion.1
  69.2 0.1 collective-permute-start.24
  69.3 2.6 %collective-permute-start.25 = (bf16[32,4096]{1,0:T(8,128)(2,1)S(1)}, bf16[32,4096]{1,0:T(8,128)(2,1)S(1)}, u32[]{:S(2)}, u32[]{:S(2)}) collective-permute-start(bf16[32,4096]{1,0:T(8,128)(2,1)S(1)} %get-tuple-element.22), channel_id=1, source_target_pairs={{0,12},{2,14},{4,0},{6,2},{8,4},{10,6},{12,8},{14,10},{1,13},{3,15... | collective-permute-start | bytes 786440 | tf_op jit(solution)/shard_map/ppermute | solution.py:140
  71.9 6.4 %collective-permute-done.24 = bf16[32,4096]{1,0:T(8,128)(2,1)S(1)} collective-permute-done((bf16[32,4096]{1,0:T(8,128)(2,1)S(1)}, bf16[32,4096]{1,0:T(8,128)(2,1)S(1)}, u32[]{:S(2)}, u32[]{:S(2)}) %collective-permute-start.24) | collective-permute-done | bytes 262176 | tf_op jit(solution)/shard_map/ppermute | solution.py:140
  78.4 2.9 %collective-permute-done.25 = bf16[32,4096]{1,0:T(8,128)(2,1)S(1)} collective-permute-done((bf16[32,4096]{1,0:T(8,128)(2,1)S(1)}, bf16[32,4096]{1,0:T(8,128)(2,1)S(1)}, u32[]{:S(2)}, u32[]{:S(2)}) %collective-permute-start.25) | collective-permute-done | bytes 262176 | tf_op jit(solution)/shard_map/ppermute | solution.py:140
  81.3 3.3 %collective-permute-done.26 = bf16[32,4096]{1,0:T(8,128)(2,1)S(1)} collective-permute-done((bf16[32,4096]{1,0:T(8,128)(2,1)S(1)}, bf16[32,4096]{1,0:T(8,128)(2,1)S(1)}, u32[]{:S(2)}, u32[]{:S(2)}) %collective-permute-start.26) | collective-permute-done | bytes 262176 | tf_op jit(solution)/shard_map/ppermute | solution.py:140
  84.6 0.7 constant_dynamic-update-slice_fusion.10
  (58 shorter events, 0.5 us)
Async XLA Ops:
  0.7 10.3 %collective-permute-start.1 = (bf16[64,128]{1,0:T(8,128)(2,1)S(1)}, bf16[64,128]{1,0:T(8,128)(2,1)S(1)}, u32[]{:S(2)}, u32[]{:S(2)}) collective-permute-start(bf16[64,128]{1,0:T(8,128)(2,1)S(1)} %pad_maximum_fusion.2), channel_id=1, source_target_pairs={{0,8},{2,10},{4,12},{6,14},{8,0},{10,2},{12,4},{14,6},{1,9},{3,11}... | collective-permute-start | bytes 49160 | tf_op jit(solution)/shard_map/ppermute | solution.py:140
  4.3 6.7 %collective-permute-start = (bf16[64,128]{1,0:T(8,128)(2,1)S(1)}, bf16[64,128]{1,0:T(8,128)(2,1)S(1)}, u32[]{:S(2)}, u32[]{:S(2)}) collective-permute-start(bf16[64,128]{1,0:T(8,128)(2,1)S(1)} %pad_maximum_fusion.2), channel_id=1, source_target_pairs={{0,4},{2,6},{4,8},{6,10},{8,12},{10,14},{12,0},{14,2},{1,5},{3,7},... | collective-permute-start | bytes 49160 | tf_op jit(solution)/shard_map/ppermute | solution.py:140
  4.6 6.4 %collective-permute-start.2 = (bf16[64,128]{1,0:T(8,128)(2,1)S(1)}, bf16[64,128]{1,0:T(8,128)(2,1)S(1)}, u32[]{:S(2)}, u32[]{:S(2)}) collective-permute-start(bf16[64,128]{1,0:T(8,128)(2,1)S(1)} %pad_maximum_fusion.2), channel_id=1, source_target_pairs={{0,12},{2,14},{4,0},{6,2},{8,4},{10,6},{12,8},{14,10},{1,13},{3,15... | collective-permute-start | bytes 49160 | tf_op jit(solution)/shard_map/ppermute | solution.py:140
  11.0 13.4 %collective-permute-start.3 = (bf16[296,128]{1,0:T(8,128)(2,1)S(1)}, bf16[296,128]{1,0:T(8,128)(2,1)S(1)}, u32[]{:S(2)}, u32[]{:S(2)}) collective-permute-start(bf16[296,128]{1,0:T(8,128)(2,1)S(1)} %constant_dynamic-update-slice_fusion), channel_id=1, source_target_pairs={{0,16},{16,32},{32,48},{48,1},{1,17},{17,33},{33,49},{49,0},{64,80... | collective-permute-start | bytes 227336 | tf_op jit(solution)/shard_map/ppermute | solution.py:148
  12.7 14.2 %collective-permute-start.4 = (bf16[296,128]{1,0:T(8,128)(2,1)S(1)}, bf16[296,128]{1,0:T(8,128)(2,1)S(1)}, u32[]{:S(2)}, u32[]{:S(2)}) collective-permute-start(bf16[296,128]{1,0:T(8,128)(2,1)S(1)} %constant_dynamic-update-slice_fusion), channel_id=1, source_target_pairs={{0,32},{16,48},{32,1},{48,17},{1,33},{17,49},{33,0},{49,16},{64,96... | collective-permute-start | bytes 227336 | tf_op jit(solution)/shard_map/ppermute | solution.py:148
  15.7 12.0 %collective-permute-start.5 = (bf16[296,128]{1,0:T(8,128)(2,1)S(1)}, bf16[296,128]{1,0:T(8,128)(2,1)S(1)}, u32[]{:S(2)}, u32[]{:S(2)}) collective-permute-start(bf16[296,128]{1,0:T(8,128)(2,1)S(1)} %constant_dynamic-update-slice_fusion), channel_id=1, source_target_pairs={{0,48},{16,1},{32,17},{48,33},{1,49},{17,0},{33,16},{49,32},{64,11... | collective-permute-start | bytes 227336 | tf_op jit(solution)/shard_map/ppermute | solution.py:148
  19.5 8.8 %collective-permute-start.6 = (bf16[296,128]{1,0:T(8,128)(2,1)S(1)}, bf16[296,128]{1,0:T(8,128)(2,1)S(1)}, u32[]{:S(2)}, u32[]{:S(2)}) collective-permute-start(bf16[296,128]{1,0:T(8,128)(2,1)S(1)} %constant_dynamic-update-slice_fusion), channel_id=1, source_target_pairs={{0,1},{16,17},{32,33},{48,49},{1,0},{17,16},{33,32},{49,48},{64,65... | collective-permute-start | bytes 227336 | tf_op jit(solution)/shard_map/ppermute | solution.py:148
  20.0 9.0 %collective-permute-start.7 = (bf16[296,128]{1,0:T(8,128)(2,1)S(1)}, bf16[296,128]{1,0:T(8,128)(2,1)S(1)}, u32[]{:S(2)}, u32[]{:S(2)}) collective-permute-start(bf16[296,128]{1,0:T(8,128)(2,1)S(1)} %constant_dynamic-update-slice_fusion), channel_id=1, source_target_pairs={{0,17},{16,33},{32,49},{48,0},{1,16},{17,32},{33,48},{49,1},{64,81... | collective-permute-start | bytes 227336 | tf_op jit(solution)/shard_map/ppermute | solution.py:148
  24.5 11.7 %collective-permute-start.8 = (bf16[296,128]{1,0:T(8,128)(2,1)S(1)}, bf16[296,128]{1,0:T(8,128)(2,1)S(1)}, u32[]{:S(2)}, u32[]{:S(2)}) collective-permute-start(bf16[296,128]{1,0:T(8,128)(2,1)S(1)} %constant_dynamic-update-slice_fusion), channel_id=1, source_target_pairs={{0,33},{16,49},{32,0},{48,16},{1,32},{17,48},{33,1},{49,17},{64,97... | collective-permute-start | bytes 227336 | tf_op jit(solution)/shard_map/ppermute | solution.py:148
  26.9 9.9 %collective-permute-start.9 = (bf16[296,128]{1,0:T(8,128)(2,1)S(1)}, bf16[296,128]{1,0:T(8,128)(2,1)S(1)}, u32[]{:S(2)}, u32[]{:S(2)}) collective-permute-start(bf16[296,128]{1,0:T(8,128)(2,1)S(1)} %constant_dynamic-update-slice_fusion), channel_id=1, source_target_pairs={{0,49},{16,0},{32,16},{48,32},{1,48},{17,1},{33,17},{49,33},{64,11... | collective-permute-start | bytes 227336 | tf_op jit(solution)/shard_map/ppermute | solution.py:148
  27.8 12.0 %collective-permute-start.19 = (bf16[32,4096]{1,0:T(8,128)(2,1)S(1)}, bf16[32,4096]{1,0:T(8,128)(2,1)S(1)}, u32[]{:S(2)}, u32[]{:S(2)}) collective-permute-start(bf16[32,4096]{1,0:T(8,128)(2,1)S(1)} %get-tuple-element.10), channel_id=1, source_target_pairs={{0,8},{2,10},{4,12},{6,14},{8,0},{10,2},{12,4},{14,6},{1,9},{3,11}... | collective-permute-start | bytes 786440 | tf_op jit(solution)/shard_map/ppermute | solution.py:140
  36.9 14.3 %collective-permute-start.10 = (bf16[8,272,128]{2,1,0:T(8,128)(2,1)S(1)}, bf16[8,272,128]{2,1,0:T(8,128)(2,1)S(1)}, u32[]{:S(2)}, u32[]{:S(2)}) collective-permute-start(bf16[8,272,128]{2,1,0:T(8,128)(2,1)S(1)} %fusion.10.refs_0_), channel_id=1, source_target_pairs={{0,64},{16,80},{32,96},{48,112},{1,65},{17,81},{33,97},{49,113},{6... | collective-permute-start | bytes 1671176 | tf_op jit(solution)/shard_map/ppermute | solution.py:144
  38.3 13.1 %collective-permute-start.12 = (bf16[8,272,128]{2,1,0:T(8,128)(2,1)S(1)}, bf16[8,272,128]{2,1,0:T(8,128)(2,1)S(1)}, u32[]{:S(2)}, u32[]{:S(2)}) collective-permute-start(bf16[8,272,128]{2,1,0:T(8,128)(2,1)S(1)} %fusion.10.refs_0_), channel_id=1, source_target_pairs={{0,192},{16,208},{32,224},{48,240},{1,193},{17,209},{33,225},{49,2... | collective-permute-start | bytes 1671176 | tf_op jit(solution)/shard_map/ppermute | solution.py:144
  39.8 7.4 %collective-permute-start.20 = (bf16[32,4096]{1,0:T(8,128)(2,1)S(1)}, bf16[32,4096]{1,0:T(8,128)(2,1)S(1)}, u32[]{:S(2)}, u32[]{:S(2)}) collective-permute-start(bf16[32,4096]{1,0:T(8,128)(2,1)S(1)} %get-tuple-element.11), channel_id=1, source_target_pairs={{0,4},{2,6},{4,8},{6,10},{8,12},{10,14},{12,0},{14,2},{1,5},{3,7},... | collective-permute-start | bytes 786440 | tf_op jit(solution)/shard_map/ppermute | solution.py:140
  47.2 9.5 %collective-permute-start.21 = (bf16[32,4096]{1,0:T(8,128)(2,1)S(1)}, bf16[32,4096]{1,0:T(8,128)(2,1)S(1)}, u32[]{:S(2)}, u32[]{:S(2)}) collective-permute-start(bf16[32,4096]{1,0:T(8,128)(2,1)S(1)} %get-tuple-element.12), channel_id=1, source_target_pairs={{0,12},{2,14},{4,0},{6,2},{8,4},{10,6},{12,8},{14,10},{1,13},{3,15... | collective-permute-start | bytes 786440 | tf_op jit(solution)/shard_map/ppermute | solution.py:140
  47.2 9.7 %collective-permute-start.14 = (bf16[8,272,128]{2,1,0:T(8,128)(2,1)S(1)}, bf16[8,272,128]{2,1,0:T(8,128)(2,1)S(1)}, u32[]{:S(2)}, u32[]{:S(2)}) collective-permute-start(bf16[8,272,128]{2,1,0:T(8,128)(2,1)S(1)} %fusion.10.refs_0_), channel_id=1, source_target_pairs={{0,2},{2,0},{4,6},{6,4},{8,10},{10,8},{12,14},{14,12},{1,3},{3,1},... | collective-permute-start | bytes 1671176 | tf_op jit(solution)/shard_map/ppermute | solution.py:152
  51.3 7.4 %collective-permute-start.11 = (bf16[4,272,128]{2,1,0:T(8,128)(2,1)S(1)}, bf16[4,272,128]{2,1,0:T(8,128)(2,1)S(1)}, u32[]{:S(2)}, u32[]{:S(2)}) collective-permute-start(bf16[4,272,128]{2,1,0:T(8,128)(2,1)S(1)} %slice.61), channel_id=1, source_target_pairs={{0,64},{16,80},{32,96},{48,112},{1,65},{17,81},{33,97},{49,113},{6... | collective-permute-start | bytes 835592 | tf_op jit(solution)/shard_map/ppermute | solution.py:144
  51.4 10.2 %collective-permute-start.13 = (bf16[4,272,128]{2,1,0:T(8,128)(2,1)S(1)}, bf16[4,272,128]{2,1,0:T(8,128)(2,1)S(1)}, u32[]{:S(2)}, u32[]{:S(2)}) collective-permute-start(bf16[4,272,128]{2,1,0:T(8,128)(2,1)S(1)} %slice.62), channel_id=1, source_target_pairs={{0,192},{16,208},{32,224},{48,240},{1,193},{17,209},{33,225},{49,2... | collective-permute-start | bytes 835592 | tf_op jit(solution)/shard_map/ppermute | solution.py:144
  54.1 9.1 %collective-permute-start.15 = (bf16[8,272,128]{2,1,0:T(8,128)(2,1)S(1)}, bf16[8,272,128]{2,1,0:T(8,128)(2,1)S(1)}, u32[]{:S(2)}, u32[]{:S(2)}) collective-permute-start(bf16[8,272,128]{2,1,0:T(8,128)(2,1)S(1)} %collective-permute-done.10.refs_1_), channel_id=1, source_target_pairs={{0,2},{2,0},{4,6},{6,4},{8,10},{10,8},{12,14},{14,12},{1,3},{3,1},... | collective-permute-start | bytes 1671176 | tf_op jit(solution)/shard_map/ppermute | solution.py:152
  56.7 6.5 %collective-permute-start.18 = (bf16[8,272,128]{2,1,0:T(8,128)(2,1)S(1)}, bf16[8,272,128]{2,1,0:T(8,128)(2,1)S(1)}, u32[]{:S(2)}, u32[]{:S(2)}) collective-permute-start(bf16[8,272,128]{2,1,0:T(8,128)(2,1)S(1)} %collective-permute-done.12.refs_4_), channel_id=1, source_target_pairs={{0,2},{2,0},{4,6},{6,4},{8,10},{10,8},{12,14},{14,12},{1,3},{3,1},... | collective-permute-start | bytes 1671176 | tf_op jit(solution)/shard_map/ppermute | solution.py:152
  56.8 6.5 %copy-start = (bf16[64,128]{1,0:T(8,128)(2,1)S(1)}, bf16[64,128]{1,0:T(8,128)(2,1)}, u32[]{:S(2)}) copy-start(bf16[64,128]{1,0:T(8,128)(2,1)} %refs_12_.1) | copy-start | bytes 49156
  57.0 6.3 %collective-permute-start.22 = (bf16[128,2048]{1,0:T(8,128)(2,1)S(1)}, bf16[128,2048]{1,0:T(8,128)(2,1)S(1)}, u32[]{:S(2)}, u32[]{:S(2)}) collective-permute-start(bf16[128,2048]{1,0:T(8,128)(2,1)S(1)} %get-tuple-element.25), channel_id=1, source_target_pairs={{0,2},{2,0},{4,6},{6,4},{8,10},{10,8},{12,14},{14,12},{1,3},{3,1},... | collective-permute-start | bytes 1572872 | tf_op jit(solution)/shard_map/ppermute | solution.py:152
  58.7 4.2 %collective-permute-start.16 = (bf16[4,272,128]{2,1,0:T(8,128)(2,1)S(1)}, bf16[4,272,128]{2,1,0:T(8,128)(2,1)S(1)}, u32[]{:S(2)}, u32[]{:S(2)}) collective-permute-start(bf16[4,272,128]{2,1,0:T(8,128)(2,1)S(1)} %collective-permute-done.11.refs_2_), channel_id=1, source_target_pairs={{0,2},{2,0},{4,6},{6,4},{8,10},{10,8},{12,14},{14,12},{1,3},{3,1},... | collective-permute-start | bytes 835592 | tf_op jit(solution)/shard_map/ppermute | solution.py:152
  61.6 1.6 %collective-permute-start.17 = (bf16[4,272,128]{2,1,0:T(8,128)(2,1)S(1)}, bf16[4,272,128]{2,1,0:T(8,128)(2,1)S(1)}, u32[]{:S(2)}, u32[]{:S(2)}) collective-permute-start(bf16[4,272,128]{2,1,0:T(8,128)(2,1)S(1)} %collective-permute-done.13.refs_3_), channel_id=1, source_target_pairs={{0,2},{2,0},{4,6},{6,4},{8,10},{10,8},{12,14},{14,12},{1,3},{3,1},... | collective-permute-start | bytes 835592 | tf_op jit(solution)/shard_map/ppermute | solution.py:152
  66.9 2.0 %collective-permute-start.23 = (bf16[128,2048]{1,0:T(8,128)(2,1)S(1)}, bf16[128,2048]{1,0:T(8,128)(2,1)S(1)}, u32[]{:S(2)}, u32[]{:S(2)}) collective-permute-start(bf16[128,2048]{1,0:T(8,128)(2,1)S(1)} %get-tuple-element.14), channel_id=1, source_target_pairs={{0,2},{2,0},{4,6},{6,4},{8,10},{10,8},{12,14},{14,12},{1,3},{3,1},... | collective-permute-start | bytes 1572872 | tf_op jit(solution)/shard_map/ppermute | solution.py:152
  69.2 9.2 %collective-permute-start.24 = (bf16[32,4096]{1,0:T(8,128)(2,1)S(1)}, bf16[32,4096]{1,0:T(8,128)(2,1)S(1)}, u32[]{:S(2)}, u32[]{:S(2)}) collective-permute-start(bf16[32,4096]{1,0:T(8,128)(2,1)S(1)} %get-tuple-element.21), channel_id=1, source_target_pairs={{0,8},{2,10},{4,12},{6,14},{8,0},{10,2},{12,4},{14,6},{1,9},{3,11}... | collective-permute-start | bytes 786440 | tf_op jit(solution)/shard_map/ppermute | solution.py:140
  69.3 12.0 %collective-permute-start.25 = (bf16[32,4096]{1,0:T(8,128)(2,1)S(1)}, bf16[32,4096]{1,0:T(8,128)(2,1)S(1)}, u32[]{:S(2)}, u32[]{:S(2)}) collective-permute-start(bf16[32,4096]{1,0:T(8,128)(2,1)S(1)} %get-tuple-element.22), channel_id=1, source_target_pairs={{0,12},{2,14},{4,0},{6,2},{8,4},{10,6},{12,8},{14,10},{1,13},{3,15... | collective-permute-start | bytes 786440 | tf_op jit(solution)/shard_map/ppermute | solution.py:140
  71.9 12.7 %collective-permute-start.26 = (bf16[32,4096]{1,0:T(8,128)(2,1)S(1)}, bf16[32,4096]{1,0:T(8,128)(2,1)S(1)}, u32[]{:S(2)}, u32[]{:S(2)}) collective-permute-start(bf16[32,4096]{1,0:T(8,128)(2,1)S(1)} %get-tuple-element.19), channel_id=1, source_target_pairs={{0,4},{2,6},{4,8},{6,10},{8,12},{10,14},{12,0},{14,2},{1,5},{3,7},... | collective-permute-start | bytes 786440 | tf_op jit(solution)/shard_map/ppermute | solution.py:140
  81.3 3.3 %copy-start.1 = (bf16[32,16384]{1,0:T(8,128)(2,1)}, bf16[32,16384]{1,0:T(8,128)(2,1)S(1)}, u32[]{:S(2)}) copy-start(bf16[32,16384]{1,0:T(8,128)(2,1)S(1)} %constant_dynamic-update-slice_fusion.11) | copy-start | bytes 3145732

commit v4 on v3

v4 whole, which is shorter than its diff:
```python
import jax
import jax.numpy as jnp
from jax import lax
from jax.experimental import pallas as pl
from jax.experimental.pallas import tpu as pltpu
from jax.sharding import PartitionSpec as P

M = 256
EMPTY = 512
X, GROUPS = 4, 32
LIST_ROWS = 8
DN_NT = (((1,), (1,)), ((), ()))
DN_TN = (((0,), (0,)), ((), ()))


def prepare_kernel(anom_hbm, innov_hbm, seg_hbm, prof_hbm, sent_ref, data, lists, sems):
    sources = (anom_hbm, innov_hbm, seg_hbm, prof_hbm)
    targets = (data.at[0], data.at[1], lists.at[0], lists.at[1])
    loads = [pltpu.make_async_copy(src, dst, sems.at[i]) for i, (src, dst) in enumerate(zip(sources, targets))]
    for load in loads:
        load.start()
    me_cell, me_dp, me_mem = (lax.axis_index(n) for n in ("cell", "dp", "mem"))
    _, mem_dev, data_dev = data.shape
    per_group = lists.shape[1]
    per_block = 2 * per_group
    own_blocks = 128 // per_block

    lane_in = lax.broadcasted_iota(jnp.int32, (128, 128), 0)
    lane_out = lax.broadcasted_iota(jnp.int32, (128, 128), 1)
    select = lane_in == me_mem * own_blocks + lax.rem(lane_out, own_blocks)
    select = jnp.where(select, 1.0, 0.0).astype(jnp.bfloat16)
    for load in loads[2:]:
        load.wait()
    ids = lists[0]
    ids = jnp.where(ids >= 0, ids - (me_cell * 2 + me_dp) * data_dev, EMPTY)
    both = jnp.concatenate([ids, lists[1]], axis=0).astype(jnp.float32)
    tiles = [both[:, g * 128 : (g + 1) * 128] for g in range(GROUPS)]
    spread = jnp.dot(jnp.concatenate(tiles, axis=0).astype(jnp.bfloat16), select, preferred_element_type=jnp.float32)
    shape = (GROUPS, per_block, 128)
    kept = lax.broadcasted_iota(jnp.int32, shape, 1) == lax.div(lax.broadcasted_iota(jnp.int32, shape, 2), own_blocks)
    packed = jnp.sum(jnp.where(kept, spread.reshape(shape), 0.0), axis=1)
    for load in loads[:2]:
        load.wait()
    block = jnp.concatenate([data[0], data[1]], axis=0)
    filler = jnp.zeros((LIST_ROWS - 1, 128), jnp.float32)
    for g in range(GROUPS):
        rows = jnp.concatenate([packed[g : g + 1], filler], axis=0).astype(jnp.bfloat16)
        sent_ref[g] = jnp.concatenate([block, rows], axis=0)


def prepare(anom, innov, seg, prof):
    mem_dev, data_dev = anom.shape
    return pl.pallas_call(
        prepare_kernel,
        out_shape=jax.ShapeDtypeStruct((GROUPS, 2 * mem_dev + LIST_ROWS, data_dev), jnp.bfloat16),
        in_specs=[pl.BlockSpec(memory_space=pl.ANY)] * 4,
        out_specs=pl.BlockSpec(memory_space=pltpu.VMEM),
        scratch_shapes=[
            pltpu.VMEM((2,) + anom.shape, jnp.bfloat16),
            pltpu.VMEM((2,) + seg.shape, jnp.int32),
            pltpu.SemaphoreType.DMA((4,)),
        ],
        compiler_params=pltpu.CompilerParams(vmem_limit_bytes=60 * 1024 * 1024),
        cost_estimate=pl.CostEstimate(flops=10_000_000, bytes_accessed=400_000, transcendentals=0),
        name="prepare",
    )(anom, innov, seg, prof)


def update_kernel(*refs):
    n_side = X + 1
    n_data = 2 * n_side
    data_hbm, (near_hbm, far_hbm, lists_ref, table_ref) = refs[:n_data], refs[n_data : n_data + 4]
    out_near, out_far, data, state, cols, weights, sems, state_sems = refs[n_data + 4 :]
    mem_dev = data.shape[3] // 2
    data_dev = data.shape[4]
    half = X * mem_dev
    n_block = near_hbm.shape[1] // 128

    loads = {}
    for s in range(n_side):
        for side in range(2):
            if s < 2:
                dst = data.at[side, s]
            elif s < 4:
                dst = data.at[side, 2, pl.ds((s - 2) * (GROUPS // 2), GROUPS // 2)]
            else:
                dst = data.at[side, 3]
            loads[side, s] = pltpu.make_async_copy(data_hbm[side * n_side + s], dst, sems.at[side, s])
            loads[side, s].start()
    state_loads = [pltpu.make_async_copy(src, state.at[i], state_sems.at[i]) for i, src in enumerate((near_hbm, far_hbm))]
    for load in state_loads:
        load.start()

    row = lax.broadcasted_iota(jnp.int32, (128, 128), 0)
    lane = lax.broadcasted_iota(jnp.int32, (128, 128), 1)
    order = jnp.where(lane == lax.rem(row, 8) * n_block + lax.div(row, 8), 1.0, 0.0).astype(jnp.bfloat16)
    lists = jnp.concatenate([lists_ref[...], jnp.zeros((128 - GROUPS, 128), jnp.bfloat16)], axis=0)
    lists = lax.dot_general(order, lists, DN_NT, preferred_element_type=jnp.float32)
    later = pltpu.roll(lists, 127, 1)
    is_first = lax.rem(lax.broadcasted_iota(jnp.int32, (128, 128), 0), 8) < 4
    ids = jnp.where(is_first, lists, pltpu.roll(later, 4, 0) + data_dev)
    prof_ids = jnp.where(is_first, pltpu.roll(lists, 124, 0), later)

    table = table_ref[...]
    lanes = lax.broadcasted_iota(jnp.int32, (128, 2 * data_dev), 1).astype(jnp.float32)
    prof_lanes = lax.broadcasted_iota(jnp.int32, (128, table.shape[0]), 1).astype(jnp.float32)
    for load in loads.values():
        load.wait()
    for pair in range(GROUPS // 2):
        column = slice(2 * pair, 2 * pair + 1)
        place = slice(pair * 8, (pair + 1) * 8)
        chooser = jnp.where(prof_lanes == prof_ids[:, column], 1.0, 0.0).astype(jnp.bfloat16)
        weight = jnp.dot(chooser, table, preferred_element_type=jnp.float32)
        weights[:, place] = weight.reshape(n_block, 8, 128)
        picker = jnp.where(lanes == ids[:, column], 1.0, 0.0).astype(jnp.bfloat16)
        for side in range(2):
            values = jnp.concatenate(
                [
                    jnp.concatenate(
                        [
                            data[side, s, 2 * pair + g, a * mem_dev : (a + 1) * mem_dev]
                            for a in range(2)
                            for s in range(X)
                        ],
                        axis=0,
                    )
                    for g in range(2)
                ],
                axis=1,
            )
            picked = lax.dot_general(picker, values, DN_NT, preferred_element_type=jnp.float32)
            picked = picked.reshape(n_block, 8, 2 * half)
            for a in range(2):
                cols[a, :, place, side * half : (side + 1) * half] = picked[:, :, a * half : (a + 1) * half]

    for load in state_loads:
        load.wait()
    for b in range(n_block):
        spot = pl.ds(b * 128, 128)
        own = jnp.concatenate([state[0, :, spot], state[1, :, spot]], axis=0)
        anom = cols[0, b].astype(jnp.bfloat16)
        innov = cols[1, b].astype(jnp.bfloat16)
        inner = jnp.dot(anom, own, preferred_element_type=jnp.float32)
        coef = (weights[b] * inner / (M - 1)).astype(jnp.bfloat16)
        corr = lax.dot_general(innov, coef, DN_TN, preferred_element_type=jnp.float32)
        new = (own.astype(jnp.float32) + corr).astype(jnp.bfloat16)
        out_near[:, spot] = new[:half]
        out_far[:, spot] = new[half:]


def run_update(data, near, far, lists, table):
    half, width = near.shape
    n_block = width // 128
    n_slot = GROUPS * 4
    any_space = pl.BlockSpec(memory_space=pl.ANY)
    whole = pl.BlockSpec(memory_space=pltpu.VMEM)
    return pl.pallas_call(
        update_kernel,
        out_shape=[jax.ShapeDtypeStruct(near.shape, jnp.bfloat16)] * 2,
        in_specs=[any_space] * (len(data) + 2) + [whole] * 2,
        out_specs=[whole] * 2,
        scratch_shapes=[
            pltpu.VMEM((2, X) + data[0].shape, jnp.bfloat16),
            pltpu.VMEM((2,) + near.shape, jnp.bfloat16),
            pltpu.VMEM((2, n_block, n_slot, 2 * half), jnp.float32),
            pltpu.VMEM((n_block, n_slot, 128), jnp.float32),
            pltpu.SemaphoreType.DMA((2, X + 1)),
            pltpu.SemaphoreType.DMA((2,)),
        ],
        compiler_params=pltpu.CompilerParams(vmem_limit_bytes=24 * 1024 * 1024),
        cost_estimate=pl.CostEstimate(flops=800_000_000, bytes_accessed=6_500_000, transcendentals=0),
        name="update",
    )(*data, near, far, lists, table)


X_SHIFT = [[(x * 2 + c, ((x + s) % X) * 2 + c) for x in range(X) for c in range(2)] for s in range(X)]
CORE_SWAP = [(i, i ^ 1) for i in range(2 * X)]


def to_x(piece, s):
    return lax.ppermute(piece, "mem", X_SHIFT[s % X])


def swap(piece):
    return lax.ppermute(piece, "mem", CORE_SWAP)


def local(ensemble, data_anom, weighted_innov, profiles, seg_data, seg_profile):
    me_dp, me_mem = lax.axis_index("dp"), lax.axis_index("mem")
    me_x, me_core = me_mem // 2, me_mem % 2
    mem_dev, cells_dev = ensemble.shape
    half_cells = cells_dev // 2
    x_cells = half_cells // X
    own_cells = x_cells // 2

    sent = prepare(data_anom, weighted_innov, seg_data, seg_profile)
    got = lax.all_to_all(sent, ("cell", "dp"), 0, 0, tiled=True)

    def state_for(s):
        x_to = (me_x + s) % X
        return lax.dynamic_slice_in_dim(ensemble, me_dp * half_cells + x_to * x_cells, x_cells, 1)

    pieces = [state_for(0)] + [None] * 3
    for s in (2, 1, 3):
        pieces[s] = to_x(state_for(s), s)
    state = jnp.concatenate(pieces, axis=0)
    near = lax.dynamic_slice_in_dim(state, me_core * own_cells, own_cells, 1)
    far = swap(lax.dynamic_slice_in_dim(state, (1 - me_core) * own_cells, own_cells, 1))

    data_rows = 2 * mem_dev
    own, lists = got[:, :data_rows], got[:, data_rows]
    up, down = to_x(own, 1), to_x(own, -1)
    up2, down2 = to_x(up[: GROUPS // 2], 1), to_x(down[GROUPS // 2 :], -1)
    data_near = [own, up, up2, down2, down]
    data_far = [swap(d) for d in data_near]

    new_near, new_far = run_update(data_near + data_far, near, far, lists, profiles)

    back_far = swap(new_far)
    first = me_core == 0
    new = jnp.concatenate([jnp.where(first, new_near, back_far), jnp.where(first, back_far, new_near)], axis=1)
    out = jnp.zeros((mem_dev, half_cells), jnp.bfloat16)
    for s in (0, 2, 1, 3):
        piece = new[s * mem_dev : (s + 1) * mem_dev]
        if s:
            piece = to_x(piece, -s)
        out = lax.dynamic_update_slice_in_dim(out, piece, ((me_x + s) % X) * x_cells, 1)
    return out


def solution(mesh):
    placed = (
        P("mem", "cell"),
        P("mem", ("cell", "dp")),
        P("mem", ("cell", "dp")),
        P(),
        P(("cell", "dp"), None),
        P(("cell", "dp"), None),
    )
    return jax.shard_map(
        local, mesh=mesh, in_specs=placed, out_specs=P("mem", ("cell", "dp")), check_vma=False
    )
```

time: 85.9 us -> 78.5 us (0.914)
  waiting for transfers between devices: 34.7 us -> 29.5 us
  other arithmetic: 2.03 us -> 0.25 us
  Pallas kernels: 3.67 us -> 5.26 us
  local copies, waits for them, and re-layouts: 4.05 us -> 2.92 us
    ppermute x11 -> x0, starting transfers between devices: 22.4 us -> none  [the longest x7 16.7 us: to_z(): return lax.ppermute(piece, ('cell', 'dp'), Z_SHIFT[s % Z])]
    all_to_all x0 -> x1, starting transfers between devices: none -> 12 us  [local(): got = lax.all_to_all(sent, ('cell', 'dp'), 0, 0, tiled=True)]
    ppermute x11 -> x0, waiting for transfers between devices: 11.5 us -> none  [the longest x7 8.85 us: to_z(): return lax.ppermute(piece, ('cell', 'dp'), Z_SHIFT[s % Z])]
    ppermute x9 -> x10, waiting for transfers between devices: 20.1 us -> 26.1 us  [to_x(): return lax.ppermute(piece, 'mem', X_SHIFT[s % X])]
    ppermute x7, starting transfers between devices: 9.15 us -> 14.3 us  [swap(): return lax.ppermute(piece, 'mem', CORE_SWAP)]
    ppermute x9 -> x10, starting transfers between devices: 9.04 us -> 13.8 us  [to_x(): return lax.ppermute(piece, 'mem', X_SHIFT[s % X])]
    pallas_call x0 -> x1, Pallas kernels: none -> 1.99 us  [prepare(): pl.pallas_call(prepare_kernel, out_shape=jax.ShapeDtypeStruct((GROUPS, 2...]
    unnamed x7 -> x0, other arithmetic: 0.94 us -> none
  transfers between devices with their start and end apart: 27 -> 18, of which waited for: 13 -> 11; matrix products, arithmetic and copies ran while one was open for 5% -> 2% of each run, Pallas kernels for 0% -> 0%
where the time goes in v4:
time: 78.5 us; the launch traced here: 78.3 us
  starting transfers between devices  40.1 us (51%)
  waiting for transfers between devices  29.5 us (38%)
  Pallas kernels  5.26 us (7%)
  local copies, waits for them, and re-layouts  2.92 us (4%)
    ppermute x10, waiting for transfers between devices, to_x(): return lax.ppermute(piece, 'mem', X_SHIFT[s % X])  26.1 us
    ppermute x7, starting transfers between devices, swap(): return lax.ppermute(piece, 'mem', CORE_SWAP)  14.3 us
    ppermute x10, starting transfers between devices, to_x(): return lax.ppermute(piece, 'mem', X_SHIFT[s % X])  13.8 us
    all_to_all x1, starting transfers between devices, local(): got = lax.all_to_all(sent, ('cell', 'dp'), 0, 0, tiled=True)  12 us
    pallas_call x1, Pallas kernels, run_update(): pl.pallas_call(update_kernel, out_shape=[jax.ShapeDtypeStruct(near.shape,...  3.27 us
    ppermute x7, waiting for transfers between devices, swap(): return lax.ppermute(piece, 'mem', CORE_SWAP)  2.73 us
    pallas_call x1, Pallas kernels, prepare(): pl.pallas_call(prepare_kernel, out_shape=jax.ShapeDtypeStruct((GROUPS, 2...  1.99 us
  transfers between devices with their start and end apart: 18, of which 11 were waited for; matrix products, arithmetic and copies ran while one was open for 2% of the time, Pallas kernels for 0%

profile of v4, /device:TPU:1, one launch (start us, length us, event | category | flops | bytes accessed | tf_op | source)
XLA Modules:
  0.0 78.3 jit_solution(10279161184865036347)
XLA Ops:
  0.0 2.0 %prepare.1 = bf16[32,72,128]{2,1,0:T(8,128)(2,1)} custom-call(bf16[32,128]{1,0:T(8,128)(2,1)} %anom_hbm.1, bf16[32,128]{1,0:T(8,128)(2,1)} %innov_hbm.1, s32[4,4096]{1,0:T(4,128)} %seg_hbm.1, s32[4,4096]{1,0:T(4,128)} %prof_hbm.1), custom_call_target="tpu_custom_call" | custom-call | flops 10000000 | bytes 400000 | tf_op jit(solution)/shard_map/prepare/pallas_call | solution.py:53
  2.0 12.0 %all-to-all-start = ((bf16[32,72,128]{2,1,0:T(8,128)(2,1)}), bf16[32,72,128]{2,1,0:T(8,128)(2,1)S(1)}, u32[]{:S(2)}, u32[]{:S(2)}) async-start(bf16[32,72,128]{2,1,0:T(8,128)(2,1)} %prepare.1), calls=%async_computation | async-start | bytes 1179648 | tf_op jit(solution)/shard_map/all_to_all | solution.py:197
  14.2 1.3 %constant_dynamic-slice_fusion.5 = (bf16[32,4096]{1,0:T(8,128)(2,1)S(1)}, bf16[32,4096]{1,0:T(8,128)(2,1)S(1)}, bf16[32,4096]{1,0:T(8,128)(2,1)S(1)}, bf16[32,4096]{1,0:T(8,128)(2,1)S(1)}) fusion(bf16[32,32768]{1,0:T(8,128)(2,1)} %param.6, s32[]{:T(128)S(6)} %select_n.81, s32[]{:T(128)S(6)} %select_n.83, s32[]{:T(128)S(6)} %select_n.87, s32[]{:T(128)S(6)} %select_n.85), kind=kLoop, calls=%fused_computation.23 | loop fusion | bytes 2097168 | tf_op jit(solution)/shard_map/dynamic_slice | solution.py:201
  15.4 2.8 %collective-permute-start.10 = (bf16[32,4096]{1,0:T(8,128)(2,1)S(1)}, bf16[32,4096]{1,0:T(8,128)(2,1)S(1)}, u32[]{:S(2)}, u32[]{:S(2)}) collective-permute-start(bf16[32,4096]{1,0:T(8,128)(2,1)S(1)} %get-tuple-element.12), channel_id=1, source_target_pairs={{0,8},{2,10},{4,12},{6,14},{8,0},{10,2},{12,4},{14,6},{1,9},{3,11}... | collective-permute-start | bytes 786440 | tf_op jit(solution)/shard_map/ppermute | solution.py:181
  18.3 0.9 %collective-permute-start.11 = (bf16[32,4096]{1,0:T(8,128)(2,1)S(1)}, bf16[32,4096]{1,0:T(8,128)(2,1)S(1)}, u32[]{:S(2)}, u32[]{:S(2)}) collective-permute-start(bf16[32,4096]{1,0:T(8,128)(2,1)S(1)} %get-tuple-element.11), channel_id=1, source_target_pairs={{0,12},{2,14},{4,0},{6,2},{8,4},{10,6},{12,8},{14,10},{1,13},{3,15... | collective-permute-start | bytes 786440 | tf_op jit(solution)/shard_map/ppermute | solution.py:181
  19.1 0.6 collective-permute-start.9
  19.7 4.2 %collective-permute-done.10 = bf16[32,4096]{1,0:T(8,128)(2,1)S(1)} collective-permute-done((bf16[32,4096]{1,0:T(8,128)(2,1)S(1)}, bf16[32,4096]{1,0:T(8,128)(2,1)S(1)}, u32[]{:S(2)}, u32[]{:S(2)}) %collective-permute-start.10) | collective-permute-done | bytes 262176 | tf_op jit(solution)/shard_map/ppermute | solution.py:181
  23.9 6.1 %collective-permute-done.11 = bf16[32,4096]{1,0:T(8,128)(2,1)S(1)} collective-permute-done((bf16[32,4096]{1,0:T(8,128)(2,1)S(1)}, bf16[32,4096]{1,0:T(8,128)(2,1)S(1)}, u32[]{:S(2)}, u32[]{:S(2)}) %collective-permute-start.11) | collective-permute-done | bytes 262176 | tf_op jit(solution)/shard_map/ppermute | solution.py:181
  29.9 0.4 collective-permute-done.9
  30.3 0.1 pad_maximum_fusion
  30.4 0.0 copy-start
  30.4 0.6 all-to-all-done
  31.1 0.1 slice.32.refs_0_
  31.1 1.3 %collective-permute-start = (bf16[32,64,128]{2,1,0:T(8,128)(2,1)S(1)}, bf16[32,64,128]{2,1,0:T(8,128)(2,1)S(1)}, u32[]{:S(2)}, u32[]{:S(2)}) collective-permute-start(bf16[32,64,128]{2,1,0:T(8,128)(2,1)S(1)} %slice.32.refs_0_), channel_id=1, source_target_pairs={{0,4},{2,6},{4,8},{6,10},{8,12},{10,14},{12,0},{14,2},{1,5},{3,7},... | collective-permute-start | bytes 1572872 | tf_op jit(solution)/shard_map/ppermute | solution.py:181
  32.4 1.5 %collective-permute-start.2 = (bf16[32,64,128]{2,1,0:T(8,128)(2,1)S(1)}, bf16[32,64,128]{2,1,0:T(8,128)(2,1)S(1)}, u32[]{:S(2)}, u32[]{:S(2)}) collective-permute-start(bf16[32,64,128]{2,1,0:T(8,128)(2,1)S(1)} %slice.32.refs_0_), channel_id=1, source_target_pairs={{0,12},{2,14},{4,0},{6,2},{8,4},{10,6},{12,8},{14,10},{1,13},{3,15... | collective-permute-start | bytes 1572872 | tf_op jit(solution)/shard_map/ppermute | solution.py:181
  33.9 0.1 constant_dynamic-slice_fusion
  34.0 4.2 %collective-permute-start.12 = (bf16[128,2048]{1,0:T(8,128)(2,1)S(1)}, bf16[128,2048]{1,0:T(8,128)(2,1)S(1)}, u32[]{:S(2)}, u32[]{:S(2)}) collective-permute-start(bf16[128,2048]{1,0:T(8,128)(2,1)S(1)} %get-tuple-element.19), channel_id=1, source_target_pairs={{0,2},{2,0},{4,6},{6,4},{8,10},{10,8},{12,14},{14,12},{1,3},{3,1},... | collective-permute-start | bytes 1572872 | tf_op jit(solution)/shard_map/ppermute | solution.py:185
  38.2 0.1 collective-permute-start.4
  38.3 4.1 %collective-permute-done.refs_1_ = bf16[32,64,128]{2,1,0:T(8,128)(2,1)S(1)} collective-permute-done((bf16[32,64,128]{2,1,0:T(8,128)(2,1)S(1)}, bf16[32,64,128]{2,1,0:T(8,128)(2,1)S(1)}, u32[]{:S(2)}, u32[]{:S(2)}) %collective-permute-start) | collective-permute-done | bytes 524320 | tf_op jit(solution)/shard_map/ppermute | solution.py:181
  42.4 0.1 collective-permute-start.1
  42.4 0.0 collective-permute-done.2.refs_4_
  42.5 2.7 %collective-permute-start.3 = (bf16[16,64,128]{2,1,0:T(8,128)(2,1)S(1)}, bf16[16,64,128]{2,1,0:T(8,128)(2,1)S(1)}, u32[]{:S(2)}, u32[]{:S(2)}) collective-permute-start(bf16[16,64,128]{2,1,0:T(8,128)(2,1)S(1)} %slice.34), channel_id=1, source_target_pairs={{0,12},{2,14},{4,0},{6,2},{8,4},{10,6},{12,8},{14,10},{1,13},{3,15... | collective-permute-start | bytes 786440 | tf_op jit(solution)/shard_map/ppermute | solution.py:181
  45.2 5.0 %collective-permute-start.5 = (bf16[32,64,128]{2,1,0:T(8,128)(2,1)S(1)}, bf16[32,64,128]{2,1,0:T(8,128)(2,1)S(1)}, u32[]{:S(2)}, u32[]{:S(2)}) collective-permute-start(bf16[32,64,128]{2,1,0:T(8,128)(2,1)S(1)} %collective-permute-done.refs_1_), channel_id=1, source_target_pairs={{0,2},{2,0},{4,6},{6,4},{8,10},{10,8},{12,14},{14,12},{1,3},{3,1},... | collective-permute-start | bytes 1572872 | tf_op jit(solution)/shard_map/ppermute | solution.py:185
  50.2 0.0 collective-permute-done.12.refs_11_
  50.2 0.0 collective-permute-start.8
  50.2 0.0 collective-permute-done.1.refs_2_
  50.2 4.2 %collective-permute-start.6 = (bf16[16,64,128]{2,1,0:T(8,128)(2,1)S(1)}, bf16[16,64,128]{2,1,0:T(8,128)(2,1)S(1)}, u32[]{:S(2)}, u32[]{:S(2)}) collective-permute-start(bf16[16,64,128]{2,1,0:T(8,128)(2,1)S(1)} %collective-permute-done.1.refs_2_), channel_id=1, source_target_pairs={{0,2},{2,0},{4,6},{6,4},{8,10},{10,8},{12,14},{14,12},{1,3},{3,1},... | collective-permute-start | bytes 786440 | tf_op jit(solution)/shard_map/ppermute | solution.py:185
  54.5 0.0 collective-permute-done.3.refs_3_
  54.5 0.3 collective-permute-start.7
  54.8 0.8 %collective-permute-done.6.refs_7_ = bf16[16,64,128]{2,1,0:T(8,128)(2,1)S(1)} collective-permute-done((bf16[16,64,128]{2,1,0:T(8,128)(2,1)S(1)}, bf16[16,64,128]{2,1,0:T(8,128)(2,1)S(1)}, u32[]{:S(2)}, u32[]{:S(2)}) %collective-permute-start.6) | collective-permute-done | bytes 262176 | tf_op jit(solution)/shard_map/ppermute | solution.py:185
  55.6 0.4 collective-permute-done.7.refs_8_
  56.0 0.0 collective-permute-done.5.refs_6_
  56.0 0.0 collective-permute-done.8.refs_9_
  56.0 3.3 %update.1 = (bf16[128,2048]{1,0:T(8,128)(2,1)S(1)}, bf16[128,2048]{1,0:T(8,128)(2,1)S(1)}) custom-call(bf16[32,64,128]{2,1,0:T(8,128)(2,1)S(1)} %slice.32.refs_0_, bf16[32,64,128]{2,1,0:T(8,128)(2,1)S(1)} %collective-permute-done.refs_1_, bf16[16,64,128]{2,1,0:T(8,128)(2,1)S(1)} %collective-permute-done.1.refs_2_, ...), custom_call_target="tpu_custom_call" | custom-call | flops 800000000 | bytes 6500000 | tf_op jit(solution)/shard_map/update/pallas_call | solution.py:157
  59.3 0.5 collective-permute-start.13
  59.7 1.5 %collective-permute-done.13 = bf16[128,2048]{1,0:T(8,128)(2,1)S(1)} collective-permute-done((bf16[128,2048]{1,0:T(8,128)(2,1)S(1)}, bf16[128,2048]{1,0:T(8,128)(2,1)S(1)}, u32[]{:S(2)}, u32[]{:S(2)}) %collective-permute-start.13) | collective-permute-done | bytes 524320 | tf_op jit(solution)/shard_map/ppermute | solution.py:185
  61.3 0.1 broadcast_select_fusion
  61.4 0.1 broadcast_in_dim.3
  61.4 0.1 pad_maximum_fusion.1
  61.5 2.5 %collective-permute-start.14 = (bf16[32,4096]{1,0:T(8,128)(2,1)S(1)}, bf16[32,4096]{1,0:T(8,128)(2,1)S(1)}, u32[]{:S(2)}, u32[]{:S(2)}) collective-permute-start(bf16[32,4096]{1,0:T(8,128)(2,1)S(1)} %get-tuple-element.15), channel_id=1, source_target_pairs={{0,8},{2,10},{4,12},{6,14},{8,0},{10,2},{12,4},{14,6},{1,9},{3,11}... | collective-permute-start | bytes 786440 | tf_op jit(solution)/shard_map/ppermute | solution.py:181
  64.0 1.1 %collective-permute-start.15 = (bf16[32,4096]{1,0:T(8,128)(2,1)S(1)}, bf16[32,4096]{1,0:T(8,128)(2,1)S(1)}, u32[]{:S(2)}, u32[]{:S(2)}) collective-permute-start(bf16[32,4096]{1,0:T(8,128)(2,1)S(1)} %get-tuple-element.16), channel_id=1, source_target_pairs={{0,12},{2,14},{4,0},{6,2},{8,4},{10,6},{12,8},{14,10},{1,13},{3,15... | collective-permute-start | bytes 786440 | tf_op jit(solution)/shard_map/ppermute | solution.py:181
  65.2 0.3 collective-permute-start.16
  65.5 5.2 %collective-permute-done.14 = bf16[32,4096]{1,0:T(8,128)(2,1)S(1)} collective-permute-done((bf16[32,4096]{1,0:T(8,128)(2,1)S(1)}, bf16[32,4096]{1,0:T(8,128)(2,1)S(1)}, u32[]{:S(2)}, u32[]{:S(2)}) %collective-permute-start.14) | collective-permute-done | bytes 262176 | tf_op jit(solution)/shard_map/ppermute | solution.py:181
  70.7 5.9 %collective-permute-done.15 = bf16[32,4096]{1,0:T(8,128)(2,1)S(1)} collective-permute-done((bf16[32,4096]{1,0:T(8,128)(2,1)S(1)}, bf16[32,4096]{1,0:T(8,128)(2,1)S(1)}, u32[]{:S(2)}, u32[]{:S(2)}) %collective-permute-start.15) | collective-permute-done | bytes 262176 | tf_op jit(solution)/shard_map/ppermute | solution.py:181
  76.6 0.0 copy-start.1
  76.6 0.3 collective-permute-done.16
  77.0 0.6 copy-done.1
  77.6 0.7 constant_dynamic-update-slice_fusion
  (8 shorter events, 0.1 us)
Async XLA Ops:
  2.0 29.1 %all-to-all-start = ((bf16[32,72,128]{2,1,0:T(8,128)(2,1)}), bf16[32,72,128]{2,1,0:T(8,128)(2,1)S(1)}, u32[]{:S(2)}, u32[]{:S(2)}) async-start(bf16[32,72,128]{2,1,0:T(8,128)(2,1)} %prepare.1), calls=%async_computation | async-start | bytes 1179648 | tf_op jit(solution)/shard_map/all_to_all | solution.py:197
  15.4 8.4 %collective-permute-start.10 = (bf16[32,4096]{1,0:T(8,128)(2,1)S(1)}, bf16[32,4096]{1,0:T(8,128)(2,1)S(1)}, u32[]{:S(2)}, u32[]{:S(2)}) collective-permute-start(bf16[32,4096]{1,0:T(8,128)(2,1)S(1)} %get-tuple-element.12), channel_id=1, source_target_pairs={{0,8},{2,10},{4,12},{6,14},{8,0},{10,2},{12,4},{14,6},{1,9},{3,11}... | collective-permute-start | bytes 786440 | tf_op jit(solution)/shard_map/ppermute | solution.py:181
  18.3 11.7 %collective-permute-start.11 = (bf16[32,4096]{1,0:T(8,128)(2,1)S(1)}, bf16[32,4096]{1,0:T(8,128)(2,1)S(1)}, u32[]{:S(2)}, u32[]{:S(2)}) collective-permute-start(bf16[32,4096]{1,0:T(8,128)(2,1)S(1)} %get-tuple-element.11), channel_id=1, source_target_pairs={{0,12},{2,14},{4,0},{6,2},{8,4},{10,6},{12,8},{14,10},{1,13},{3,15... | collective-permute-start | bytes 786440 | tf_op jit(solution)/shard_map/ppermute | solution.py:181
  19.1 11.2 %collective-permute-start.9 = (bf16[32,4096]{1,0:T(8,128)(2,1)S(1)}, bf16[32,4096]{1,0:T(8,128)(2,1)S(1)}, u32[]{:S(2)}, u32[]{:S(2)}) collective-permute-start(bf16[32,4096]{1,0:T(8,128)(2,1)S(1)} %get-tuple-element.10), channel_id=1, source_target_pairs={{0,4},{2,6},{4,8},{6,10},{8,12},{10,14},{12,0},{14,2},{1,5},{3,7},... | collective-permute-start | bytes 786440 | tf_op jit(solution)/shard_map/ppermute | solution.py:181
  30.4 25.6 %copy-start = (bf16[64,128]{1,0:T(8,128)(2,1)S(1)}, bf16[64,128]{1,0:T(8,128)(2,1)}, u32[]{:S(2)}) copy-start(bf16[64,128]{1,0:T(8,128)(2,1)} %refs_13_.1) | copy-start | bytes 49156
  31.1 11.2 %collective-permute-start = (bf16[32,64,128]{2,1,0:T(8,128)(2,1)S(1)}, bf16[32,64,128]{2,1,0:T(8,128)(2,1)S(1)}, u32[]{:S(2)}, u32[]{:S(2)}) collective-permute-start(bf16[32,64,128]{2,1,0:T(8,128)(2,1)S(1)} %slice.32.refs_0_), channel_id=1, source_target_pairs={{0,4},{2,6},{4,8},{6,10},{8,12},{10,14},{12,0},{14,2},{1,5},{3,7},... | collective-permute-start | bytes 1572872 | tf_op jit(solution)/shard_map/ppermute | solution.py:181
  32.4 10.0 %collective-permute-start.2 = (bf16[32,64,128]{2,1,0:T(8,128)(2,1)S(1)}, bf16[32,64,128]{2,1,0:T(8,128)(2,1)S(1)}, u32[]{:S(2)}, u32[]{:S(2)}) collective-permute-start(bf16[32,64,128]{2,1,0:T(8,128)(2,1)S(1)} %slice.32.refs_0_), channel_id=1, source_target_pairs={{0,12},{2,14},{4,0},{6,2},{8,4},{10,6},{12,8},{14,10},{1,13},{3,15... | collective-permute-start | bytes 1572872 | tf_op jit(solution)/shard_map/ppermute | solution.py:181
  34.0 16.2 %collective-permute-start.12 = (bf16[128,2048]{1,0:T(8,128)(2,1)S(1)}, bf16[128,2048]{1,0:T(8,128)(2,1)S(1)}, u32[]{:S(2)}, u32[]{:S(2)}) collective-permute-start(bf16[128,2048]{1,0:T(8,128)(2,1)S(1)} %get-tuple-element.19), channel_id=1, source_target_pairs={{0,2},{2,0},{4,6},{6,4},{8,10},{10,8},{12,14},{14,12},{1,3},{3,1},... | collective-permute-start | bytes 1572872 | tf_op jit(solution)/shard_map/ppermute | solution.py:185
  38.2 16.7 %collective-permute-start.4 = (bf16[32,64,128]{2,1,0:T(8,128)(2,1)S(1)}, bf16[32,64,128]{2,1,0:T(8,128)(2,1)S(1)}, u32[]{:S(2)}, u32[]{:S(2)}) collective-permute-start(bf16[32,64,128]{2,1,0:T(8,128)(2,1)S(1)} %slice.32.refs_0_), channel_id=1, source_target_pairs={{0,2},{2,0},{4,6},{6,4},{8,10},{10,8},{12,14},{14,12},{1,3},{3,1},... | collective-permute-start | bytes 1572872 | tf_op jit(solution)/shard_map/ppermute | solution.py:185
  42.4 7.9 %collective-permute-start.1 = (bf16[16,64,128]{2,1,0:T(8,128)(2,1)S(1)}, bf16[16,64,128]{2,1,0:T(8,128)(2,1)S(1)}, u32[]{:S(2)}, u32[]{:S(2)}) collective-permute-start(bf16[16,64,128]{2,1,0:T(8,128)(2,1)S(1)} %slice.33), channel_id=1, source_target_pairs={{0,4},{2,6},{4,8},{6,10},{8,12},{10,14},{12,0},{14,2},{1,5},{3,7},... | collective-permute-start | bytes 786440 | tf_op jit(solution)/shard_map/ppermute | solution.py:181
  42.5 12.0 %collective-permute-start.3 = (bf16[16,64,128]{2,1,0:T(8,128)(2,1)S(1)}, bf16[16,64,128]{2,1,0:T(8,128)(2,1)S(1)}, u32[]{:S(2)}, u32[]{:S(2)}) collective-permute-start(bf16[16,64,128]{2,1,0:T(8,128)(2,1)S(1)} %slice.34), channel_id=1, source_target_pairs={{0,12},{2,14},{4,0},{6,2},{8,4},{10,6},{12,8},{14,10},{1,13},{3,15... | collective-permute-start | bytes 786440 | tf_op jit(solution)/shard_map/ppermute | solution.py:181
  45.2 10.8 %collective-permute-start.5 = (bf16[32,64,128]{2,1,0:T(8,128)(2,1)S(1)}, bf16[32,64,128]{2,1,0:T(8,128)(2,1)S(1)}, u32[]{:S(2)}, u32[]{:S(2)}) collective-permute-start(bf16[32,64,128]{2,1,0:T(8,128)(2,1)S(1)} %collective-permute-done.refs_1_), channel_id=1, source_target_pairs={{0,2},{2,0},{4,6},{6,4},{8,10},{10,8},{12,14},{14,12},{1,3},{3,1},... | collective-permute-start | bytes 1572872 | tf_op jit(solution)/shard_map/ppermute | solution.py:185
  50.2 5.8 %collective-permute-start.8 = (bf16[32,64,128]{2,1,0:T(8,128)(2,1)S(1)}, bf16[32,64,128]{2,1,0:T(8,128)(2,1)S(1)}, u32[]{:S(2)}, u32[]{:S(2)}) collective-permute-start(bf16[32,64,128]{2,1,0:T(8,128)(2,1)S(1)} %collective-permute-done.2.refs_4_), channel_id=1, source_target_pairs={{0,2},{2,0},{4,6},{6,4},{8,10},{10,8},{12,14},{14,12},{1,3},{3,1},... | collective-permute-start | bytes 1572872 | tf_op jit(solution)/shard_map/ppermute | solution.py:185
  50.2 5.4 %collective-permute-start.6 = (bf16[16,64,128]{2,1,0:T(8,128)(2,1)S(1)}, bf16[16,64,128]{2,1,0:T(8,128)(2,1)S(1)}, u32[]{:S(2)}, u32[]{:S(2)}) collective-permute-start(bf16[16,64,128]{2,1,0:T(8,128)(2,1)S(1)} %collective-permute-done.1.refs_2_), channel_id=1, source_target_pairs={{0,2},{2,0},{4,6},{6,4},{8,10},{10,8},{12,14},{14,12},{1,3},{3,1},... | collective-permute-start | bytes 786440 | tf_op jit(solution)/shard_map/ppermute | solution.py:185
  54.5 1.5 %collective-permute-start.7 = (bf16[16,64,128]{2,1,0:T(8,128)(2,1)S(1)}, bf16[16,64,128]{2,1,0:T(8,128)(2,1)S(1)}, u32[]{:S(2)}, u32[]{:S(2)}) collective-permute-start(bf16[16,64,128]{2,1,0:T(8,128)(2,1)S(1)} %collective-permute-done.3.refs_3_), channel_id=1, source_target_pairs={{0,2},{2,0},{4,6},{6,4},{8,10},{10,8},{12,14},{14,12},{1,3},{3,1},... | collective-permute-start | bytes 786440 | tf_op jit(solution)/shard_map/ppermute | solution.py:185
  59.3 2.0 %collective-permute-start.13 = (bf16[128,2048]{1,0:T(8,128)(2,1)S(1)}, bf16[128,2048]{1,0:T(8,128)(2,1)S(1)}, u32[]{:S(2)}, u32[]{:S(2)}) collective-permute-start(bf16[128,2048]{1,0:T(8,128)(2,1)S(1)} %get-tuple-element.8), channel_id=1, source_target_pairs={{0,2},{2,0},{4,6},{6,4},{8,10},{10,8},{12,14},{14,12},{1,3},{3,1},... | collective-permute-start | bytes 1572872 | tf_op jit(solution)/shard_map/ppermute | solution.py:185
  61.5 9.1 %collective-permute-start.14 = (bf16[32,4096]{1,0:T(8,128)(2,1)S(1)}, bf16[32,4096]{1,0:T(8,128)(2,1)S(1)}, u32[]{:S(2)}, u32[]{:S(2)}) collective-permute-start(bf16[32,4096]{1,0:T(8,128)(2,1)S(1)} %get-tuple-element.15), channel_id=1, source_target_pairs={{0,8},{2,10},{4,12},{6,14},{8,0},{10,2},{12,4},{14,6},{1,9},{3,11}... | collective-permute-start | bytes 786440 | tf_op jit(solution)/shard_map/ppermute | solution.py:181
  64.0 12.6 %collective-permute-start.15 = (bf16[32,4096]{1,0:T(8,128)(2,1)S(1)}, bf16[32,4096]{1,0:T(8,128)(2,1)S(1)}, u32[]{:S(2)}, u32[]{:S(2)}) collective-permute-start(bf16[32,4096]{1,0:T(8,128)(2,1)S(1)} %get-tuple-element.16), channel_id=1, source_target_pairs={{0,12},{2,14},{4,0},{6,2},{8,4},{10,6},{12,8},{14,10},{1,13},{3,15... | collective-permute-start | bytes 786440 | tf_op jit(solution)/shard_map/ppermute | solution.py:181
  65.2 11.8 %collective-permute-start.16 = (bf16[32,4096]{1,0:T(8,128)(2,1)S(1)}, bf16[32,4096]{1,0:T(8,128)(2,1)S(1)}, u32[]{:S(2)}, u32[]{:S(2)}) collective-permute-start(bf16[32,4096]{1,0:T(8,128)(2,1)S(1)} %get-tuple-element.13), channel_id=1, source_target_pairs={{0,4},{2,6},{4,8},{6,10},{8,12},{10,14},{12,0},{14,2},{1,5},{3,7},... | collective-permute-start | bytes 786440 | tf_op jit(solution)/shard_map/ppermute | solution.py:181
  76.6 1.0 %copy-start.1 = (bf16[32,16384]{1,0:T(8,128)(2,1)}, bf16[32,16384]{1,0:T(8,128)(2,1)S(1)}, u32[]{:S(2)}) copy-start(bf16[32,16384]{1,0:T(8,128)(2,1)S(1)} %constant_dynamic-update-slice_fusion.1) | copy-start | bytes 3145732

commit v5 on v4

v5 whole, which is shorter than its diff:
```python
import jax
import jax.numpy as jnp
from jax import lax
from jax.experimental import pallas as pl
from jax.experimental.pallas import tpu as pltpu
from jax.sharding import PartitionSpec as P

M = 256
EMPTY = 512
X, Y, Z, GROUPS = 4, 4, 8, 32
LIST_ROWS = 8
DN_NT = (((1,), (1,)), ((), ()))
DN_TN = (((0,), (0,)), ((), ()))


def prepare_kernel(anom_hbm, innov_hbm, seg_hbm, prof_hbm, sent_ref, data, lists, sems):
    sources = (anom_hbm, innov_hbm, seg_hbm, prof_hbm)
    targets = (data.at[0], data.at[1], lists.at[0], lists.at[1])
    loads = [pltpu.make_async_copy(src, dst, sems.at[i]) for i, (src, dst) in enumerate(zip(sources, targets))]
    for load in loads:
        load.start()
    me_cell, me_dp, me_mem = (lax.axis_index(n) for n in ("cell", "dp", "mem"))
    _, mem_dev, data_dev = data.shape
    per_group = lists.shape[1]
    per_block = 2 * per_group
    own_blocks = 128 // per_block

    lane_in = lax.broadcasted_iota(jnp.int32, (128, 256), 0)
    lane_out = lax.broadcasted_iota(jnp.int32, (128, 256), 1)
    start = lax.div(me_mem, 2) * 2 * own_blocks + lax.div(lane_out, 128) * own_blocks
    select = jnp.where(lane_in == start + lax.rem(lane_out, own_blocks), 1.0, 0.0).astype(jnp.bfloat16)
    for load in loads[2:]:
        load.wait()
    ids = lists[0]
    ids = jnp.where(ids >= 0, ids - (me_cell * 2 + me_dp) * data_dev, EMPTY)
    both = jnp.concatenate([ids, lists[1]], axis=0).astype(jnp.float32)
    tiles = [both[:, g * 128 : (g + 1) * 128] for g in range(GROUPS)]
    spread = jnp.dot(jnp.concatenate(tiles, axis=0).astype(jnp.bfloat16), select, preferred_element_type=jnp.float32)
    shape = (GROUPS, per_block, 256)
    lane_out = lax.rem(lax.broadcasted_iota(jnp.int32, shape, 2), 128)
    kept = lax.broadcasted_iota(jnp.int32, shape, 1) == lax.div(lane_out, own_blocks)
    packed = jnp.sum(jnp.where(kept, spread.reshape(shape), 0.0), axis=1)
    for load in loads[:2]:
        load.wait()
    block = jnp.concatenate([data[0], data[1]], axis=0)
    filler = jnp.zeros((LIST_ROWS - 2, 128), jnp.float32)
    for g in range(GROUPS):
        rows = jnp.concatenate([packed[g : g + 1, :128], packed[g : g + 1, 128:], filler], axis=0).astype(jnp.bfloat16)
        sent_ref[g] = jnp.concatenate([block, rows], axis=0)


def prepare(anom, innov, seg, prof):
    mem_dev, data_dev = anom.shape
    return pl.pallas_call(
        prepare_kernel,
        out_shape=jax.ShapeDtypeStruct((GROUPS, 2 * mem_dev + LIST_ROWS, data_dev), jnp.bfloat16),
        in_specs=[pl.BlockSpec(memory_space=pl.ANY)] * 4,
        out_specs=pl.BlockSpec(memory_space=pltpu.VMEM),
        scratch_shapes=[
            pltpu.VMEM((2,) + anom.shape, jnp.bfloat16),
            pltpu.VMEM((2,) + seg.shape, jnp.int32),
            pltpu.SemaphoreType.DMA((4,)),
        ],
        compiler_params=pltpu.CompilerParams(vmem_limit_bytes=60 * 1024 * 1024),
        cost_estimate=pl.CostEstimate(flops=10_000_000, bytes_accessed=400_000, transcendentals=0),
        name="prepare",
    )(anom, innov, seg, prof)


def update_kernel(*refs):
    data = (refs[:X], refs[X : 2 * X])
    near_hbm, far_hbm, lists_near, lists_far, table_ref = refs[2 * X : 2 * X + 5]
    out_near, out_far, state, cols, weights, columns, state_sems = refs[2 * X + 5 :]
    half = near_hbm.shape[0]
    mem_dev = half // X
    data_dev = refs[0].shape[2]
    n_block = near_hbm.shape[1] // 128

    state_loads = [pltpu.make_async_copy(src, state.at[i], state_sems.at[i]) for i, src in enumerate((near_hbm, far_hbm))]
    for load in state_loads:
        load.start()

    me_y = lax.div(lax.axis_index("cell"), 4)
    me_mem = lax.axis_index("mem")
    me_x, me_core = lax.div(me_mem, 2), lax.rem(me_mem, 2)
    x_at = [lax.rem(me_x - i + X, X) * Z for i in range(X)]
    y_at = [lax.rem(me_y - i + Y, Y) * Z for i in range(Y)]

    row = lax.broadcasted_iota(jnp.int32, (128, 128), 0)
    lane = lax.broadcasted_iota(jnp.int32, (128, 128), 1)
    order = jnp.where(lane == lax.rem(row, 8) * n_block + lax.div(row, 8), 1.0, 0.0).astype(jnp.bfloat16)
    lists = []
    for i in range(Y):
        here = [part[pl.ds(y_at[i], Z)].astype(jnp.float32) for part in (lists_near, lists_far)]
        here = jnp.where(me_core == 0, here[0], here[1])
        wanted = lax.broadcasted_iota(jnp.int32, here.shape, 1) == me_core
        lists.append(jnp.sum(jnp.where(wanted, here, 0.0), axis=1))
    lists = jnp.concatenate(lists + [jnp.zeros((128 - GROUPS, 128), jnp.float32)], axis=0).astype(jnp.bfloat16)
    lists = lax.dot_general(order, lists, DN_NT, preferred_element_type=jnp.float32)
    later = pltpu.roll(lists, 127, 1)
    is_first = lax.rem(row, 8) < 4
    columns[...] = jnp.where(is_first, lists, pltpu.roll(later, 4, 0) + data_dev)
    prof_ids = jnp.where(is_first, pltpu.roll(lists, 124, 0), later)

    table = table_ref[...]
    prof_lanes = lax.broadcasted_iota(jnp.int32, (128, table.shape[0]), 1).astype(jnp.float32)
    for pair in range(GROUPS // 2):
        chooser = jnp.where(prof_lanes == prof_ids[:, 2 * pair : 2 * pair + 1], 1.0, 0.0).astype(jnp.bfloat16)
        weight = jnp.dot(chooser, table, preferred_element_type=jnp.float32)
        weights[:, pair * 8 : (pair + 1) * 8] = weight.reshape(n_block, 8, 128)

    def select(core):
        lanes = lax.broadcasted_iota(jnp.int32, (128, 2 * data_dev), 1).astype(jnp.float32)
        ids = columns[...]
        for pair in range(GROUPS // 2):
            i, q = pair // (Z // 2), pair % (Z // 2)
            picker = jnp.where(lanes == ids[:, 2 * pair : 2 * pair + 1], 1.0, 0.0).astype(jnp.bfloat16)
            for side in range(2):

                def piece(s, g, a):
                    rows = slice(a * mem_dev, (a + 1) * mem_dev)
                    if side == core:
                        return data[side][s][y_at[i] + 2 * q + g, rows]
                    return data[side][i][x_at[s] + 2 * q + g, rows]

                values = jnp.concatenate(
                    [
                        jnp.concatenate([piece(s, g, a) for a in range(2) for s in range(X)], axis=0)
                        for g in range(2)
                    ],
                    axis=1,
                )
                picked = lax.dot_general(picker, values, DN_NT, preferred_element_type=jnp.float32)
                picked = picked.reshape(n_block, 8, 2 * half)
                for a in range(2):
                    cols[a, :, pair * 8 : (pair + 1) * 8, side * half : (side + 1) * half] = picked[:, :, a * half : (a + 1) * half]

    for core in range(2):
        pl.when(me_core == core)(lambda core=core: select(core))

    for load in state_loads:
        load.wait()
    for b in range(n_block):
        spot = pl.ds(b * 128, 128)
        own = jnp.concatenate([state[0, :, spot], state[1, :, spot]], axis=0)
        anom = cols[0, b].astype(jnp.bfloat16)
        innov = cols[1, b].astype(jnp.bfloat16)
        inner = jnp.dot(anom, own, preferred_element_type=jnp.float32)
        coef = (weights[b] * inner / (M - 1)).astype(jnp.bfloat16)
        corr = lax.dot_general(innov, coef, DN_TN, preferred_element_type=jnp.float32)
        new = (own.astype(jnp.float32) + corr).astype(jnp.bfloat16)
        out_near[:, spot] = new[:half]
        out_far[:, spot] = new[half:]


def run_update(data, near, far, lists_near, lists_far, table):
    half, width = near.shape
    n_block = width // 128
    n_slot = GROUPS * 4
    any_space = pl.BlockSpec(memory_space=pl.ANY)
    whole = pl.BlockSpec(memory_space=pltpu.VMEM)
    return pl.pallas_call(
        update_kernel,
        out_shape=[jax.ShapeDtypeStruct(near.shape, jnp.bfloat16)] * 2,
        in_specs=[whole] * len(data) + [any_space] * 2 + [whole] * 3,
        out_specs=[whole] * 2,
        scratch_shapes=[
            pltpu.VMEM((2,) + near.shape, jnp.bfloat16),
            pltpu.VMEM((2, n_block, n_slot, 2 * half), jnp.float32),
            pltpu.VMEM((n_block, n_slot, 128), jnp.float32),
            pltpu.VMEM((128, 128), jnp.float32),
            pltpu.SemaphoreType.DMA((2,)),
        ],
        compiler_params=pltpu.CompilerParams(vmem_limit_bytes=16 * 1024 * 1024),
        cost_estimate=pl.CostEstimate(flops=800_000_000, bytes_accessed=6_500_000, transcendentals=0),
        name="update",
    )(*data, near, far, lists_near, lists_far, table)


def device(x, y, z, core):
    return ((y * 4 + z // 2) * 2 * X + x * 2 + core) * 2 + z % 2


X_SHIFT = [[(x * 2 + c, ((x + s) % X) * 2 + c) for x in range(X) for c in range(2)] for s in range(X)]
EVERY = ("cell", "mem", "dp")
PLANES = [[device(x, y, z, 0) for y in range(Y) for z in range(Z)] for x in range(X)]
PLANES += [[device(x, y, z, 1) for x in range(X) for z in range(Z)] for y in range(Y)]
CROSS = [
    [(device(x, y, z, 0), device((x + s) % X, y, z, 0)) for x in range(X) for y in range(Y) for z in range(Z)]
    + [(device(x, y, z, 1), device(x, (y + s) % Y, z, 1)) for x in range(X) for y in range(Y) for z in range(Z)]
    for s in range(X)
]
CORE_SWAP = [(i, i ^ 1) for i in range(2 * X)]


def to_x(piece, s):
    return lax.ppermute(piece, "mem", X_SHIFT[s % X])


def cross(piece, s):
    return lax.ppermute(piece, EVERY, CROSS[s % X])


def after(pieces, others):
    return lax.optimization_barrier((pieces, others))[0]


def swap(piece):
    return lax.ppermute(piece, "mem", CORE_SWAP)


def local(ensemble, data_anom, weighted_innov, profiles, seg_data, seg_profile):
    me_dp, me_mem = lax.axis_index("dp"), lax.axis_index("mem")
    me_x, me_core = me_mem // 2, me_mem % 2
    mem_dev, cells_dev = ensemble.shape
    half_cells = cells_dev // 2
    x_cells = half_cells // X
    own_cells = x_cells // 2

    sent = prepare(data_anom, weighted_innov, seg_data, seg_profile)
    got = lax.all_to_all(sent, EVERY, 0, 0, tiled=True, axis_index_groups=PLANES)

    def state_for(s):
        x_to = (me_x + s) % X
        return lax.dynamic_slice_in_dim(ensemble, me_dp * half_cells + x_to * x_cells, x_cells, 1)

    pieces = [state_for(0)] + [None] * 3
    for s in (2, 1, 3):
        pieces[s] = to_x(state_for(s), s)
    data_rows = 2 * mem_dev
    own = after(got, pieces[1:])[:, :data_rows]
    data_near = [got] + [None] * 3
    for s in (2, 1, 3):
        data_near[s] = cross(own, s)
    data_far = [swap(d) for d in data_near]
    first = me_core == 0
    lists_near, lists_far = got[:, data_rows:], data_far[0][:, data_rows:]

    state = jnp.concatenate(after(pieces, data_near[1]), axis=0)
    near = lax.dynamic_slice_in_dim(state, me_core * own_cells, own_cells, 1)
    far = swap(lax.dynamic_slice_in_dim(state, (1 - me_core) * own_cells, own_cells, 1))

    new_near, new_far = run_update(data_near + data_far, near, far, lists_near, lists_far, profiles)

    across = slice(2 * mem_dev, 3 * mem_dev)
    near2 = to_x(new_near[across], 2)
    back_far = swap(new_far)
    far2 = to_x(back_far[across], 2)
    new = jnp.concatenate([jnp.where(first, new_near, back_far), jnp.where(first, back_far, new_near)], axis=1)
    out = jnp.zeros((mem_dev, half_cells), jnp.bfloat16)

    def place(out, piece, s, start):
        return lax.dynamic_update_slice_in_dim(out, piece, ((me_x + s) % X) * x_cells + start, 1)

    out = place(out, new[:mem_dev], 0, 0)
    backs = [to_x(new[s * mem_dev : (s + 1) * mem_dev], -s) for s in (1, 3)]
    out = place(out, near2, 2, me_core * own_cells)
    out = place(out, far2, 2, (1 - me_core) * own_cells)
    out = place(out, backs[0], 1, 0)
    return place(out, backs[1], 3, 0)


def solution(mesh):
    placed = (
        P("mem", "cell"),
        P("mem", ("cell", "dp")),
        P("mem", ("cell", "dp")),
        P(),
        P(("cell", "dp"), None),
        P(("cell", "dp"), None),
    )
    return jax.shard_map(
        local, mesh=mesh, in_specs=placed, out_specs=P("mem", ("cell", "dp")), check_vma=False
    )
```

time: 78.5 us -> 74 us (0.943)
  starting transfers between devices: 40.1 us -> 34.5 us
  waiting for transfers between devices: 29.5 us -> 31.1 us
    ppermute x7 -> x6, starting transfers between devices: 14.3 us -> 7.63 us  [swap(): return lax.ppermute(piece, 'mem', CORE_SWAP)]
    ppermute x0 -> x3, waiting for transfers between devices: none -> 6.3 us  [cross(): return lax.ppermute(piece, EVERY, CROSS[s % X])]
    ppermute x0 -> x3, starting transfers between devices: none -> 4.96 us  [cross(): return lax.ppermute(piece, EVERY, CROSS[s % X])]
    ppermute x10 -> x7, starting transfers between devices: 13.8 us -> 10 us  [to_x(): return lax.ppermute(piece, 'mem', X_SHIFT[s % X])]
    ppermute x10 -> x7, waiting for transfers between devices: 26.1 us -> 22.5 us  [to_x(): return lax.ppermute(piece, 'mem', X_SHIFT[s % X])]
    ppermute x7 -> x6, waiting for transfers between devices: 2.73 us -> 2.24 us  [swap(): return lax.ppermute(piece, 'mem', CORE_SWAP)]
  transfers between devices with their start and end apart: 18 -> 17, of which waited for: 11 -> 10; matrix products, arithmetic and copies ran while one was open for 2% -> 2% of each run, Pallas kernels for 0% -> 0%
where the time goes in v5:
time: 74 us; the launch traced here: 73.6 us
  starting transfers between devices  34.5 us (47%)
  waiting for transfers between devices  31.1 us (42%)
  Pallas kernels  5.26 us (7%)
  local copies, waits for them, and re-layouts  2.43 us (3%)
    ppermute x7, waiting for transfers between devices, to_x(): return lax.ppermute(piece, 'mem', X_SHIFT[s % X])  22.5 us
    all_to_all x1, starting transfers between devices, local(): lax.all_to_all(sent, EVERY, 0, 0, tiled=True, axis_index_groups=PLANES)  11.9 us
    ppermute x7, starting transfers between devices, to_x(): return lax.ppermute(piece, 'mem', X_SHIFT[s % X])  10 us
    ppermute x6, starting transfers between devices, swap(): return lax.ppermute(piece, 'mem', CORE_SWAP)  7.63 us
    ppermute x3, waiting for transfers between devices, cross(): return lax.ppermute(piece, EVERY, CROSS[s % X])  6.3 us
    ppermute x3, starting transfers between devices, cross(): return lax.ppermute(piece, EVERY, CROSS[s % X])  4.96 us
    pallas_call x1, Pallas kernels, run_update(): pl.pallas_call(update_kernel, out_shape=[jax.ShapeDtypeStruct(near.shape,...  3.23 us
    ppermute x6, waiting for transfers between devices, swap(): return lax.ppermute(piece, 'mem', CORE_SWAP)  2.24 us
  transfers between devices with their start and end apart: 17, of which 10 were waited for; matrix products, arithmetic and copies ran while one was open for 2% of the time, Pallas kernels for 0%

profile of v5, /device:TPU:1, one launch (start us, length us, event | category | flops | bytes accessed | tf_op | source)
XLA Modules:
  0.0 73.6 jit_solution(3940565211238880147)
XLA Ops:
  0.0 2.0 %prepare.1 = bf16[32,72,128]{2,1,0:T(8,128)(2,1)} custom-call(bf16[32,128]{1,0:T(8,128)(2,1)} %anom_hbm.1, bf16[32,128]{1,0:T(8,128)(2,1)} %innov_hbm.1, s32[4,4096]{1,0:T(4,128)} %seg_hbm.1, s32[4,4096]{1,0:T(4,128)} %prof_hbm.1), custom_call_target="tpu_custom_call" | custom-call | flops 10000000 | bytes 400000 | tf_op jit(solution)/shard_map/prepare/pallas_call | solution.py:54
  2.0 11.9 %all-to-all-start = ((bf16[32,72,128]{2,1,0:T(8,128)(2,1)}), bf16[32,72,128]{2,1,0:T(8,128)(2,1)S(1)}, u32[]{:S(2)}, u32[]{:S(2)}) async-start(bf16[32,72,128]{2,1,0:T(8,128)(2,1)} %prepare.1), calls=%async_computation | async-start | bytes 1179648 | tf_op jit(solution)/shard_map/all_to_all | solution.py:221
  14.0 1.3 %constant_dynamic-slice_fusion.2 = (bf16[32,4096]{1,0:T(8,128)(2,1)S(1)}, bf16[32,4096]{1,0:T(8,128)(2,1)S(1)}, bf16[32,4096]{1,0:T(8,128)(2,1)S(1)}, bf16[32,4096]{1,0:T(8,128)(2,1)S(1)}) fusion(bf16[32,32768]{1,0:T(8,128)(2,1)} %param.6, s32[]{:T(128)S(6)} %select_n.92, s32[]{:T(128)S(6)} %select_n.88, s32[]{:T(128)S(6)} %select_n.86, s32[]{:T(128)S(6)} %select_n.90), kind=kLoop, calls=%fused_computation.15 | loop fusion | bytes 2097168 | tf_op jit(solution)/shard_map/dynamic_slice | solution.py:225
  15.3 1.3 %collective-permute-start = (bf16[32,4096]{1,0:T(8,128)(2,1)S(1)}, bf16[32,4096]{1,0:T(8,128)(2,1)S(1)}, u32[]{:S(2)}, u32[]{:S(2)}) collective-permute-start(bf16[32,4096]{1,0:T(8,128)(2,1)S(1)} %get-tuple-element.21), channel_id=1, source_target_pairs={{0,4},{2,6},{4,8},{6,10},{8,12},{10,14},{12,0},{14,2},{1,5},{3,7},... | collective-permute-start | bytes 786440 | tf_op jit(solution)/shard_map/ppermute | solution.py:197
  16.6 2.4 %collective-permute-start.1 = (bf16[32,4096]{1,0:T(8,128)(2,1)S(1)}, bf16[32,4096]{1,0:T(8,128)(2,1)S(1)}, u32[]{:S(2)}, u32[]{:S(2)}) collective-permute-start(bf16[32,4096]{1,0:T(8,128)(2,1)S(1)} %get-tuple-element.20), channel_id=1, source_target_pairs={{0,8},{2,10},{4,12},{6,14},{8,0},{10,2},{12,4},{14,6},{1,9},{3,11}... | collective-permute-start | bytes 786440 | tf_op jit(solution)/shard_map/ppermute | solution.py:197
  19.0 1.1 %collective-permute-start.2 = (bf16[32,4096]{1,0:T(8,128)(2,1)S(1)}, bf16[32,4096]{1,0:T(8,128)(2,1)S(1)}, u32[]{:S(2)}, u32[]{:S(2)}) collective-permute-start(bf16[32,4096]{1,0:T(8,128)(2,1)S(1)} %get-tuple-element.22), channel_id=1, source_target_pairs={{0,12},{2,14},{4,0},{6,2},{8,4},{10,6},{12,8},{14,10},{1,13},{3,15... | collective-permute-start | bytes 786440 | tf_op jit(solution)/shard_map/ppermute | solution.py:197
  20.2 5.3 %collective-permute-done = bf16[32,4096]{1,0:T(8,128)(2,1)S(1)} collective-permute-done((bf16[32,4096]{1,0:T(8,128)(2,1)S(1)}, bf16[32,4096]{1,0:T(8,128)(2,1)S(1)}, u32[]{:S(2)}, u32[]{:S(2)}) %collective-permute-start) | collective-permute-done | bytes 262176 | tf_op jit(solution)/shard_map/ppermute | solution.py:197
  25.5 7.5 %collective-permute-done.1 = bf16[32,4096]{1,0:T(8,128)(2,1)S(1)} collective-permute-done((bf16[32,4096]{1,0:T(8,128)(2,1)S(1)}, bf16[32,4096]{1,0:T(8,128)(2,1)S(1)}, u32[]{:S(2)}, u32[]{:S(2)}) %collective-permute-start.1) | collective-permute-done | bytes 262176 | tf_op jit(solution)/shard_map/ppermute | solution.py:197
  33.0 0.0 collective-permute-done.2
  33.0 0.0 all-to-all-done.refs_0_
  33.0 0.1 slice.24
  33.1 1.2 %collective-permute-start.3 = (bf16[32,64,128]{2,1,0:T(8,128)(2,1)S(1)}, bf16[32,64,128]{2,1,0:T(8,128)(2,1)S(1)}, u32[]{:S(2)}, u32[]{:S(2)}) collective-permute-start(bf16[32,64,128]{2,1,0:T(8,128)(2,1)S(1)} %slice.24), channel_id=1, source_target_pairs={{0,4},{1,5},{16,20},{17,21},{32,36},{33,37},{48,52},{49,53},{64,68... | collective-permute-start | bytes 1572872 | tf_op jit(solution)/shard_map/ppermute | solution.py:201
  34.2 2.8 %collective-permute-start.4 = (bf16[32,64,128]{2,1,0:T(8,128)(2,1)S(1)}, bf16[32,64,128]{2,1,0:T(8,128)(2,1)S(1)}, u32[]{:S(2)}, u32[]{:S(2)}) collective-permute-start(bf16[32,64,128]{2,1,0:T(8,128)(2,1)S(1)} %slice.24), channel_id=1, source_target_pairs={{0,8},{1,9},{16,24},{17,25},{32,40},{33,41},{48,56},{49,57},{64,72... | collective-permute-start | bytes 1572872 | tf_op jit(solution)/shard_map/ppermute | solution.py:201
  37.0 1.0 %collective-permute-start.5 = (bf16[32,64,128]{2,1,0:T(8,128)(2,1)S(1)}, bf16[32,64,128]{2,1,0:T(8,128)(2,1)S(1)}, u32[]{:S(2)}, u32[]{:S(2)}) collective-permute-start(bf16[32,64,128]{2,1,0:T(8,128)(2,1)S(1)} %slice.24), channel_id=1, source_target_pairs={{0,12},{1,13},{16,28},{17,29},{32,44},{33,45},{48,60},{49,61},{64,... | collective-permute-start | bytes 1572872 | tf_op jit(solution)/shard_map/ppermute | solution.py:201
  38.0 2.4 %collective-permute-start.6 = (bf16[32,72,128]{2,1,0:T(8,128)(2,1)S(1)}, bf16[32,72,128]{2,1,0:T(8,128)(2,1)S(1)}, u32[]{:S(2)}, u32[]{:S(2)}) collective-permute-start(bf16[32,72,128]{2,1,0:T(8,128)(2,1)S(1)} %all-to-all-done.refs_0_), channel_id=1, source_target_pairs={{0,2},{2,0},{4,6},{6,4},{8,10},{10,8},{12,14},{14,12},{1,3},{3,1},... | collective-permute-start | bytes 1769480 | tf_op jit(solution)/shard_map/ppermute | solution.py:209
  40.4 2.3 %collective-permute-done.3.refs_1_ = bf16[32,64,128]{2,1,0:T(8,128)(2,1)S(1)} collective-permute-done((bf16[32,64,128]{2,1,0:T(8,128)(2,1)S(1)}, bf16[32,64,128]{2,1,0:T(8,128)(2,1)S(1)}, u32[]{:S(2)}, u32[]{:S(2)}) %collective-permute-start.3) | collective-permute-done | bytes 524320 | tf_op jit(solution)/shard_map/ppermute | solution.py:201
  42.7 0.0 copy-start
  42.8 0.1 constant_dynamic-slice_fusion
  42.9 2.4 %collective-permute-start.10 = (bf16[128,2048]{1,0:T(8,128)(2,1)S(1)}, bf16[128,2048]{1,0:T(8,128)(2,1)S(1)}, u32[]{:S(2)}, u32[]{:S(2)}) collective-permute-start(bf16[128,2048]{1,0:T(8,128)(2,1)S(1)} %get-tuple-element.28), channel_id=1, source_target_pairs={{0,2},{2,0},{4,6},{6,4},{8,10},{10,8},{12,14},{14,12},{1,3},{3,1},... | collective-permute-start | bytes 1572872 | tf_op jit(solution)/shard_map/ppermute | solution.py:209
  45.4 0.1 collective-permute-start.7
  45.5 4.0 %collective-permute-done.4.refs_2_ = bf16[32,64,128]{2,1,0:T(8,128)(2,1)S(1)} collective-permute-done((bf16[32,64,128]{2,1,0:T(8,128)(2,1)S(1)}, bf16[32,64,128]{2,1,0:T(8,128)(2,1)S(1)}, u32[]{:S(2)}, u32[]{:S(2)}) %collective-permute-start.4) | collective-permute-done | bytes 524320 | tf_op jit(solution)/shard_map/ppermute | solution.py:201
  49.5 2.3 %collective-permute-start.8 = (bf16[32,64,128]{2,1,0:T(8,128)(2,1)S(1)}, bf16[32,64,128]{2,1,0:T(8,128)(2,1)S(1)}, u32[]{:S(2)}, u32[]{:S(2)}) collective-permute-start(bf16[32,64,128]{2,1,0:T(8,128)(2,1)S(1)} %collective-permute-done.4.refs_2_), channel_id=1, source_target_pairs={{0,2},{2,0},{4,6},{6,4},{8,10},{10,8},{12,14},{14,12},{1,3},{3,1},... | collective-permute-start | bytes 1572872 | tf_op jit(solution)/shard_map/ppermute | solution.py:209
  51.8 0.0 collective-permute-done.5.refs_3_
  51.8 0.0 collective-permute-start.9
  51.8 0.0 collective-permute-done.6.refs_4_
  51.8 0.0 collective-permute-done.10.refs_9_
  51.8 0.0 collective-permute-done.7.refs_5_
  51.8 1.5 %collective-permute-done.8.refs_6_ = bf16[32,64,128]{2,1,0:T(8,128)(2,1)S(1)} collective-permute-done((bf16[32,64,128]{2,1,0:T(8,128)(2,1)S(1)}, bf16[32,64,128]{2,1,0:T(8,128)(2,1)S(1)}, u32[]{:S(2)}, u32[]{:S(2)}) %collective-permute-start.8) | collective-permute-done | bytes 524320 | tf_op jit(solution)/shard_map/ppermute | solution.py:209
  53.3 0.7 %collective-permute-done.9.refs_7_ = bf16[32,64,128]{2,1,0:T(8,128)(2,1)S(1)} collective-permute-done((bf16[32,64,128]{2,1,0:T(8,128)(2,1)S(1)}, bf16[32,64,128]{2,1,0:T(8,128)(2,1)S(1)}, u32[]{:S(2)}, u32[]{:S(2)}) %collective-permute-start.9) | collective-permute-done | bytes 524320 | tf_op jit(solution)/shard_map/ppermute | solution.py:209
  54.0 0.0 copy-done
  54.1 3.2 %update.1 = (bf16[128,2048]{1,0:T(8,128)(2,1)S(1)}, bf16[128,2048]{1,0:T(8,128)(2,1)S(1)}) custom-call(bf16[32,72,128]{2,1,0:T(8,128)(2,1)S(1)} %all-to-all-done.refs_0_, bf16[32,64,128]{2,1,0:T(8,128)(2,1)S(1)} %collective-permute-done.3.refs_1_, bf16[32,64,128]{2,1,0:T(8,128)(2,1)S(1)} %collective-permute-done.4.refs_2_, ...), custom_call_target="tpu_custom_call" | custom-call | flops 800000000 | bytes 6500000 | tf_op jit(solution)/shard_map/update/pallas_call | solution.py:162
  57.3 0.4 collective-permute-start.11
  57.7 2.2 %collective-permute-start.12 = (bf16[32,2048]{1,0:T(8,128)(2,1)S(1)}, bf16[32,2048]{1,0:T(8,128)(2,1)S(1)}, u32[]{:S(2)}, u32[]{:S(2)}) collective-permute-start(bf16[32,2048]{1,0:T(8,128)(2,1)S(1)} %slice.28), channel_id=1, source_target_pairs={{0,8},{2,10},{4,12},{6,14},{8,0},{10,2},{12,4},{14,6},{1,9},{3,11}... | collective-permute-start | bytes 393224 | tf_op jit(solution)/shard_map/ppermute | solution.py:197
  59.9 0.0 collective-permute-done.11
  59.9 1.4 %collective-permute-start.13 = (bf16[32,2048]{1,0:T(8,128)(2,1)S(1)}, bf16[32,2048]{1,0:T(8,128)(2,1)S(1)}, u32[]{:S(2)}, u32[]{:S(2)}) collective-permute-start(bf16[32,2048]{1,0:T(8,128)(2,1)S(1)} %slice.34), channel_id=1, source_target_pairs={{0,8},{2,10},{4,12},{6,14},{8,0},{10,2},{12,4},{14,6},{1,9},{3,11}... | collective-permute-start | bytes 393224 | tf_op jit(solution)/shard_map/ppermute | solution.py:197
  61.3 0.1 broadcast_select_fusion.1
  61.4 0.1 broadcast_in_dim.3
  61.5 0.1 pad_maximum_fusion
  61.5 1.3 %collective-permute-start.14 = (bf16[32,4096]{1,0:T(8,128)(2,1)S(1)}, bf16[32,4096]{1,0:T(8,128)(2,1)S(1)}, u32[]{:S(2)}, u32[]{:S(2)}) collective-permute-start(bf16[32,4096]{1,0:T(8,128)(2,1)S(1)} %get-tuple-element.24), channel_id=1, source_target_pairs={{0,12},{2,14},{4,0},{6,2},{8,4},{10,6},{12,8},{14,10},{1,13},{3,15... | collective-permute-start | bytes 786440 | tf_op jit(solution)/shard_map/ppermute | solution.py:197
  62.9 0.2 collective-permute-start.15
  63.1 1.3 %collective-permute-done.12 = bf16[32,2048]{1,0:T(8,128)(2,1)S(1)} collective-permute-done((bf16[32,2048]{1,0:T(8,128)(2,1)S(1)}, bf16[32,2048]{1,0:T(8,128)(2,1)S(1)}, u32[]{:S(2)}, u32[]{:S(2)}) %collective-permute-start.12) | collective-permute-done | bytes 131104 | tf_op jit(solution)/shard_map/ppermute | solution.py:197
  64.4 2.8 %collective-permute-done.13 = bf16[32,2048]{1,0:T(8,128)(2,1)S(1)} collective-permute-done((bf16[32,2048]{1,0:T(8,128)(2,1)S(1)}, bf16[32,2048]{1,0:T(8,128)(2,1)S(1)}, u32[]{:S(2)}, u32[]{:S(2)}) %collective-permute-start.13) | collective-permute-done | bytes 131104 | tf_op jit(solution)/shard_map/ppermute | solution.py:197
  67.2 4.7 %collective-permute-done.14 = bf16[32,4096]{1,0:T(8,128)(2,1)S(1)} collective-permute-done((bf16[32,4096]{1,0:T(8,128)(2,1)S(1)}, bf16[32,4096]{1,0:T(8,128)(2,1)S(1)}, u32[]{:S(2)}, u32[]{:S(2)}) %collective-permute-start.14) | collective-permute-done | bytes 262176 | tf_op jit(solution)/shard_map/ppermute | solution.py:197
  72.0 0.0 copy-start.1
  72.0 0.9 %collective-permute-done.15 = bf16[32,4096]{1,0:T(8,128)(2,1)S(1)} collective-permute-done((bf16[32,4096]{1,0:T(8,128)(2,1)S(1)}, bf16[32,4096]{1,0:T(8,128)(2,1)S(1)}, u32[]{:S(2)}, u32[]{:S(2)}) %collective-permute-start.15) | collective-permute-done | bytes 262176 | tf_op jit(solution)/shard_map/ppermute | solution.py:197
  72.9 0.0 copy-done.1
  72.9 0.7 constant_dynamic-update-slice_fusion.4
  (11 shorter events, 0.2 us)
Async XLA Ops:
  2.0 31.0 %all-to-all-start = ((bf16[32,72,128]{2,1,0:T(8,128)(2,1)}), bf16[32,72,128]{2,1,0:T(8,128)(2,1)S(1)}, u32[]{:S(2)}, u32[]{:S(2)}) async-start(bf16[32,72,128]{2,1,0:T(8,128)(2,1)} %prepare.1), calls=%async_computation | async-start | bytes 1179648 | tf_op jit(solution)/shard_map/all_to_all | solution.py:221
  15.3 10.2 %collective-permute-start = (bf16[32,4096]{1,0:T(8,128)(2,1)S(1)}, bf16[32,4096]{1,0:T(8,128)(2,1)S(1)}, u32[]{:S(2)}, u32[]{:S(2)}) collective-permute-start(bf16[32,4096]{1,0:T(8,128)(2,1)S(1)} %get-tuple-element.21), channel_id=1, source_target_pairs={{0,4},{2,6},{4,8},{6,10},{8,12},{10,14},{12,0},{14,2},{1,5},{3,7},... | collective-permute-start | bytes 786440 | tf_op jit(solution)/shard_map/ppermute | solution.py:197
  16.6 16.4 %collective-permute-start.1 = (bf16[32,4096]{1,0:T(8,128)(2,1)S(1)}, bf16[32,4096]{1,0:T(8,128)(2,1)S(1)}, u32[]{:S(2)}, u32[]{:S(2)}) collective-permute-start(bf16[32,4096]{1,0:T(8,128)(2,1)S(1)} %get-tuple-element.20), channel_id=1, source_target_pairs={{0,8},{2,10},{4,12},{6,14},{8,0},{10,2},{12,4},{14,6},{1,9},{3,11}... | collective-permute-start | bytes 786440 | tf_op jit(solution)/shard_map/ppermute | solution.py:197
  19.0 13.9 %collective-permute-start.2 = (bf16[32,4096]{1,0:T(8,128)(2,1)S(1)}, bf16[32,4096]{1,0:T(8,128)(2,1)S(1)}, u32[]{:S(2)}, u32[]{:S(2)}) collective-permute-start(bf16[32,4096]{1,0:T(8,128)(2,1)S(1)} %get-tuple-element.22), channel_id=1, source_target_pairs={{0,12},{2,14},{4,0},{6,2},{8,4},{10,6},{12,8},{14,10},{1,13},{3,15... | collective-permute-start | bytes 786440 | tf_op jit(solution)/shard_map/ppermute | solution.py:197
  33.1 9.7 %collective-permute-start.3 = (bf16[32,64,128]{2,1,0:T(8,128)(2,1)S(1)}, bf16[32,64,128]{2,1,0:T(8,128)(2,1)S(1)}, u32[]{:S(2)}, u32[]{:S(2)}) collective-permute-start(bf16[32,64,128]{2,1,0:T(8,128)(2,1)S(1)} %slice.24), channel_id=1, source_target_pairs={{0,4},{1,5},{16,20},{17,21},{32,36},{33,37},{48,52},{49,53},{64,68... | collective-permute-start | bytes 1572872 | tf_op jit(solution)/shard_map/ppermute | solution.py:201
  34.2 15.3 %collective-permute-start.4 = (bf16[32,64,128]{2,1,0:T(8,128)(2,1)S(1)}, bf16[32,64,128]{2,1,0:T(8,128)(2,1)S(1)}, u32[]{:S(2)}, u32[]{:S(2)}) collective-permute-start(bf16[32,64,128]{2,1,0:T(8,128)(2,1)S(1)} %slice.24), channel_id=1, source_target_pairs={{0,8},{1,9},{16,24},{17,25},{32,40},{33,41},{48,56},{49,57},{64,72... | collective-permute-start | bytes 1572872 | tf_op jit(solution)/shard_map/ppermute | solution.py:201
  37.0 14.7 %collective-permute-start.5 = (bf16[32,64,128]{2,1,0:T(8,128)(2,1)S(1)}, bf16[32,64,128]{2,1,0:T(8,128)(2,1)S(1)}, u32[]{:S(2)}, u32[]{:S(2)}) collective-permute-start(bf16[32,64,128]{2,1,0:T(8,128)(2,1)S(1)} %slice.24), channel_id=1, source_target_pairs={{0,12},{1,13},{16,28},{17,29},{32,44},{33,45},{48,60},{49,61},{64,... | collective-permute-start | bytes 1572872 | tf_op jit(solution)/shard_map/ppermute | solution.py:201
  38.0 13.8 %collective-permute-start.6 = (bf16[32,72,128]{2,1,0:T(8,128)(2,1)S(1)}, bf16[32,72,128]{2,1,0:T(8,128)(2,1)S(1)}, u32[]{:S(2)}, u32[]{:S(2)}) collective-permute-start(bf16[32,72,128]{2,1,0:T(8,128)(2,1)S(1)} %all-to-all-done.refs_0_), channel_id=1, source_target_pairs={{0,2},{2,0},{4,6},{6,4},{8,10},{10,8},{12,14},{14,12},{1,3},{3,1},... | collective-permute-start | bytes 1769480 | tf_op jit(solution)/shard_map/ppermute | solution.py:209
  42.7 11.3 %copy-start = (bf16[64,128]{1,0:T(8,128)(2,1)S(1)}, bf16[64,128]{1,0:T(8,128)(2,1)}, u32[]{:S(2)}) copy-start(bf16[64,128]{1,0:T(8,128)(2,1)} %refs_12_.1) | copy-start | bytes 49156
  42.9 8.9 %collective-permute-start.10 = (bf16[128,2048]{1,0:T(8,128)(2,1)S(1)}, bf16[128,2048]{1,0:T(8,128)(2,1)S(1)}, u32[]{:S(2)}, u32[]{:S(2)}) collective-permute-start(bf16[128,2048]{1,0:T(8,128)(2,1)S(1)} %get-tuple-element.28), channel_id=1, source_target_pairs={{0,2},{2,0},{4,6},{6,4},{8,10},{10,8},{12,14},{14,12},{1,3},{3,1},... | collective-permute-start | bytes 1572872 | tf_op jit(solution)/shard_map/ppermute | solution.py:209
  45.4 6.4 %collective-permute-start.7 = (bf16[32,64,128]{2,1,0:T(8,128)(2,1)S(1)}, bf16[32,64,128]{2,1,0:T(8,128)(2,1)S(1)}, u32[]{:S(2)}, u32[]{:S(2)}) collective-permute-start(bf16[32,64,128]{2,1,0:T(8,128)(2,1)S(1)} %collective-permute-done.3.refs_1_), channel_id=1, source_target_pairs={{0,2},{2,0},{4,6},{6,4},{8,10},{10,8},{12,14},{14,12},{1,3},{3,1},... | collective-permute-start | bytes 1572872 | tf_op jit(solution)/shard_map/ppermute | solution.py:209
  49.5 3.8 %collective-permute-start.8 = (bf16[32,64,128]{2,1,0:T(8,128)(2,1)S(1)}, bf16[32,64,128]{2,1,0:T(8,128)(2,1)S(1)}, u32[]{:S(2)}, u32[]{:S(2)}) collective-permute-start(bf16[32,64,128]{2,1,0:T(8,128)(2,1)S(1)} %collective-permute-done.4.refs_2_), channel_id=1, source_target_pairs={{0,2},{2,0},{4,6},{6,4},{8,10},{10,8},{12,14},{14,12},{1,3},{3,1},... | collective-permute-start | bytes 1572872 | tf_op jit(solution)/shard_map/ppermute | solution.py:209
  51.8 2.3 %collective-permute-start.9 = (bf16[32,64,128]{2,1,0:T(8,128)(2,1)S(1)}, bf16[32,64,128]{2,1,0:T(8,128)(2,1)S(1)}, u32[]{:S(2)}, u32[]{:S(2)}) collective-permute-start(bf16[32,64,128]{2,1,0:T(8,128)(2,1)S(1)} %collective-permute-done.5.refs_3_), channel_id=1, source_target_pairs={{0,2},{2,0},{4,6},{6,4},{8,10},{10,8},{12,14},{14,12},{1,3},{3,1},... | collective-permute-start | bytes 1572872 | tf_op jit(solution)/shard_map/ppermute | solution.py:209
  57.3 2.6 %collective-permute-start.11 = (bf16[128,2048]{1,0:T(8,128)(2,1)S(1)}, bf16[128,2048]{1,0:T(8,128)(2,1)S(1)}, u32[]{:S(2)}, u32[]{:S(2)}) collective-permute-start(bf16[128,2048]{1,0:T(8,128)(2,1)S(1)} %get-tuple-element.18), channel_id=1, source_target_pairs={{0,2},{2,0},{4,6},{6,4},{8,10},{10,8},{12,14},{14,12},{1,3},{3,1},... | collective-permute-start | bytes 1572872 | tf_op jit(solution)/shard_map/ppermute | solution.py:209
  57.7 6.7 %collective-permute-start.12 = (bf16[32,2048]{1,0:T(8,128)(2,1)S(1)}, bf16[32,2048]{1,0:T(8,128)(2,1)S(1)}, u32[]{:S(2)}, u32[]{:S(2)}) collective-permute-start(bf16[32,2048]{1,0:T(8,128)(2,1)S(1)} %slice.28), channel_id=1, source_target_pairs={{0,8},{2,10},{4,12},{6,14},{8,0},{10,2},{12,4},{14,6},{1,9},{3,11}... | collective-permute-start | bytes 393224 | tf_op jit(solution)/shard_map/ppermute | solution.py:197
  59.9 7.3 %collective-permute-start.13 = (bf16[32,2048]{1,0:T(8,128)(2,1)S(1)}, bf16[32,2048]{1,0:T(8,128)(2,1)S(1)}, u32[]{:S(2)}, u32[]{:S(2)}) collective-permute-start(bf16[32,2048]{1,0:T(8,128)(2,1)S(1)} %slice.34), channel_id=1, source_target_pairs={{0,8},{2,10},{4,12},{6,14},{8,0},{10,2},{12,4},{14,6},{1,9},{3,11}... | collective-permute-start | bytes 393224 | tf_op jit(solution)/shard_map/ppermute | solution.py:197
  61.5 10.4 %collective-permute-start.14 = (bf16[32,4096]{1,0:T(8,128)(2,1)S(1)}, bf16[32,4096]{1,0:T(8,128)(2,1)S(1)}, u32[]{:S(2)}, u32[]{:S(2)}) collective-permute-start(bf16[32,4096]{1,0:T(8,128)(2,1)S(1)} %get-tuple-element.24), channel_id=1, source_target_pairs={{0,12},{2,14},{4,0},{6,2},{8,4},{10,6},{12,8},{14,10},{1,13},{3,15... | collective-permute-start | bytes 786440 | tf_op jit(solution)/shard_map/ppermute | solution.py:197
  62.9 10.0 %collective-permute-start.15 = (bf16[32,4096]{1,0:T(8,128)(2,1)S(1)}, bf16[32,4096]{1,0:T(8,128)(2,1)S(1)}, u32[]{:S(2)}, u32[]{:S(2)}) collective-permute-start(bf16[32,4096]{1,0:T(8,128)(2,1)S(1)} %get-tuple-element.23), channel_id=1, source_target_pairs={{0,4},{2,6},{4,8},{6,10},{8,12},{10,14},{12,0},{14,2},{1,5},{3,7},... | collective-permute-start | bytes 786440 | tf_op jit(solution)/shard_map/ppermute | solution.py:197
  72.0 1.0 %copy-start.1 = (bf16[32,16384]{1,0:T(8,128)(2,1)}, bf16[32,16384]{1,0:T(8,128)(2,1)S(1)}, u32[]{:S(2)}) copy-start(bf16[32,16384]{1,0:T(8,128)(2,1)S(1)} %constant_dynamic-update-slice_fusion.5) | copy-start | bytes 3145732

commit v6 on v5

--- a/solution.py
+++ b/solution.py
@@ -67,23 +67,11 @@
     )(anom, innov, seg, prof)
 
 
-def update_kernel(*refs):
-    data = (refs[:X], refs[X : 2 * X])
-    near_hbm, far_hbm, lists_near, lists_far, table_ref = refs[2 * X : 2 * X + 5]
-    out_near, out_far, state, cols, weights, columns, state_sems = refs[2 * X + 5 :]
-    half = near_hbm.shape[0]
-    mem_dev = half // X
-    data_dev = refs[0].shape[2]
-    n_block = near_hbm.shape[1] // 128
-
-    state_loads = [pltpu.make_async_copy(src, state.at[i], state_sems.at[i]) for i, src in enumerate((near_hbm, far_hbm))]
-    for load in state_loads:
-        load.start()
-
+def choose_kernel(lists_near, lists_far, table_ref, picker_ref, weights_ref):
+    n_block = weights_ref.shape[0]
+    data_dev = picker_ref.shape[2] // 2
     me_y = lax.div(lax.axis_index("cell"), 4)
-    me_mem = lax.axis_index("mem")
-    me_x, me_core = lax.div(me_mem, 2), lax.rem(me_mem, 2)
-    x_at = [lax.rem(me_x - i + X, X) * Z for i in range(X)]
+    me_core = lax.rem(lax.axis_index("mem"), 2)
     y_at = [lax.rem(me_y - i + Y, Y) * Z for i in range(Y)]
 
     row = lax.broadcasted_iota(jnp.int32, (128, 128), 0)
@@ -99,22 +87,59 @@
     lists = lax.dot_general(order, lists, DN_NT, preferred_element_type=jnp.float32)
     later = pltpu.roll(lists, 127, 1)
     is_first = lax.rem(row, 8) < 4
-    columns[...] = jnp.where(is_first, lists, pltpu.roll(later, 4, 0) + data_dev)
+    ids = jnp.where(is_first, lists, pltpu.roll(later, 4, 0) + data_dev)
     prof_ids = jnp.where(is_first, pltpu.roll(lists, 124, 0), later)
 
     table = table_ref[...]
     prof_lanes = lax.broadcasted_iota(jnp.int32, (128, table.shape[0]), 1).astype(jnp.float32)
+    lanes = lax.broadcasted_iota(jnp.int32, (128, picker_ref.shape[2]), 1).astype(jnp.float32)
     for pair in range(GROUPS // 2):
-        chooser = jnp.where(prof_lanes == prof_ids[:, 2 * pair : 2 * pair + 1], 1.0, 0.0).astype(jnp.bfloat16)
+        column = slice(2 * pair, 2 * pair + 1)
+        picker_ref[pair] = jnp.where(lanes == ids[:, column], 1.0, 0.0).astype(jnp.bfloat16)
+        chooser = jnp.where(prof_lanes == prof_ids[:, column], 1.0, 0.0).astype(jnp.bfloat16)
         weight = jnp.dot(chooser, table, preferred_element_type=jnp.float32)
-        weights[:, pair * 8 : (pair + 1) * 8] = weight.reshape(n_block, 8, 128)
+        weights_ref[:, pair * 8 : (pair + 1) * 8] = weight.reshape(n_block, 8, 128)
+
+
+def choose(lists_near, lists_far, table, n_block, data_dev):
+    whole = pl.BlockSpec(memory_space=pltpu.VMEM)
+    n_slot = GROUPS * 4
+    return pl.pallas_call(
+        choose_kernel,
+        out_shape=[
+            jax.ShapeDtypeStruct((GROUPS // 2, 8 * n_block, 2 * data_dev), jnp.bfloat16),
+            jax.ShapeDtypeStruct((n_block, n_slot, 128), jnp.float32),
+        ],
+        in_specs=[whole] * 3,
+        out_specs=[whole] * 2,
+        compiler_params=pltpu.CompilerParams(vmem_limit_bytes=8 * 1024 * 1024),
+        cost_estimate=pl.CostEstimate(flops=40_000_000, bytes_accessed=2_300_000, transcendentals=0),
+        name="choose",
+    )(lists_near, lists_far, table)
+
+
+def update_kernel(*refs):
+    data = (refs[:X], refs[X : 2 * X])
+    near_hbm, far_hbm, picker_ref, weights = refs[2 * X : 2 * X + 4]
+    out_near, out_far, state, cols, state_sems = refs[2 * X + 4 :]
+    half = near_hbm.shape[0]
+    mem_dev = half // X
+    n_block = near_hbm.shape[1] // 128
+
+    state_loads = [pltpu.make_async_copy(src, state.at[i], state_sems.at[i]) for i, src in enumerate((near_hbm, far_hbm))]
+    for load in state_loads:
+        load.start()
+
+    me_y = lax.div(lax.axis_index("cell"), 4)
+    me_mem = lax.axis_index("mem")
+    me_x, me_core = lax.div(me_mem, 2), lax.rem(me_mem, 2)
+    x_at = [lax.rem(me_x - i + X, X) * Z for i in range(X)]
+    y_at = [lax.rem(me_y - i + Y, Y) * Z for i in range(Y)]
 
     def select(core):
-        lanes = lax.broadcasted_iota(jnp.int32, (128, 2 * data_dev), 1).astype(jnp.float32)
-        ids = columns[...]
         for pair in range(GROUPS // 2):
             i, q = pair // (Z // 2), pair % (Z // 2)
-            picker = jnp.where(lanes == ids[:, 2 * pair : 2 * pair + 1], 1.0, 0.0).astype(jnp.bfloat16)
+            picker = picker_ref[pair]
             for side in range(2):
 
                 def piece(s, g, a):
@@ -153,7 +178,7 @@
         out_far[:, spot] = new[half:]
 
 
-def run_update(data, near, far, lists_near, lists_far, table):
+def run_update(data, near, far, picker, weights):
     half, width = near.shape
     n_block = width // 128
     n_slot = GROUPS * 4
@@ -162,19 +187,17 @@
     return pl.pallas_call(
         update_kernel,
         out_shape=[jax.ShapeDtypeStruct(near.shape, jnp.bfloat16)] * 2,
-        in_specs=[whole] * len(data) + [any_space] * 2 + [whole] * 3,
+        in_specs=[whole] * len(data) + [any_space] * 2 + [whole] * 2,
         out_specs=[whole] * 2,
         scratch_shapes=[
             pltpu.VMEM((2,) + near.shape, jnp.bfloat16),
             pltpu.VMEM((2, n_block, n_slot, 2 * half), jnp.float32),
-            pltpu.VMEM((n_block, n_slot, 128), jnp.float32),
-            pltpu.VMEM((128, 128), jnp.float32),
             pltpu.SemaphoreType.DMA((2,)),
         ],
         compiler_params=pltpu.CompilerParams(vmem_limit_bytes=16 * 1024 * 1024),
         cost_estimate=pl.CostEstimate(flops=800_000_000, bytes_accessed=6_500_000, transcendentals=0),
         name="update",
-    )(*data, near, far, lists_near, lists_far, table)
+    )(*data, near, far, picker, weights)
 
 
 def device(x, y, z, core):
@@ -240,7 +263,8 @@
     near = lax.dynamic_slice_in_dim(state, me_core * own_cells, own_cells, 1)
     far = swap(lax.dynamic_slice_in_dim(state, (1 - me_core) * own_cells, own_cells, 1))
 
-    new_near, new_far = run_update(data_near + data_far, near, far, lists_near, lists_far, profiles)
+    picker, weights = choose(lists_near, lists_far, profiles, own_cells // 128, data_anom.shape[1])
+    new_near, new_far = run_update(data_near + data_far, near, far, picker, weights)
 
     across = slice(2 * mem_dev, 3 * mem_dev)
     near2 = to_x(new_near[across], 2)

time: 74 us -> 73.3 us (level)
  waiting for transfers between devices: 31.1 us -> 29.8 us
    ppermute x6, waiting for transfers between devices: 2.24 us -> 1.19 us  [swap(): return lax.ppermute(piece, 'mem', CORE_SWAP)]
    pallas_call x0 -> x1, Pallas kernels: none -> 1.04 us  [choose(): pl.pallas_call(choose_kernel, out_shape=[jax.ShapeDtypeStruct((GROUPS //...]
    pallas_call x1, Pallas kernels: 3.23 us -> 2.46 us  [run_update(): pl.pallas_call(update_kernel, out_shape=[jax.ShapeDtypeStruct(near.shape,...]
  transfers between devices with their start and end apart: 17 -> 17, of which waited for: 10 -> 10; matrix products, arithmetic and copies ran while one was open for 2% -> 2% of each run, Pallas kernels for 0% -> 1%
where the time goes in v6:
time: 73.3 us; the launch traced here: 72.9 us
  starting transfers between devices  34.6 us (47%)
  waiting for transfers between devices  29.8 us (41%)
  Pallas kernels  5.53 us (8%)
  local copies, waits for them, and re-layouts  2.48 us (3%)
    ppermute x7, waiting for transfers between devices, to_x(): return lax.ppermute(piece, 'mem', X_SHIFT[s % X])  22.4 us
    all_to_all x1, starting transfers between devices, local(): lax.all_to_all(sent, EVERY, 0, 0, tiled=True, axis_index_groups=PLANES)  11.9 us
    ppermute x7, starting transfers between devices, to_x(): return lax.ppermute(piece, 'mem', X_SHIFT[s % X])  9.97 us
    ppermute x6, starting transfers between devices, swap(): return lax.ppermute(piece, 'mem', CORE_SWAP)  7.84 us
    ppermute x3, waiting for transfers between devices, cross(): return lax.ppermute(piece, EVERY, CROSS[s % X])  6.3 us
    ppermute x3, starting transfers between devices, cross(): return lax.ppermute(piece, EVERY, CROSS[s % X])  4.96 us
    pallas_call x1, Pallas kernels, run_update(): pl.pallas_call(update_kernel, out_shape=[jax.ShapeDtypeStruct(near.shape,...  2.46 us
    pallas_call x1, Pallas kernels, prepare(): pl.pallas_call(prepare_kernel, out_shape=jax.ShapeDtypeStruct((GROUPS, 2...  2.03 us
  transfers between devices with their start and end apart: 17, of which 10 were waited for; matrix products, arithmetic and copies ran while one was open for 2% of the time, Pallas kernels for 1%

profile of v6, /device:TPU:1, one launch (start us, length us, event | category | flops | bytes accessed | tf_op | source)
XLA Modules:
  0.0 72.9 jit_solution(12736963349440769725)
XLA Ops:
  0.0 2.0 %prepare.1 = bf16[32,72,128]{2,1,0:T(8,128)(2,1)} custom-call(bf16[32,128]{1,0:T(8,128)(2,1)} %anom_hbm.1, bf16[32,128]{1,0:T(8,128)(2,1)} %innov_hbm.1, s32[4,4096]{1,0:T(4,128)} %seg_hbm.1, s32[4,4096]{1,0:T(4,128)} %prof_hbm.1), custom_call_target="tpu_custom_call" | custom-call | flops 10000000 | bytes 400000 | tf_op jit(solution)/shard_map/prepare/pallas_call | solution.py:54
  2.0 11.9 %all-to-all-start = ((bf16[32,72,128]{2,1,0:T(8,128)(2,1)}), bf16[32,72,128]{2,1,0:T(8,128)(2,1)S(1)}, u32[]{:S(2)}, u32[]{:S(2)}) async-start(bf16[32,72,128]{2,1,0:T(8,128)(2,1)} %prepare.1), calls=%async_computation | async-start | bytes 1179648 | tf_op jit(solution)/shard_map/all_to_all | solution.py:244
  14.0 1.3 %constant_dynamic-slice_fusion.2 = (bf16[32,4096]{1,0:T(8,128)(2,1)S(1)}, bf16[32,4096]{1,0:T(8,128)(2,1)S(1)}, bf16[32,4096]{1,0:T(8,128)(2,1)S(1)}, bf16[32,4096]{1,0:T(8,128)(2,1)S(1)}) fusion(bf16[32,32768]{1,0:T(8,128)(2,1)} %param.6, s32[]{:T(128)S(6)} %select_n.92, s32[]{:T(128)S(6)} %select_n.88, s32[]{:T(128)S(6)} %select_n.86, s32[]{:T(128)S(6)} %select_n.90), kind=kLoop, calls=%fused_computation.15 | loop fusion | bytes 2097168 | tf_op jit(solution)/shard_map/dynamic_slice | solution.py:248
  15.3 1.3 %collective-permute-start = (bf16[32,4096]{1,0:T(8,128)(2,1)S(1)}, bf16[32,4096]{1,0:T(8,128)(2,1)S(1)}, u32[]{:S(2)}, u32[]{:S(2)}) collective-permute-start(bf16[32,4096]{1,0:T(8,128)(2,1)S(1)} %get-tuple-element.25), channel_id=1, source_target_pairs={{0,4},{2,6},{4,8},{6,10},{8,12},{10,14},{12,0},{14,2},{1,5},{3,7},... | collective-permute-start | bytes 786440 | tf_op jit(solution)/shard_map/ppermute | solution.py:220
  16.6 2.4 %collective-permute-start.1 = (bf16[32,4096]{1,0:T(8,128)(2,1)S(1)}, bf16[32,4096]{1,0:T(8,128)(2,1)S(1)}, u32[]{:S(2)}, u32[]{:S(2)}) collective-permute-start(bf16[32,4096]{1,0:T(8,128)(2,1)S(1)} %get-tuple-element.24), channel_id=1, source_target_pairs={{0,8},{2,10},{4,12},{6,14},{8,0},{10,2},{12,4},{14,6},{1,9},{3,11}... | collective-permute-start | bytes 786440 | tf_op jit(solution)/shard_map/ppermute | solution.py:220
  19.0 1.1 %collective-permute-start.2 = (bf16[32,4096]{1,0:T(8,128)(2,1)S(1)}, bf16[32,4096]{1,0:T(8,128)(2,1)S(1)}, u32[]{:S(2)}, u32[]{:S(2)}) collective-permute-start(bf16[32,4096]{1,0:T(8,128)(2,1)S(1)} %get-tuple-element.26), channel_id=1, source_target_pairs={{0,12},{2,14},{4,0},{6,2},{8,4},{10,6},{12,8},{14,10},{1,13},{3,15... | collective-permute-start | bytes 786440 | tf_op jit(solution)/shard_map/ppermute | solution.py:220
  20.2 5.3 %collective-permute-done = bf16[32,4096]{1,0:T(8,128)(2,1)S(1)} collective-permute-done((bf16[32,4096]{1,0:T(8,128)(2,1)S(1)}, bf16[32,4096]{1,0:T(8,128)(2,1)S(1)}, u32[]{:S(2)}, u32[]{:S(2)}) %collective-permute-start) | collective-permute-done | bytes 262176 | tf_op jit(solution)/shard_map/ppermute | solution.py:220
  25.5 7.5 %collective-permute-done.1 = bf16[32,4096]{1,0:T(8,128)(2,1)S(1)} collective-permute-done((bf16[32,4096]{1,0:T(8,128)(2,1)S(1)}, bf16[32,4096]{1,0:T(8,128)(2,1)S(1)}, u32[]{:S(2)}, u32[]{:S(2)}) %collective-permute-start.1) | collective-permute-done | bytes 262176 | tf_op jit(solution)/shard_map/ppermute | solution.py:220
  33.0 0.0 collective-permute-done.2
  33.0 0.0 all-to-all-done.refs_0_
  33.0 0.1 slice.24
  33.1 1.2 %collective-permute-start.3 = (bf16[32,64,128]{2,1,0:T(8,128)(2,1)S(1)}, bf16[32,64,128]{2,1,0:T(8,128)(2,1)S(1)}, u32[]{:S(2)}, u32[]{:S(2)}) collective-permute-start(bf16[32,64,128]{2,1,0:T(8,128)(2,1)S(1)} %slice.24), channel_id=1, source_target_pairs={{0,4},{1,5},{16,20},{17,21},{32,36},{33,37},{48,52},{49,53},{64,68... | collective-permute-start | bytes 1572872 | tf_op jit(solution)/shard_map/ppermute | solution.py:224
  34.2 2.8 %collective-permute-start.4 = (bf16[32,64,128]{2,1,0:T(8,128)(2,1)S(1)}, bf16[32,64,128]{2,1,0:T(8,128)(2,1)S(1)}, u32[]{:S(2)}, u32[]{:S(2)}) collective-permute-start(bf16[32,64,128]{2,1,0:T(8,128)(2,1)S(1)} %slice.24), channel_id=1, source_target_pairs={{0,8},{1,9},{16,24},{17,25},{32,40},{33,41},{48,56},{49,57},{64,72... | collective-permute-start | bytes 1572872 | tf_op jit(solution)/shard_map/ppermute | solution.py:224
  37.0 1.0 %collective-permute-start.5 = (bf16[32,64,128]{2,1,0:T(8,128)(2,1)S(1)}, bf16[32,64,128]{2,1,0:T(8,128)(2,1)S(1)}, u32[]{:S(2)}, u32[]{:S(2)}) collective-permute-start(bf16[32,64,128]{2,1,0:T(8,128)(2,1)S(1)} %slice.24), channel_id=1, source_target_pairs={{0,12},{1,13},{16,28},{17,29},{32,44},{33,45},{48,60},{49,61},{64,... | collective-permute-start | bytes 1572872 | tf_op jit(solution)/shard_map/ppermute | solution.py:224
  38.0 2.4 %collective-permute-start.6 = (bf16[32,72,128]{2,1,0:T(8,128)(2,1)S(1)}, bf16[32,72,128]{2,1,0:T(8,128)(2,1)S(1)}, u32[]{:S(2)}, u32[]{:S(2)}) collective-permute-start(bf16[32,72,128]{2,1,0:T(8,128)(2,1)S(1)} %all-to-all-done.refs_0_), channel_id=1, source_target_pairs={{0,2},{2,0},{4,6},{6,4},{8,10},{10,8},{12,14},{14,12},{1,3},{3,1},... | collective-permute-start | bytes 1769480 | tf_op jit(solution)/shard_map/ppermute | solution.py:232
  40.4 2.3 %collective-permute-done.3.refs_1_ = bf16[32,64,128]{2,1,0:T(8,128)(2,1)S(1)} collective-permute-done((bf16[32,64,128]{2,1,0:T(8,128)(2,1)S(1)}, bf16[32,64,128]{2,1,0:T(8,128)(2,1)S(1)}, u32[]{:S(2)}, u32[]{:S(2)}) %collective-permute-start.3) | collective-permute-done | bytes 524320 | tf_op jit(solution)/shard_map/ppermute | solution.py:224
  42.7 0.0 copy-start
  42.8 0.1 constant_dynamic-slice_fusion
  42.9 2.4 %collective-permute-start.10 = (bf16[128,2048]{1,0:T(8,128)(2,1)S(1)}, bf16[128,2048]{1,0:T(8,128)(2,1)S(1)}, u32[]{:S(2)}, u32[]{:S(2)}) collective-permute-start(bf16[128,2048]{1,0:T(8,128)(2,1)S(1)} %get-tuple-element.32), channel_id=1, source_target_pairs={{0,2},{2,0},{4,6},{6,4},{8,10},{10,8},{12,14},{14,12},{1,3},{3,1},... | collective-permute-start | bytes 1572872 | tf_op jit(solution)/shard_map/ppermute | solution.py:232
  45.4 0.1 collective-permute-start.7
  45.5 4.0 %collective-permute-done.4.refs_2_ = bf16[32,64,128]{2,1,0:T(8,128)(2,1)S(1)} collective-permute-done((bf16[32,64,128]{2,1,0:T(8,128)(2,1)S(1)}, bf16[32,64,128]{2,1,0:T(8,128)(2,1)S(1)}, u32[]{:S(2)}, u32[]{:S(2)}) %collective-permute-start.4) | collective-permute-done | bytes 524320 | tf_op jit(solution)/shard_map/ppermute | solution.py:224
  49.5 2.3 %collective-permute-start.8 = (bf16[32,64,128]{2,1,0:T(8,128)(2,1)S(1)}, bf16[32,64,128]{2,1,0:T(8,128)(2,1)S(1)}, u32[]{:S(2)}, u32[]{:S(2)}) collective-permute-start(bf16[32,64,128]{2,1,0:T(8,128)(2,1)S(1)} %collective-permute-done.4.refs_2_), channel_id=1, source_target_pairs={{0,2},{2,0},{4,6},{6,4},{8,10},{10,8},{12,14},{14,12},{1,3},{3,1},... | collective-permute-start | bytes 1572872 | tf_op jit(solution)/shard_map/ppermute | solution.py:232
  51.8 0.0 collective-permute-done.5.refs_3_
  51.8 0.0 collective-permute-start.9
  51.8 0.0 collective-permute-done.6.refs_4_
  51.8 0.0 copy-done
  51.8 1.0 %choose.1 = (bf16[16,128,256]{2,1,0:T(8,128)(2,1)S(1)}, f32[16,128,128]{2,1,0:T(8,128)S(1)}) custom-call(bf16[32,8,128]{2,1,0:T(8,128)(2,1)S(1)} %slice.32.lists_near, bf16[32,8,128]{2,1,0:T(8,128)(2,1)S(1)} %slice.33.lists_far, bf16[64,128]{1,0:T(8,128)(2,1)S(1)} %copy-done), custom_call_target="tpu_custom_call" | custom-call | flops 40000000 | bytes 2300000 | tf_op jit(solution)/shard_map/choose/pallas_call | solution.py:107
  52.9 0.0 collective-permute-done.10.refs_9_
  52.9 0.0 collective-permute-done.7.refs_5_
  52.9 0.4 collective-permute-done.8.refs_6_
  53.3 0.7 %collective-permute-done.9.refs_7_ = bf16[32,64,128]{2,1,0:T(8,128)(2,1)S(1)} collective-permute-done((bf16[32,64,128]{2,1,0:T(8,128)(2,1)S(1)}, bf16[32,64,128]{2,1,0:T(8,128)(2,1)S(1)}, u32[]{:S(2)}, u32[]{:S(2)}) %collective-permute-start.9) | collective-permute-done | bytes 524320 | tf_op jit(solution)/shard_map/ppermute | solution.py:232
  54.0 2.5 %update.1 = (bf16[128,2048]{1,0:T(8,128)(2,1)S(1)}, bf16[128,2048]{1,0:T(8,128)(2,1)S(1)}) custom-call(bf16[32,72,128]{2,1,0:T(8,128)(2,1)S(1)} %all-to-all-done.refs_0_, bf16[32,64,128]{2,1,0:T(8,128)(2,1)S(1)} %collective-permute-done.3.refs_1_, bf16[32,64,128]{2,1,0:T(8,128)(2,1)S(1)} %collective-permute-done.4.refs_2_, ...), custom_call_target="tpu_custom_call" | custom-call | flops 800000000 | bytes 6500000 | tf_op jit(solution)/shard_map/update/pallas_call | solution.py:187
  56.5 0.6 collective-permute-start.11
  57.2 2.0 %collective-permute-start.12 = (bf16[32,2048]{1,0:T(8,128)(2,1)S(1)}, bf16[32,2048]{1,0:T(8,128)(2,1)S(1)}, u32[]{:S(2)}, u32[]{:S(2)}) collective-permute-start(bf16[32,2048]{1,0:T(8,128)(2,1)S(1)} %slice.28), channel_id=1, source_target_pairs={{0,8},{2,10},{4,12},{6,14},{8,0},{10,2},{12,4},{14,6},{1,9},{3,11}... | collective-permute-start | bytes 393224 | tf_op jit(solution)/shard_map/ppermute | solution.py:220
  59.2 0.0 collective-permute-done.11
  59.2 1.5 %collective-permute-start.13 = (bf16[32,2048]{1,0:T(8,128)(2,1)S(1)}, bf16[32,2048]{1,0:T(8,128)(2,1)S(1)}, u32[]{:S(2)}, u32[]{:S(2)}) collective-permute-start(bf16[32,2048]{1,0:T(8,128)(2,1)S(1)} %slice.34), channel_id=1, source_target_pairs={{0,8},{2,10},{4,12},{6,14},{8,0},{10,2},{12,4},{14,6},{1,9},{3,11}... | collective-permute-start | bytes 393224 | tf_op jit(solution)/shard_map/ppermute | solution.py:220
  60.7 0.1 broadcast_select_fusion.1
  60.8 0.1 broadcast_in_dim.3
  60.9 0.1 pad_maximum_fusion
  60.9 1.3 %collective-permute-start.14 = (bf16[32,4096]{1,0:T(8,128)(2,1)S(1)}, bf16[32,4096]{1,0:T(8,128)(2,1)S(1)}, u32[]{:S(2)}, u32[]{:S(2)}) collective-permute-start(bf16[32,4096]{1,0:T(8,128)(2,1)S(1)} %get-tuple-element.28), channel_id=1, source_target_pairs={{0,12},{2,14},{4,0},{6,2},{8,4},{10,6},{12,8},{14,10},{1,13},{3,15... | collective-permute-start | bytes 786440 | tf_op jit(solution)/shard_map/ppermute | solution.py:220
  62.3 0.2 collective-permute-start.15
  62.5 1.2 %collective-permute-done.12 = bf16[32,2048]{1,0:T(8,128)(2,1)S(1)} collective-permute-done((bf16[32,2048]{1,0:T(8,128)(2,1)S(1)}, bf16[32,2048]{1,0:T(8,128)(2,1)S(1)}, u32[]{:S(2)}, u32[]{:S(2)}) %collective-permute-start.12) | collective-permute-done | bytes 131104 | tf_op jit(solution)/shard_map/ppermute | solution.py:220
  63.7 2.8 %collective-permute-done.13 = bf16[32,2048]{1,0:T(8,128)(2,1)S(1)} collective-permute-done((bf16[32,2048]{1,0:T(8,128)(2,1)S(1)}, bf16[32,2048]{1,0:T(8,128)(2,1)S(1)}, u32[]{:S(2)}, u32[]{:S(2)}) %collective-permute-start.13) | collective-permute-done | bytes 131104 | tf_op jit(solution)/shard_map/ppermute | solution.py:220
  66.5 4.7 %collective-permute-done.14 = bf16[32,4096]{1,0:T(8,128)(2,1)S(1)} collective-permute-done((bf16[32,4096]{1,0:T(8,128)(2,1)S(1)}, bf16[32,4096]{1,0:T(8,128)(2,1)S(1)}, u32[]{:S(2)}, u32[]{:S(2)}) %collective-permute-start.14) | collective-permute-done | bytes 262176 | tf_op jit(solution)/shard_map/ppermute | solution.py:220
  71.2 0.0 copy-start.1
  71.2 0.9 %collective-permute-done.15 = bf16[32,4096]{1,0:T(8,128)(2,1)S(1)} collective-permute-done((bf16[32,4096]{1,0:T(8,128)(2,1)S(1)}, bf16[32,4096]{1,0:T(8,128)(2,1)S(1)}, u32[]{:S(2)}, u32[]{:S(2)}) %collective-permute-start.15) | collective-permute-done | bytes 262176 | tf_op jit(solution)/shard_map/ppermute | solution.py:220
  72.1 0.1 copy-done.1
  72.2 0.7 constant_dynamic-update-slice_fusion.4
  (11 shorter events, 0.2 us)
Async XLA Ops:
  2.0 31.0 %all-to-all-start = ((bf16[32,72,128]{2,1,0:T(8,128)(2,1)}), bf16[32,72,128]{2,1,0:T(8,128)(2,1)S(1)}, u32[]{:S(2)}, u32[]{:S(2)}) async-start(bf16[32,72,128]{2,1,0:T(8,128)(2,1)} %prepare.1), calls=%async_computation | async-start | bytes 1179648 | tf_op jit(solution)/shard_map/all_to_all | solution.py:244
  15.3 10.2 %collective-permute-start = (bf16[32,4096]{1,0:T(8,128)(2,1)S(1)}, bf16[32,4096]{1,0:T(8,128)(2,1)S(1)}, u32[]{:S(2)}, u32[]{:S(2)}) collective-permute-start(bf16[32,4096]{1,0:T(8,128)(2,1)S(1)} %get-tuple-element.25), channel_id=1, source_target_pairs={{0,4},{2,6},{4,8},{6,10},{8,12},{10,14},{12,0},{14,2},{1,5},{3,7},... | collective-permute-start | bytes 786440 | tf_op jit(solution)/shard_map/ppermute | solution.py:220
  16.6 16.4 %collective-permute-start.1 = (bf16[32,4096]{1,0:T(8,128)(2,1)S(1)}, bf16[32,4096]{1,0:T(8,128)(2,1)S(1)}, u32[]{:S(2)}, u32[]{:S(2)}) collective-permute-start(bf16[32,4096]{1,0:T(8,128)(2,1)S(1)} %get-tuple-element.24), channel_id=1, source_target_pairs={{0,8},{2,10},{4,12},{6,14},{8,0},{10,2},{12,4},{14,6},{1,9},{3,11}... | collective-permute-start | bytes 786440 | tf_op jit(solution)/shard_map/ppermute | solution.py:220
  19.0 13.9 %collective-permute-start.2 = (bf16[32,4096]{1,0:T(8,128)(2,1)S(1)}, bf16[32,4096]{1,0:T(8,128)(2,1)S(1)}, u32[]{:S(2)}, u32[]{:S(2)}) collective-permute-start(bf16[32,4096]{1,0:T(8,128)(2,1)S(1)} %get-tuple-element.26), channel_id=1, source_target_pairs={{0,12},{2,14},{4,0},{6,2},{8,4},{10,6},{12,8},{14,10},{1,13},{3,15... | collective-permute-start | bytes 786440 | tf_op jit(solution)/shard_map/ppermute | solution.py:220
  33.1 9.7 %collective-permute-start.3 = (bf16[32,64,128]{2,1,0:T(8,128)(2,1)S(1)}, bf16[32,64,128]{2,1,0:T(8,128)(2,1)S(1)}, u32[]{:S(2)}, u32[]{:S(2)}) collective-permute-start(bf16[32,64,128]{2,1,0:T(8,128)(2,1)S(1)} %slice.24), channel_id=1, source_target_pairs={{0,4},{1,5},{16,20},{17,21},{32,36},{33,37},{48,52},{49,53},{64,68... | collective-permute-start | bytes 1572872 | tf_op jit(solution)/shard_map/ppermute | solution.py:224
  34.2 15.3 %collective-permute-start.4 = (bf16[32,64,128]{2,1,0:T(8,128)(2,1)S(1)}, bf16[32,64,128]{2,1,0:T(8,128)(2,1)S(1)}, u32[]{:S(2)}, u32[]{:S(2)}) collective-permute-start(bf16[32,64,128]{2,1,0:T(8,128)(2,1)S(1)} %slice.24), channel_id=1, source_target_pairs={{0,8},{1,9},{16,24},{17,25},{32,40},{33,41},{48,56},{49,57},{64,72... | collective-permute-start | bytes 1572872 | tf_op jit(solution)/shard_map/ppermute | solution.py:224
  37.0 14.7 %collective-permute-start.5 = (bf16[32,64,128]{2,1,0:T(8,128)(2,1)S(1)}, bf16[32,64,128]{2,1,0:T(8,128)(2,1)S(1)}, u32[]{:S(2)}, u32[]{:S(2)}) collective-permute-start(bf16[32,64,128]{2,1,0:T(8,128)(2,1)S(1)} %slice.24), channel_id=1, source_target_pairs={{0,12},{1,13},{16,28},{17,29},{32,44},{33,45},{48,60},{49,61},{64,... | collective-permute-start | bytes 1572872 | tf_op jit(solution)/shard_map/ppermute | solution.py:224
  38.0 13.8 %collective-permute-start.6 = (bf16[32,72,128]{2,1,0:T(8,128)(2,1)S(1)}, bf16[32,72,128]{2,1,0:T(8,128)(2,1)S(1)}, u32[]{:S(2)}, u32[]{:S(2)}) collective-permute-start(bf16[32,72,128]{2,1,0:T(8,128)(2,1)S(1)} %all-to-all-done.refs_0_), channel_id=1, source_target_pairs={{0,2},{2,0},{4,6},{6,4},{8,10},{10,8},{12,14},{14,12},{1,3},{3,1},... | collective-permute-start | bytes 1769480 | tf_op jit(solution)/shard_map/ppermute | solution.py:232
  42.7 9.1 %copy-start = (bf16[64,128]{1,0:T(8,128)(2,1)S(1)}, bf16[64,128]{1,0:T(8,128)(2,1)}, u32[]{:S(2)}) copy-start(bf16[64,128]{1,0:T(8,128)(2,1)} %table_ref.1) | copy-start | bytes 49156
  42.9 9.9 %collective-permute-start.10 = (bf16[128,2048]{1,0:T(8,128)(2,1)S(1)}, bf16[128,2048]{1,0:T(8,128)(2,1)S(1)}, u32[]{:S(2)}, u32[]{:S(2)}) collective-permute-start(bf16[128,2048]{1,0:T(8,128)(2,1)S(1)} %get-tuple-element.32), channel_id=1, source_target_pairs={{0,2},{2,0},{4,6},{6,4},{8,10},{10,8},{12,14},{14,12},{1,3},{3,1},... | collective-permute-start | bytes 1572872 | tf_op jit(solution)/shard_map/ppermute | solution.py:232
  45.4 7.5 %collective-permute-start.7 = (bf16[32,64,128]{2,1,0:T(8,128)(2,1)S(1)}, bf16[32,64,128]{2,1,0:T(8,128)(2,1)S(1)}, u32[]{:S(2)}, u32[]{:S(2)}) collective-permute-start(bf16[32,64,128]{2,1,0:T(8,128)(2,1)S(1)} %collective-permute-done.3.refs_1_), channel_id=1, source_target_pairs={{0,2},{2,0},{4,6},{6,4},{8,10},{10,8},{12,14},{14,12},{1,3},{3,1},... | collective-permute-start | bytes 1572872 | tf_op jit(solution)/shard_map/ppermute | solution.py:232
  49.5 3.8 %collective-permute-start.8 = (bf16[32,64,128]{2,1,0:T(8,128)(2,1)S(1)}, bf16[32,64,128]{2,1,0:T(8,128)(2,1)S(1)}, u32[]{:S(2)}, u32[]{:S(2)}) collective-permute-start(bf16[32,64,128]{2,1,0:T(8,128)(2,1)S(1)} %collective-permute-done.4.refs_2_), channel_id=1, source_target_pairs={{0,2},{2,0},{4,6},{6,4},{8,10},{10,8},{12,14},{14,12},{1,3},{3,1},... | collective-permute-start | bytes 1572872 | tf_op jit(solution)/shard_map/ppermute | solution.py:232
  51.8 2.3 %collective-permute-start.9 = (bf16[32,64,128]{2,1,0:T(8,128)(2,1)S(1)}, bf16[32,64,128]{2,1,0:T(8,128)(2,1)S(1)}, u32[]{:S(2)}, u32[]{:S(2)}) collective-permute-start(bf16[32,64,128]{2,1,0:T(8,128)(2,1)S(1)} %collective-permute-done.5.refs_3_), channel_id=1, source_target_pairs={{0,2},{2,0},{4,6},{6,4},{8,10},{10,8},{12,14},{14,12},{1,3},{3,1},... | collective-permute-start | bytes 1572872 | tf_op jit(solution)/shard_map/ppermute | solution.py:232
  56.5 2.7 %collective-permute-start.11 = (bf16[128,2048]{1,0:T(8,128)(2,1)S(1)}, bf16[128,2048]{1,0:T(8,128)(2,1)S(1)}, u32[]{:S(2)}, u32[]{:S(2)}) collective-permute-start(bf16[128,2048]{1,0:T(8,128)(2,1)S(1)} %get-tuple-element.22), channel_id=1, source_target_pairs={{0,2},{2,0},{4,6},{6,4},{8,10},{10,8},{12,14},{14,12},{1,3},{3,1},... | collective-permute-start | bytes 1572872 | tf_op jit(solution)/shard_map/ppermute | solution.py:232
  57.2 6.5 %collective-permute-start.12 = (bf16[32,2048]{1,0:T(8,128)(2,1)S(1)}, bf16[32,2048]{1,0:T(8,128)(2,1)S(1)}, u32[]{:S(2)}, u32[]{:S(2)}) collective-permute-start(bf16[32,2048]{1,0:T(8,128)(2,1)S(1)} %slice.28), channel_id=1, source_target_pairs={{0,8},{2,10},{4,12},{6,14},{8,0},{10,2},{12,4},{14,6},{1,9},{3,11}... | collective-permute-start | bytes 393224 | tf_op jit(solution)/shard_map/ppermute | solution.py:220
  59.2 7.3 %collective-permute-start.13 = (bf16[32,2048]{1,0:T(8,128)(2,1)S(1)}, bf16[32,2048]{1,0:T(8,128)(2,1)S(1)}, u32[]{:S(2)}, u32[]{:S(2)}) collective-permute-start(bf16[32,2048]{1,0:T(8,128)(2,1)S(1)} %slice.34), channel_id=1, source_target_pairs={{0,8},{2,10},{4,12},{6,14},{8,0},{10,2},{12,4},{14,6},{1,9},{3,11}... | collective-permute-start | bytes 393224 | tf_op jit(solution)/shard_map/ppermute | solution.py:220
  60.9 10.3 %collective-permute-start.14 = (bf16[32,4096]{1,0:T(8,128)(2,1)S(1)}, bf16[32,4096]{1,0:T(8,128)(2,1)S(1)}, u32[]{:S(2)}, u32[]{:S(2)}) collective-permute-start(bf16[32,4096]{1,0:T(8,128)(2,1)S(1)} %get-tuple-element.28), channel_id=1, source_target_pairs={{0,12},{2,14},{4,0},{6,2},{8,4},{10,6},{12,8},{14,10},{1,13},{3,15... | collective-permute-start | bytes 786440 | tf_op jit(solution)/shard_map/ppermute | solution.py:220
  62.3 9.8 %collective-permute-start.15 = (bf16[32,4096]{1,0:T(8,128)(2,1)S(1)}, bf16[32,4096]{1,0:T(8,128)(2,1)S(1)}, u32[]{:S(2)}, u32[]{:S(2)}) collective-permute-start(bf16[32,4096]{1,0:T(8,128)(2,1)S(1)} %get-tuple-element.27), channel_id=1, source_target_pairs={{0,4},{2,6},{4,8},{6,10},{8,12},{10,14},{12,0},{14,2},{1,5},{3,7},... | collective-permute-start | bytes 786440 | tf_op jit(solution)/shard_map/ppermute | solution.py:220
  71.2 1.0 %copy-start.1 = (bf16[32,16384]{1,0:T(8,128)(2,1)}, bf16[32,16384]{1,0:T(8,128)(2,1)S(1)}, u32[]{:S(2)}) copy-start(bf16[32,16384]{1,0:T(8,128)(2,1)S(1)} %constant_dynamic-update-slice_fusion.5) | copy-start | bytes 3145732

commit v7 on v6

--- a/solution.py
+++ b/solution.py
@@ -118,58 +118,73 @@
     )(lists_near, lists_far, table)
 
 
-def update_kernel(*refs):
-    data = (refs[:X], refs[X : 2 * X])
-    near_hbm, far_hbm, picker_ref, weights = refs[2 * X : 2 * X + 4]
-    out_near, out_far, state, cols, state_sems = refs[2 * X + 4 :]
-    half = near_hbm.shape[0]
-    mem_dev = half // X
-    n_block = near_hbm.shape[1] // 128
-
-    state_loads = [pltpu.make_async_copy(src, state.at[i], state_sems.at[i]) for i, src in enumerate((near_hbm, far_hbm))]
-    for load in state_loads:
-        load.start()
-
+def select_columns(data, side, picker_ref, cols):
+    mem_dev = data[1].shape[1] // 2
+    half = X * mem_dev
+    n_block = cols.shape[1]
     me_y = lax.div(lax.axis_index("cell"), 4)
     me_mem = lax.axis_index("mem")
     me_x, me_core = lax.div(me_mem, 2), lax.rem(me_mem, 2)
     x_at = [lax.rem(me_x - i + X, X) * Z for i in range(X)]
     y_at = [lax.rem(me_y - i + Y, Y) * Z for i in range(Y)]
 
-    def select(core):
+    def select(over_x):
         for pair in range(GROUPS // 2):
             i, q = pair // (Z // 2), pair % (Z // 2)
-            picker = picker_ref[pair]
-            for side in range(2):
-
-                def piece(s, g, a):
-                    rows = slice(a * mem_dev, (a + 1) * mem_dev)
-                    if side == core:
-                        return data[side][s][y_at[i] + 2 * q + g, rows]
-                    return data[side][i][x_at[s] + 2 * q + g, rows]
-
-                values = jnp.concatenate(
-                    [
-                        jnp.concatenate([piece(s, g, a) for a in range(2) for s in range(X)], axis=0)
-                        for g in range(2)
-                    ],
-                    axis=1,
-                )
-                picked = lax.dot_general(picker, values, DN_NT, preferred_element_type=jnp.float32)
-                picked = picked.reshape(n_block, 8, 2 * half)
-                for a in range(2):
-                    cols[a, :, pair * 8 : (pair + 1) * 8, side * half : (side + 1) * half] = picked[:, :, a * half : (a + 1) * half]
-
-    for core in range(2):
-        pl.when(me_core == core)(lambda core=core: select(core))
+
+            def piece(s, g, a):
+                rows = slice(a * mem_dev, (a + 1) * mem_dev)
+                if over_x:
+                    return data[s][y_at[i] + 2 * q + g, rows]
+                return data[i][x_at[s] + 2 * q + g, rows]
+
+            values = jnp.concatenate(
+                [jnp.concatenate([piece(s, g, a) for a in range(2) for s in range(X)], axis=0) for g in range(2)],
+                axis=1,
+            )
+            picked = lax.dot_general(picker_ref[pair], values, DN_NT, preferred_element_type=jnp.float32)
+            picked = picked.reshape(n_block, 8, 2 * half)
+            for a in range(2):
+                cols[a, :, pair * 8 : (pair + 1) * 8] = picked[:, :, a * half : (a + 1) * half]
+
+    pl.when(me_core == side)(lambda: select(True))
+    pl.when(me_core != side)(lambda: select(False))
+
+
+def near_kernel(*refs):
+    select_columns(refs[:X], 0, refs[X], refs[X + 1])
+
+
+def select_near(data, picker, two_m, n_block):
+    whole = pl.BlockSpec(memory_space=pltpu.VMEM)
+    return pl.pallas_call(
+        near_kernel,
+        out_shape=jax.ShapeDtypeStruct((2, n_block, GROUPS * 4, X * two_m // 2), jnp.float32),
+        in_specs=[whole] * (X + 1),
+        out_specs=whole,
+        compiler_params=pltpu.CompilerParams(vmem_limit_bytes=8 * 1024 * 1024),
+        cost_estimate=pl.CostEstimate(flops=270_000_000, bytes_accessed=5_300_000, transcendentals=0),
+        name="select_near",
+    )(*data, picker)
+
+
+def update_kernel(*refs):
+    near_hbm, far_hbm, picker_ref, weights, cols_near = refs[X : X + 5]
+    out_near, out_far, state, cols, state_sems = refs[X + 5 :]
+    half = near_hbm.shape[0]
+    n_block = near_hbm.shape[1] // 128
+
+    state_loads = [pltpu.make_async_copy(src, state.at[i], state_sems.at[i]) for i, src in enumerate((near_hbm, far_hbm))]
+    for load in state_loads:
+        load.start()
+    select_columns(refs[:X], 1, picker_ref, cols)
 
     for load in state_loads:
         load.wait()
     for b in range(n_block):
         spot = pl.ds(b * 128, 128)
         own = jnp.concatenate([state[0, :, spot], state[1, :, spot]], axis=0)
-        anom = cols[0, b].astype(jnp.bfloat16)
-        innov = cols[1, b].astype(jnp.bfloat16)
+        anom, innov = (jnp.concatenate([cols_near[a, b], cols[a, b]], axis=1).astype(jnp.bfloat16) for a in range(2))
         inner = jnp.dot(anom, own, preferred_element_type=jnp.float32)
         coef = (weights[b] * inner / (M - 1)).astype(jnp.bfloat16)
         corr = lax.dot_general(innov, coef, DN_TN, preferred_element_type=jnp.float32)
@@ -178,7 +193,7 @@
         out_far[:, spot] = new[half:]
 
 
-def run_update(data, near, far, picker, weights):
+def run_update(data, near, far, picker, weights, cols_near):
     half, width = near.shape
     n_block = width // 128
     n_slot = GROUPS * 4
@@ -187,17 +202,17 @@
     return pl.pallas_call(
         update_kernel,
         out_shape=[jax.ShapeDtypeStruct(near.shape, jnp.bfloat16)] * 2,
-        in_specs=[whole] * len(data) + [any_space] * 2 + [whole] * 2,
+        in_specs=[whole] * len(data) + [any_space] * 2 + [whole] * 3,
         out_specs=[whole] * 2,
         scratch_shapes=[
             pltpu.VMEM((2,) + near.shape, jnp.bfloat16),
-            pltpu.VMEM((2, n_block, n_slot, 2 * half), jnp.float32),
+            pltpu.VMEM((2, n_block, n_slot, half), jnp.float32),
             pltpu.SemaphoreType.DMA((2,)),
         ],
         compiler_params=pltpu.CompilerParams(vmem_limit_bytes=16 * 1024 * 1024),
         cost_estimate=pl.CostEstimate(flops=800_000_000, bytes_accessed=6_500_000, transcendentals=0),
         name="update",
-    )(*data, near, far, picker, weights)
+    )(*data, near, far, picker, weights, cols_near)
 
 
 def device(x, y, z, core):
@@ -255,16 +270,17 @@
     data_near = [got] + [None] * 3
     for s in (2, 1, 3):
         data_near[s] = cross(own, s)
-    data_far = [swap(d) for d in data_near]
     first = me_core == 0
-    lists_near, lists_far = got[:, data_rows:], data_far[0][:, data_rows:]
+    far_got = swap(got)
+    picker, weights = choose(got[:, data_rows:], far_got[:, data_rows:], profiles, own_cells // 128, data_anom.shape[1])
+    data_far = [far_got] + [swap(data_near[1]), swap(data_near[2]), swap(data_near[3])]
 
     state = jnp.concatenate(after(pieces, data_near[1]), axis=0)
     near = lax.dynamic_slice_in_dim(state, me_core * own_cells, own_cells, 1)
     far = swap(lax.dynamic_slice_in_dim(state, (1 - me_core) * own_cells, own_cells, 1))
 
-    picker, weights = choose(lists_near, lists_far, profiles, own_cells // 128, data_anom.shape[1])
-    new_near, new_far = run_update(data_near + data_far, near, far, picker, weights)
+    cols_near = select_near(data_near, picker, data_rows, own_cells // 128)
+    new_near, new_far = run_update(data_far, near, far, picker, weights, cols_near)
 
     across = slice(2 * mem_dev, 3 * mem_dev)
     near2 = to_x(new_near[across], 2)

time: 73.3 us -> 72.7 us (level)
  waiting for transfers between devices: 29.8 us -> 28.5 us
    ppermute x6, waiting for transfers between devices: 1.19 us -> 0.35 us  [swap(): return lax.ppermute(piece, 'mem', CORE_SWAP)]
    pallas_call x0 -> x1, Pallas kernels: none -> 0.82 us  [select_near(): pl.pallas_call(near_kernel, out_shape=jax.ShapeDtypeStruct((2, n_block, G...]
  transfers between devices with their start and end apart: 17 -> 17, of which waited for: 10 -> 9; matrix products, arithmetic and copies ran while one was open for 2% -> 2% of each run, Pallas kernels for 1% -> 3%
where the time goes in v7:
time: 72.7 us; the launch traced here: 72 us
  starting transfers between devices  35.1 us (48%)
  waiting for transfers between devices  28.5 us (39%)
  Pallas kernels  5.64 us (8%)
  local copies, waits for them, and re-layouts  2.4 us (3%)
    ppermute x7, waiting for transfers between devices, to_x(): return lax.ppermute(piece, 'mem', X_SHIFT[s % X])  21.9 us
    all_to_all x1, starting transfers between devices, local(): lax.all_to_all(sent, EVERY, 0, 0, tiled=True, axis_index_groups=PLANES)  11.9 us
    ppermute x7, starting transfers between devices, to_x(): return lax.ppermute(piece, 'mem', X_SHIFT[s % X])  10.4 us
    ppermute x6, starting transfers between devices, swap(): return lax.ppermute(piece, 'mem', CORE_SWAP)  7.85 us
    ppermute x3, waiting for transfers between devices, cross(): return lax.ppermute(piece, EVERY, CROSS[s % X])  6.3 us
    ppermute x3, starting transfers between devices, cross(): return lax.ppermute(piece, EVERY, CROSS[s % X])  4.96 us
    pallas_call x1, Pallas kernels, prepare(): pl.pallas_call(prepare_kernel, out_shape=jax.ShapeDtypeStruct((GROUPS, 2...  2.03 us
    pallas_call x1, Pallas kernels, run_update(): pl.pallas_call(update_kernel, out_shape=[jax.ShapeDtypeStruct(near.shape,...  1.75 us
  transfers between devices with their start and end apart: 17, of which 9 were waited for; matrix products, arithmetic and copies ran while one was open for 2% of the time, Pallas kernels for 3%

profile of v7, /device:TPU:1, one launch (start us, length us, event | category | flops | bytes accessed | tf_op | source)
XLA Modules:
  0.0 72.0 jit_solution(5722730190451389989)
XLA Ops:
  0.0 2.0 %prepare.1 = bf16[32,72,128]{2,1,0:T(8,128)(2,1)} custom-call(bf16[32,128]{1,0:T(8,128)(2,1)} %anom_hbm.1, bf16[32,128]{1,0:T(8,128)(2,1)} %innov_hbm.1, s32[4,4096]{1,0:T(4,128)} %seg_hbm.1, s32[4,4096]{1,0:T(4,128)} %prof_hbm.1), custom_call_target="tpu_custom_call" | custom-call | flops 10000000 | bytes 400000 | tf_op jit(solution)/shard_map/prepare/pallas_call | solution.py:54
  2.0 11.9 %all-to-all-start = ((bf16[32,72,128]{2,1,0:T(8,128)(2,1)}), bf16[32,72,128]{2,1,0:T(8,128)(2,1)S(1)}, u32[]{:S(2)}, u32[]{:S(2)}) async-start(bf16[32,72,128]{2,1,0:T(8,128)(2,1)} %prepare.1), calls=%async_computation | async-start | bytes 1179648 | tf_op jit(solution)/shard_map/all_to_all | solution.py:259
  14.0 1.3 %constant_dynamic-slice_fusion.2 = (bf16[32,4096]{1,0:T(8,128)(2,1)S(1)}, bf16[32,4096]{1,0:T(8,128)(2,1)S(1)}, bf16[32,4096]{1,0:T(8,128)(2,1)S(1)}, bf16[32,4096]{1,0:T(8,128)(2,1)S(1)}) fusion(bf16[32,32768]{1,0:T(8,128)(2,1)} %param.6, s32[]{:T(128)S(6)} %select_n.92, s32[]{:T(128)S(6)} %select_n.88, s32[]{:T(128)S(6)} %select_n.86, s32[]{:T(128)S(6)} %select_n.90), kind=kLoop, calls=%fused_computation.15 | loop fusion | bytes 2097168 | tf_op jit(solution)/shard_map/dynamic_slice | solution.py:263
  15.3 1.3 %collective-permute-start.1 = (bf16[32,4096]{1,0:T(8,128)(2,1)S(1)}, bf16[32,4096]{1,0:T(8,128)(2,1)S(1)}, u32[]{:S(2)}, u32[]{:S(2)}) collective-permute-start(bf16[32,4096]{1,0:T(8,128)(2,1)S(1)} %get-tuple-element.25), channel_id=1, source_target_pairs={{0,4},{2,6},{4,8},{6,10},{8,12},{10,14},{12,0},{14,2},{1,5},{3,7},... | collective-permute-start | bytes 786440 | tf_op jit(solution)/shard_map/ppermute | solution.py:235
  16.6 2.4 %collective-permute-start.2 = (bf16[32,4096]{1,0:T(8,128)(2,1)S(1)}, bf16[32,4096]{1,0:T(8,128)(2,1)S(1)}, u32[]{:S(2)}, u32[]{:S(2)}) collective-permute-start(bf16[32,4096]{1,0:T(8,128)(2,1)S(1)} %get-tuple-element.24), channel_id=1, source_target_pairs={{0,8},{2,10},{4,12},{6,14},{8,0},{10,2},{12,4},{14,6},{1,9},{3,11}... | collective-permute-start | bytes 786440 | tf_op jit(solution)/shard_map/ppermute | solution.py:235
  19.0 1.1 %collective-permute-start.3 = (bf16[32,4096]{1,0:T(8,128)(2,1)S(1)}, bf16[32,4096]{1,0:T(8,128)(2,1)S(1)}, u32[]{:S(2)}, u32[]{:S(2)}) collective-permute-start(bf16[32,4096]{1,0:T(8,128)(2,1)S(1)} %get-tuple-element.26), channel_id=1, source_target_pairs={{0,12},{2,14},{4,0},{6,2},{8,4},{10,6},{12,8},{14,10},{1,13},{3,15... | collective-permute-start | bytes 786440 | tf_op jit(solution)/shard_map/ppermute | solution.py:235
  20.2 5.3 %collective-permute-done.1 = bf16[32,4096]{1,0:T(8,128)(2,1)S(1)} collective-permute-done((bf16[32,4096]{1,0:T(8,128)(2,1)S(1)}, bf16[32,4096]{1,0:T(8,128)(2,1)S(1)}, u32[]{:S(2)}, u32[]{:S(2)}) %collective-permute-start.1) | collective-permute-done | bytes 262176 | tf_op jit(solution)/shard_map/ppermute | solution.py:235
  25.5 7.5 %collective-permute-done.2 = bf16[32,4096]{1,0:T(8,128)(2,1)S(1)} collective-permute-done((bf16[32,4096]{1,0:T(8,128)(2,1)S(1)}, bf16[32,4096]{1,0:T(8,128)(2,1)S(1)}, u32[]{:S(2)}, u32[]{:S(2)}) %collective-permute-start.2) | collective-permute-done | bytes 262176 | tf_op jit(solution)/shard_map/ppermute | solution.py:235
  33.0 0.0 collective-permute-done.3
  33.0 0.0 all-to-all-done.refs_0_
  33.0 0.1 slice.24
  33.1 1.2 %collective-permute-start.4 = (bf16[32,64,128]{2,1,0:T(8,128)(2,1)S(1)}, bf16[32,64,128]{2,1,0:T(8,128)(2,1)S(1)}, u32[]{:S(2)}, u32[]{:S(2)}) collective-permute-start(bf16[32,64,128]{2,1,0:T(8,128)(2,1)S(1)} %slice.24), channel_id=1, source_target_pairs={{0,4},{1,5},{16,20},{17,21},{32,36},{33,37},{48,52},{49,53},{64,68... | collective-permute-start | bytes 1572872 | tf_op jit(solution)/shard_map/ppermute | solution.py:239
  34.2 2.8 %collective-permute-start.6 = (bf16[32,64,128]{2,1,0:T(8,128)(2,1)S(1)}, bf16[32,64,128]{2,1,0:T(8,128)(2,1)S(1)}, u32[]{:S(2)}, u32[]{:S(2)}) collective-permute-start(bf16[32,64,128]{2,1,0:T(8,128)(2,1)S(1)} %slice.24), channel_id=1, source_target_pairs={{0,8},{1,9},{16,24},{17,25},{32,40},{33,41},{48,56},{49,57},{64,72... | collective-permute-start | bytes 1572872 | tf_op jit(solution)/shard_map/ppermute | solution.py:239
  37.0 1.0 %collective-permute-start.8 = (bf16[32,64,128]{2,1,0:T(8,128)(2,1)S(1)}, bf16[32,64,128]{2,1,0:T(8,128)(2,1)S(1)}, u32[]{:S(2)}, u32[]{:S(2)}) collective-permute-start(bf16[32,64,128]{2,1,0:T(8,128)(2,1)S(1)} %slice.24), channel_id=1, source_target_pairs={{0,12},{1,13},{16,28},{17,29},{32,44},{33,45},{48,60},{49,61},{64,... | collective-permute-start | bytes 1572872 | tf_op jit(solution)/shard_map/ppermute | solution.py:239
  38.0 2.4 %collective-permute-start = (bf16[32,72,128]{2,1,0:T(8,128)(2,1)S(1)}, bf16[32,72,128]{2,1,0:T(8,128)(2,1)S(1)}, u32[]{:S(2)}, u32[]{:S(2)}) collective-permute-start(bf16[32,72,128]{2,1,0:T(8,128)(2,1)S(1)} %all-to-all-done.refs_0_), channel_id=1, source_target_pairs={{0,2},{2,0},{4,6},{6,4},{8,10},{10,8},{12,14},{14,12},{1,3},{3,1},... | collective-permute-start | bytes 1769480 | tf_op jit(solution)/shard_map/ppermute | solution.py:247
  40.4 2.3 %collective-permute-done.4.refs_1_ = bf16[32,64,128]{2,1,0:T(8,128)(2,1)S(1)} collective-permute-done((bf16[32,64,128]{2,1,0:T(8,128)(2,1)S(1)}, bf16[32,64,128]{2,1,0:T(8,128)(2,1)S(1)}, u32[]{:S(2)}, u32[]{:S(2)}) %collective-permute-start.4) | collective-permute-done | bytes 524320 | tf_op jit(solution)/shard_map/ppermute | solution.py:239
  42.7 0.0 copy-start
  42.8 0.1 constant_dynamic-slice_fusion
  42.9 2.4 %collective-permute-start.10 = (bf16[128,2048]{1,0:T(8,128)(2,1)S(1)}, bf16[128,2048]{1,0:T(8,128)(2,1)S(1)}, u32[]{:S(2)}, u32[]{:S(2)}) collective-permute-start(bf16[128,2048]{1,0:T(8,128)(2,1)S(1)} %get-tuple-element.32), channel_id=1, source_target_pairs={{0,2},{2,0},{4,6},{6,4},{8,10},{10,8},{12,14},{14,12},{1,3},{3,1},... | collective-permute-start | bytes 1572872 | tf_op jit(solution)/shard_map/ppermute | solution.py:247
  45.4 0.1 collective-permute-start.5
  45.5 4.0 %collective-permute-done.6.refs_2_ = bf16[32,64,128]{2,1,0:T(8,128)(2,1)S(1)} collective-permute-done((bf16[32,64,128]{2,1,0:T(8,128)(2,1)S(1)}, bf16[32,64,128]{2,1,0:T(8,128)(2,1)S(1)}, u32[]{:S(2)}, u32[]{:S(2)}) %collective-permute-start.6) | collective-permute-done | bytes 524320 | tf_op jit(solution)/shard_map/ppermute | solution.py:239
  49.5 2.3 %collective-permute-start.7 = (bf16[32,64,128]{2,1,0:T(8,128)(2,1)S(1)}, bf16[32,64,128]{2,1,0:T(8,128)(2,1)S(1)}, u32[]{:S(2)}, u32[]{:S(2)}) collective-permute-start(bf16[32,64,128]{2,1,0:T(8,128)(2,1)S(1)} %collective-permute-done.6.refs_2_), channel_id=1, source_target_pairs={{0,2},{2,0},{4,6},{6,4},{8,10},{10,8},{12,14},{14,12},{1,3},{3,1},... | collective-permute-start | bytes 1572872 | tf_op jit(solution)/shard_map/ppermute | solution.py:247
  51.8 0.0 collective-permute-done.8.refs_3_
  51.8 0.0 collective-permute-start.9
  51.8 0.0 collective-permute-done.refs_0_
  51.8 0.0 copy-done
  51.8 1.0 %choose.1 = (bf16[16,128,256]{2,1,0:T(8,128)(2,1)S(1)}, f32[16,128,128]{2,1,0:T(8,128)S(1)}) custom-call(bf16[32,8,128]{2,1,0:T(8,128)(2,1)S(1)} %slice.32.lists_near, bf16[32,8,128]{2,1,0:T(8,128)(2,1)S(1)} %slice.33.lists_far, bf16[64,128]{1,0:T(8,128)(2,1)S(1)} %copy-done), custom_call_target="tpu_custom_call" | custom-call | flops 40000000 | bytes 2300000 | tf_op jit(solution)/shard_map/choose/pallas_call | solution.py:107
  52.9 0.8 %select_near.1.refs_8_ = f32[2,16,128,128]{3,2,1,0:T(8,128)S(1)} custom-call(bf16[32,72,128]{2,1,0:T(8,128)(2,1)S(1)} %all-to-all-done.refs_0_, bf16[32,64,128]{2,1,0:T(8,128)(2,1)S(1)} %collective-permute-done.4.refs_1_, bf16[32,64,128]{2,1,0:T(8,128)(2,1)S(1)} %collective-permute-done.6.refs_2_, bf16[32,64,128]{2,1,0:T(8,128)(2,1)S(1)} %collective-permute-done.8.refs_3_, ...), custom_call_target="tpu_custom_call" | custom-call | flops 270000000 | bytes 5300000 | tf_op jit(solution)/shard_map/select_near/pallas_call | solution.py:160
  53.7 0.0 collective-permute-done.10.refs_5_
  53.7 0.0 collective-permute-done.5.refs_1_
  53.7 0.0 collective-permute-done.7.refs_2_
  53.7 0.3 collective-permute-done.9.refs_3_
  54.0 1.8 %update.1 = (bf16[128,2048]{1,0:T(8,128)(2,1)S(1)}, bf16[128,2048]{1,0:T(8,128)(2,1)S(1)}) custom-call(bf16[32,72,128]{2,1,0:T(8,128)(2,1)S(1)} %collective-permute-done.refs_0_, bf16[32,64,128]{2,1,0:T(8,128)(2,1)S(1)} %collective-permute-done.5.refs_1_, bf16[32,64,128]{2,1,0:T(8,128)(2,1)S(1)} %collective-permute-done.7.refs_2_, ...), custom_call_target="tpu_custom_call" | custom-call | flops 800000000 | bytes 6500000 | tf_op jit(solution)/shard_map/update/pallas_call | solution.py:202
  55.8 0.6 collective-permute-start.11
  56.5 2.1 %collective-permute-start.12 = (bf16[32,2048]{1,0:T(8,128)(2,1)S(1)}, bf16[32,2048]{1,0:T(8,128)(2,1)S(1)}, u32[]{:S(2)}, u32[]{:S(2)}) collective-permute-start(bf16[32,2048]{1,0:T(8,128)(2,1)S(1)} %slice.28), channel_id=1, source_target_pairs={{0,8},{2,10},{4,12},{6,14},{8,0},{10,2},{12,4},{14,6},{1,9},{3,11}... | collective-permute-start | bytes 393224 | tf_op jit(solution)/shard_map/ppermute | solution.py:235
  58.6 0.0 collective-permute-done.11
  58.6 1.8 %collective-permute-start.13 = (bf16[32,2048]{1,0:T(8,128)(2,1)S(1)}, bf16[32,2048]{1,0:T(8,128)(2,1)S(1)}, u32[]{:S(2)}, u32[]{:S(2)}) collective-permute-start(bf16[32,2048]{1,0:T(8,128)(2,1)S(1)} %slice.34), channel_id=1, source_target_pairs={{0,8},{2,10},{4,12},{6,14},{8,0},{10,2},{12,4},{14,6},{1,9},{3,11}... | collective-permute-start | bytes 393224 | tf_op jit(solution)/shard_map/ppermute | solution.py:235
  60.4 0.1 broadcast_select_fusion.1
  60.5 0.1 broadcast_in_dim.3
  60.6 0.1 pad_maximum_fusion
  60.6 1.4 %collective-permute-start.14 = (bf16[32,4096]{1,0:T(8,128)(2,1)S(1)}, bf16[32,4096]{1,0:T(8,128)(2,1)S(1)}, u32[]{:S(2)}, u32[]{:S(2)}) collective-permute-start(bf16[32,4096]{1,0:T(8,128)(2,1)S(1)} %get-tuple-element.28), channel_id=1, source_target_pairs={{0,12},{2,14},{4,0},{6,2},{8,4},{10,6},{12,8},{14,10},{1,13},{3,15... | collective-permute-start | bytes 786440 | tf_op jit(solution)/shard_map/ppermute | solution.py:235
  62.0 0.2 collective-permute-start.15
  62.2 0.8 %collective-permute-done.12 = bf16[32,2048]{1,0:T(8,128)(2,1)S(1)} collective-permute-done((bf16[32,2048]{1,0:T(8,128)(2,1)S(1)}, bf16[32,2048]{1,0:T(8,128)(2,1)S(1)}, u32[]{:S(2)}, u32[]{:S(2)}) %collective-permute-start.12) | collective-permute-done | bytes 131104 | tf_op jit(solution)/shard_map/ppermute | solution.py:235
  63.0 2.8 %collective-permute-done.13 = bf16[32,2048]{1,0:T(8,128)(2,1)S(1)} collective-permute-done((bf16[32,2048]{1,0:T(8,128)(2,1)S(1)}, bf16[32,2048]{1,0:T(8,128)(2,1)S(1)}, u32[]{:S(2)}, u32[]{:S(2)}) %collective-permute-start.13) | collective-permute-done | bytes 131104 | tf_op jit(solution)/shard_map/ppermute | solution.py:235
  65.8 4.4 %collective-permute-done.14 = bf16[32,4096]{1,0:T(8,128)(2,1)S(1)} collective-permute-done((bf16[32,4096]{1,0:T(8,128)(2,1)S(1)}, bf16[32,4096]{1,0:T(8,128)(2,1)S(1)}, u32[]{:S(2)}, u32[]{:S(2)}) %collective-permute-start.14) | collective-permute-done | bytes 262176 | tf_op jit(solution)/shard_map/ppermute | solution.py:235
  70.3 0.0 copy-start.1
  70.3 1.0 %collective-permute-done.15 = bf16[32,4096]{1,0:T(8,128)(2,1)S(1)} collective-permute-done((bf16[32,4096]{1,0:T(8,128)(2,1)S(1)}, bf16[32,4096]{1,0:T(8,128)(2,1)S(1)}, u32[]{:S(2)}, u32[]{:S(2)}) %collective-permute-start.15) | collective-permute-done | bytes 262176 | tf_op jit(solution)/shard_map/ppermute | solution.py:235
  71.3 0.7 constant_dynamic-update-slice_fusion.4
  (12 shorter events, 0.2 us)
Async XLA Ops:
  2.0 31.0 %all-to-all-start = ((bf16[32,72,128]{2,1,0:T(8,128)(2,1)}), bf16[32,72,128]{2,1,0:T(8,128)(2,1)S(1)}, u32[]{:S(2)}, u32[]{:S(2)}) async-start(bf16[32,72,128]{2,1,0:T(8,128)(2,1)} %prepare.1), calls=%async_computation | async-start | bytes 1179648 | tf_op jit(solution)/shard_map/all_to_all | solution.py:259
  15.3 10.2 %collective-permute-start.1 = (bf16[32,4096]{1,0:T(8,128)(2,1)S(1)}, bf16[32,4096]{1,0:T(8,128)(2,1)S(1)}, u32[]{:S(2)}, u32[]{:S(2)}) collective-permute-start(bf16[32,4096]{1,0:T(8,128)(2,1)S(1)} %get-tuple-element.25), channel_id=1, source_target_pairs={{0,4},{2,6},{4,8},{6,10},{8,12},{10,14},{12,0},{14,2},{1,5},{3,7},... | collective-permute-start | bytes 786440 | tf_op jit(solution)/shard_map/ppermute | solution.py:235
  16.6 16.4 %collective-permute-start.2 = (bf16[32,4096]{1,0:T(8,128)(2,1)S(1)}, bf16[32,4096]{1,0:T(8,128)(2,1)S(1)}, u32[]{:S(2)}, u32[]{:S(2)}) collective-permute-start(bf16[32,4096]{1,0:T(8,128)(2,1)S(1)} %get-tuple-element.24), channel_id=1, source_target_pairs={{0,8},{2,10},{4,12},{6,14},{8,0},{10,2},{12,4},{14,6},{1,9},{3,11}... | collective-permute-start | bytes 786440 | tf_op jit(solution)/shard_map/ppermute | solution.py:235
  19.0 13.9 %collective-permute-start.3 = (bf16[32,4096]{1,0:T(8,128)(2,1)S(1)}, bf16[32,4096]{1,0:T(8,128)(2,1)S(1)}, u32[]{:S(2)}, u32[]{:S(2)}) collective-permute-start(bf16[32,4096]{1,0:T(8,128)(2,1)S(1)} %get-tuple-element.26), channel_id=1, source_target_pairs={{0,12},{2,14},{4,0},{6,2},{8,4},{10,6},{12,8},{14,10},{1,13},{3,15... | collective-permute-start | bytes 786440 | tf_op jit(solution)/shard_map/ppermute | solution.py:235
  33.1 9.7 %collective-permute-start.4 = (bf16[32,64,128]{2,1,0:T(8,128)(2,1)S(1)}, bf16[32,64,128]{2,1,0:T(8,128)(2,1)S(1)}, u32[]{:S(2)}, u32[]{:S(2)}) collective-permute-start(bf16[32,64,128]{2,1,0:T(8,128)(2,1)S(1)} %slice.24), channel_id=1, source_target_pairs={{0,4},{1,5},{16,20},{17,21},{32,36},{33,37},{48,52},{49,53},{64,68... | collective-permute-start | bytes 1572872 | tf_op jit(solution)/shard_map/ppermute | solution.py:239
  34.2 15.3 %collective-permute-start.6 = (bf16[32,64,128]{2,1,0:T(8,128)(2,1)S(1)}, bf16[32,64,128]{2,1,0:T(8,128)(2,1)S(1)}, u32[]{:S(2)}, u32[]{:S(2)}) collective-permute-start(bf16[32,64,128]{2,1,0:T(8,128)(2,1)S(1)} %slice.24), channel_id=1, source_target_pairs={{0,8},{1,9},{16,24},{17,25},{32,40},{33,41},{48,56},{49,57},{64,72... | collective-permute-start | bytes 1572872 | tf_op jit(solution)/shard_map/ppermute | solution.py:239
  37.0 14.7 %collective-permute-start.8 = (bf16[32,64,128]{2,1,0:T(8,128)(2,1)S(1)}, bf16[32,64,128]{2,1,0:T(8,128)(2,1)S(1)}, u32[]{:S(2)}, u32[]{:S(2)}) collective-permute-start(bf16[32,64,128]{2,1,0:T(8,128)(2,1)S(1)} %slice.24), channel_id=1, source_target_pairs={{0,12},{1,13},{16,28},{17,29},{32,44},{33,45},{48,60},{49,61},{64,... | collective-permute-start | bytes 1572872 | tf_op jit(solution)/shard_map/ppermute | solution.py:239
  38.0 13.8 %collective-permute-start = (bf16[32,72,128]{2,1,0:T(8,128)(2,1)S(1)}, bf16[32,72,128]{2,1,0:T(8,128)(2,1)S(1)}, u32[]{:S(2)}, u32[]{:S(2)}) collective-permute-start(bf16[32,72,128]{2,1,0:T(8,128)(2,1)S(1)} %all-to-all-done.refs_0_), channel_id=1, source_target_pairs={{0,2},{2,0},{4,6},{6,4},{8,10},{10,8},{12,14},{14,12},{1,3},{3,1},... | collective-permute-start | bytes 1769480 | tf_op jit(solution)/shard_map/ppermute | solution.py:247
  42.7 9.1 %copy-start = (bf16[64,128]{1,0:T(8,128)(2,1)S(1)}, bf16[64,128]{1,0:T(8,128)(2,1)}, u32[]{:S(2)}) copy-start(bf16[64,128]{1,0:T(8,128)(2,1)} %table_ref.1) | copy-start | bytes 49156
  42.9 10.7 %collective-permute-start.10 = (bf16[128,2048]{1,0:T(8,128)(2,1)S(1)}, bf16[128,2048]{1,0:T(8,128)(2,1)S(1)}, u32[]{:S(2)}, u32[]{:S(2)}) collective-permute-start(bf16[128,2048]{1,0:T(8,128)(2,1)S(1)} %get-tuple-element.32), channel_id=1, source_target_pairs={{0,2},{2,0},{4,6},{6,4},{8,10},{10,8},{12,14},{14,12},{1,3},{3,1},... | collective-permute-start | bytes 1572872 | tf_op jit(solution)/shard_map/ppermute | solution.py:247
  45.4 8.3 %collective-permute-start.5 = (bf16[32,64,128]{2,1,0:T(8,128)(2,1)S(1)}, bf16[32,64,128]{2,1,0:T(8,128)(2,1)S(1)}, u32[]{:S(2)}, u32[]{:S(2)}) collective-permute-start(bf16[32,64,128]{2,1,0:T(8,128)(2,1)S(1)} %collective-permute-done.4.refs_1_), channel_id=1, source_target_pairs={{0,2},{2,0},{4,6},{6,4},{8,10},{10,8},{12,14},{14,12},{1,3},{3,1},... | collective-permute-start | bytes 1572872 | tf_op jit(solution)/shard_map/ppermute | solution.py:247
  49.5 4.2 %collective-permute-start.7 = (bf16[32,64,128]{2,1,0:T(8,128)(2,1)S(1)}, bf16[32,64,128]{2,1,0:T(8,128)(2,1)S(1)}, u32[]{:S(2)}, u32[]{:S(2)}) collective-permute-start(bf16[32,64,128]{2,1,0:T(8,128)(2,1)S(1)} %collective-permute-done.6.refs_2_), channel_id=1, source_target_pairs={{0,2},{2,0},{4,6},{6,4},{8,10},{10,8},{12,14},{14,12},{1,3},{3,1},... | collective-permute-start | bytes 1572872 | tf_op jit(solution)/shard_map/ppermute | solution.py:247
  51.8 2.3 %collective-permute-start.9 = (bf16[32,64,128]{2,1,0:T(8,128)(2,1)S(1)}, bf16[32,64,128]{2,1,0:T(8,128)(2,1)S(1)}, u32[]{:S(2)}, u32[]{:S(2)}) collective-permute-start(bf16[32,64,128]{2,1,0:T(8,128)(2,1)S(1)} %collective-permute-done.8.refs_3_), channel_id=1, source_target_pairs={{0,2},{2,0},{4,6},{6,4},{8,10},{10,8},{12,14},{14,12},{1,3},{3,1},... | collective-permute-start | bytes 1572872 | tf_op jit(solution)/shard_map/ppermute | solution.py:247
  55.8 2.8 %collective-permute-start.11 = (bf16[128,2048]{1,0:T(8,128)(2,1)S(1)}, bf16[128,2048]{1,0:T(8,128)(2,1)S(1)}, u32[]{:S(2)}, u32[]{:S(2)}) collective-permute-start(bf16[128,2048]{1,0:T(8,128)(2,1)S(1)} %get-tuple-element.22), channel_id=1, source_target_pairs={{0,2},{2,0},{4,6},{6,4},{8,10},{10,8},{12,14},{14,12},{1,3},{3,1},... | collective-permute-start | bytes 1572872 | tf_op jit(solution)/shard_map/ppermute | solution.py:247
  56.5 6.5 %collective-permute-start.12 = (bf16[32,2048]{1,0:T(8,128)(2,1)S(1)}, bf16[32,2048]{1,0:T(8,128)(2,1)S(1)}, u32[]{:S(2)}, u32[]{:S(2)}) collective-permute-start(bf16[32,2048]{1,0:T(8,128)(2,1)S(1)} %slice.28), channel_id=1, source_target_pairs={{0,8},{2,10},{4,12},{6,14},{8,0},{10,2},{12,4},{14,6},{1,9},{3,11}... | collective-permute-start | bytes 393224 | tf_op jit(solution)/shard_map/ppermute | solution.py:235
  58.6 7.2 %collective-permute-start.13 = (bf16[32,2048]{1,0:T(8,128)(2,1)S(1)}, bf16[32,2048]{1,0:T(8,128)(2,1)S(1)}, u32[]{:S(2)}, u32[]{:S(2)}) collective-permute-start(bf16[32,2048]{1,0:T(8,128)(2,1)S(1)} %slice.34), channel_id=1, source_target_pairs={{0,8},{2,10},{4,12},{6,14},{8,0},{10,2},{12,4},{14,6},{1,9},{3,11}... | collective-permute-start | bytes 393224 | tf_op jit(solution)/shard_map/ppermute | solution.py:235
  60.6 9.6 %collective-permute-start.14 = (bf16[32,4096]{1,0:T(8,128)(2,1)S(1)}, bf16[32,4096]{1,0:T(8,128)(2,1)S(1)}, u32[]{:S(2)}, u32[]{:S(2)}) collective-permute-start(bf16[32,4096]{1,0:T(8,128)(2,1)S(1)} %get-tuple-element.28), channel_id=1, source_target_pairs={{0,12},{2,14},{4,0},{6,2},{8,4},{10,6},{12,8},{14,10},{1,13},{3,15... | collective-permute-start | bytes 786440 | tf_op jit(solution)/shard_map/ppermute | solution.py:235
  62.0 9.3 %collective-permute-start.15 = (bf16[32,4096]{1,0:T(8,128)(2,1)S(1)}, bf16[32,4096]{1,0:T(8,128)(2,1)S(1)}, u32[]{:S(2)}, u32[]{:S(2)}) collective-permute-start(bf16[32,4096]{1,0:T(8,128)(2,1)S(1)} %get-tuple-element.27), channel_id=1, source_target_pairs={{0,4},{2,6},{4,8},{6,10},{8,12},{10,14},{12,0},{14,2},{1,5},{3,7},... | collective-permute-start | bytes 786440 | tf_op jit(solution)/shard_map/ppermute | solution.py:235
  70.3 1.0 %copy-start.1 = (bf16[32,16384]{1,0:T(8,128)(2,1)}, bf16[32,16384]{1,0:T(8,128)(2,1)S(1)}, u32[]{:S(2)}) copy-start(bf16[32,16384]{1,0:T(8,128)(2,1)S(1)} %constant_dynamic-update-slice_fusion.5) | copy-start | bytes 3145732

commit v8 on v7

--- a/solution.py
+++ b/solution.py
@@ -295,9 +295,9 @@
     out = place(out, new[:mem_dev], 0, 0)
     backs = [to_x(new[s * mem_dev : (s + 1) * mem_dev], -s) for s in (1, 3)]
     out = place(out, near2, 2, me_core * own_cells)
-    out = place(out, far2, 2, (1 - me_core) * own_cells)
     out = place(out, backs[0], 1, 0)
-    return place(out, backs[1], 3, 0)
+    out = place(out, backs[1], 3, 0)
+    return place(out, far2, 2, (1 - me_core) * own_cells)
 
 
 def solution(mesh):

time: 72.7 us -> 73.1 us (level)
  no operation moved by 1% of the time
where the time goes in v8:
time: 73.1 us; the launch traced here: 72.1 us
  starting transfers between devices  35.1 us (48%)
  waiting for transfers between devices  28.6 us (39%)
  Pallas kernels  5.64 us (8%)
  local copies, waits for them, and re-layouts  2.35 us (3%)
    ppermute x7, waiting for transfers between devices, to_x(): return lax.ppermute(piece, 'mem', X_SHIFT[s % X])  22 us
    all_to_all x1, starting transfers between devices, local(): lax.all_to_all(sent, EVERY, 0, 0, tiled=True, axis_index_groups=PLANES)  11.9 us
    ppermute x7, starting transfers between devices, to_x(): return lax.ppermute(piece, 'mem', X_SHIFT[s % X])  10.4 us
    ppermute x6, starting transfers between devices, swap(): return lax.ppermute(piece, 'mem', CORE_SWAP)  7.85 us
    ppermute x3, waiting for transfers between devices, cross(): return lax.ppermute(piece, EVERY, CROSS[s % X])  6.3 us
    ppermute x3, starting transfers between devices, cross(): return lax.ppermute(piece, EVERY, CROSS[s % X])  4.96 us
    pallas_call x1, Pallas kernels, prepare(): pl.pallas_call(prepare_kernel, out_shape=jax.ShapeDtypeStruct((GROUPS, 2...  2.03 us
    pallas_call x1, Pallas kernels, run_update(): pl.pallas_call(update_kernel, out_shape=[jax.ShapeDtypeStruct(near.shape,...  1.75 us
  transfers between devices with their start and end apart: 17, of which 9 were waited for; matrix products, arithmetic and copies ran while one was open for 2% of the time, Pallas kernels for 3%

profile of v8, /device:TPU:1, one launch (start us, length us, event | category | flops | bytes accessed | tf_op | source)
XLA Modules:
  0.0 72.1 jit_solution(4391839884187204049)
XLA Ops:
  0.0 2.0 %prepare.1 = bf16[32,72,128]{2,1,0:T(8,128)(2,1)} custom-call(bf16[32,128]{1,0:T(8,128)(2,1)} %anom_hbm.1, bf16[32,128]{1,0:T(8,128)(2,1)} %innov_hbm.1, s32[4,4096]{1,0:T(4,128)} %seg_hbm.1, s32[4,4096]{1,0:T(4,128)} %prof_hbm.1), custom_call_target="tpu_custom_call" | custom-call | flops 10000000 | bytes 400000 | tf_op jit(solution)/shard_map/prepare/pallas_call | solution.py:54
  2.0 11.9 %all-to-all-start = ((bf16[32,72,128]{2,1,0:T(8,128)(2,1)}), bf16[32,72,128]{2,1,0:T(8,128)(2,1)S(1)}, u32[]{:S(2)}, u32[]{:S(2)}) async-start(bf16[32,72,128]{2,1,0:T(8,128)(2,1)} %prepare.1), calls=%async_computation | async-start | bytes 1179648 | tf_op jit(solution)/shard_map/all_to_all | solution.py:259
  14.0 1.3 %constant_dynamic-slice_fusion.2 = (bf16[32,4096]{1,0:T(8,128)(2,1)S(1)}, bf16[32,4096]{1,0:T(8,128)(2,1)S(1)}, bf16[32,4096]{1,0:T(8,128)(2,1)S(1)}, bf16[32,4096]{1,0:T(8,128)(2,1)S(1)}) fusion(bf16[32,32768]{1,0:T(8,128)(2,1)} %param.6, s32[]{:T(128)S(6)} %select_n.92, s32[]{:T(128)S(6)} %select_n.88, s32[]{:T(128)S(6)} %select_n.86, s32[]{:T(128)S(6)} %select_n.90), kind=kLoop, calls=%fused_computation.15 | loop fusion | bytes 2097168 | tf_op jit(solution)/shard_map/dynamic_slice | solution.py:263
  15.3 1.3 %collective-permute-start.1 = (bf16[32,4096]{1,0:T(8,128)(2,1)S(1)}, bf16[32,4096]{1,0:T(8,128)(2,1)S(1)}, u32[]{:S(2)}, u32[]{:S(2)}) collective-permute-start(bf16[32,4096]{1,0:T(8,128)(2,1)S(1)} %get-tuple-element.25), channel_id=1, source_target_pairs={{0,4},{2,6},{4,8},{6,10},{8,12},{10,14},{12,0},{14,2},{1,5},{3,7},... | collective-permute-start | bytes 786440 | tf_op jit(solution)/shard_map/ppermute | solution.py:235
  16.6 2.4 %collective-permute-start.2 = (bf16[32,4096]{1,0:T(8,128)(2,1)S(1)}, bf16[32,4096]{1,0:T(8,128)(2,1)S(1)}, u32[]{:S(2)}, u32[]{:S(2)}) collective-permute-start(bf16[32,4096]{1,0:T(8,128)(2,1)S(1)} %get-tuple-element.24), channel_id=1, source_target_pairs={{0,8},{2,10},{4,12},{6,14},{8,0},{10,2},{12,4},{14,6},{1,9},{3,11}... | collective-permute-start | bytes 786440 | tf_op jit(solution)/shard_map/ppermute | solution.py:235
  19.0 1.1 %collective-permute-start.3 = (bf16[32,4096]{1,0:T(8,128)(2,1)S(1)}, bf16[32,4096]{1,0:T(8,128)(2,1)S(1)}, u32[]{:S(2)}, u32[]{:S(2)}) collective-permute-start(bf16[32,4096]{1,0:T(8,128)(2,1)S(1)} %get-tuple-element.26), channel_id=1, source_target_pairs={{0,12},{2,14},{4,0},{6,2},{8,4},{10,6},{12,8},{14,10},{1,13},{3,15... | collective-permute-start | bytes 786440 | tf_op jit(solution)/shard_map/ppermute | solution.py:235
  20.2 5.3 %collective-permute-done.1 = bf16[32,4096]{1,0:T(8,128)(2,1)S(1)} collective-permute-done((bf16[32,4096]{1,0:T(8,128)(2,1)S(1)}, bf16[32,4096]{1,0:T(8,128)(2,1)S(1)}, u32[]{:S(2)}, u32[]{:S(2)}) %collective-permute-start.1) | collective-permute-done | bytes 262176 | tf_op jit(solution)/shard_map/ppermute | solution.py:235
  25.5 7.5 %collective-permute-done.2 = bf16[32,4096]{1,0:T(8,128)(2,1)S(1)} collective-permute-done((bf16[32,4096]{1,0:T(8,128)(2,1)S(1)}, bf16[32,4096]{1,0:T(8,128)(2,1)S(1)}, u32[]{:S(2)}, u32[]{:S(2)}) %collective-permute-start.2) | collective-permute-done | bytes 262176 | tf_op jit(solution)/shard_map/ppermute | solution.py:235
  33.0 0.0 collective-permute-done.3
  33.0 0.0 all-to-all-done.refs_0_
  33.0 0.1 slice.24
  33.1 1.2 %collective-permute-start.4 = (bf16[32,64,128]{2,1,0:T(8,128)(2,1)S(1)}, bf16[32,64,128]{2,1,0:T(8,128)(2,1)S(1)}, u32[]{:S(2)}, u32[]{:S(2)}) collective-permute-start(bf16[32,64,128]{2,1,0:T(8,128)(2,1)S(1)} %slice.24), channel_id=1, source_target_pairs={{0,4},{1,5},{16,20},{17,21},{32,36},{33,37},{48,52},{49,53},{64,68... | collective-permute-start | bytes 1572872 | tf_op jit(solution)/shard_map/ppermute | solution.py:239
  34.2 2.8 %collective-permute-start.6 = (bf16[32,64,128]{2,1,0:T(8,128)(2,1)S(1)}, bf16[32,64,128]{2,1,0:T(8,128)(2,1)S(1)}, u32[]{:S(2)}, u32[]{:S(2)}) collective-permute-start(bf16[32,64,128]{2,1,0:T(8,128)(2,1)S(1)} %slice.24), channel_id=1, source_target_pairs={{0,8},{1,9},{16,24},{17,25},{32,40},{33,41},{48,56},{49,57},{64,72... | collective-permute-start | bytes 1572872 | tf_op jit(solution)/shard_map/ppermute | solution.py:239
  37.0 1.0 %collective-permute-start.8 = (bf16[32,64,128]{2,1,0:T(8,128)(2,1)S(1)}, bf16[32,64,128]{2,1,0:T(8,128)(2,1)S(1)}, u32[]{:S(2)}, u32[]{:S(2)}) collective-permute-start(bf16[32,64,128]{2,1,0:T(8,128)(2,1)S(1)} %slice.24), channel_id=1, source_target_pairs={{0,12},{1,13},{16,28},{17,29},{32,44},{33,45},{48,60},{49,61},{64,... | collective-permute-start | bytes 1572872 | tf_op jit(solution)/shard_map/ppermute | solution.py:239
  38.0 2.4 %collective-permute-start = (bf16[32,72,128]{2,1,0:T(8,128)(2,1)S(1)}, bf16[32,72,128]{2,1,0:T(8,128)(2,1)S(1)}, u32[]{:S(2)}, u32[]{:S(2)}) collective-permute-start(bf16[32,72,128]{2,1,0:T(8,128)(2,1)S(1)} %all-to-all-done.refs_0_), channel_id=1, source_target_pairs={{0,2},{2,0},{4,6},{6,4},{8,10},{10,8},{12,14},{14,12},{1,3},{3,1},... | collective-permute-start | bytes 1769480 | tf_op jit(solution)/shard_map/ppermute | solution.py:247
  40.4 2.3 %collective-permute-done.4.refs_1_ = bf16[32,64,128]{2,1,0:T(8,128)(2,1)S(1)} collective-permute-done((bf16[32,64,128]{2,1,0:T(8,128)(2,1)S(1)}, bf16[32,64,128]{2,1,0:T(8,128)(2,1)S(1)}, u32[]{:S(2)}, u32[]{:S(2)}) %collective-permute-start.4) | collective-permute-done | bytes 524320 | tf_op jit(solution)/shard_map/ppermute | solution.py:239
  42.7 0.0 copy-start
  42.8 0.1 constant_dynamic-slice_fusion
  42.9 2.4 %collective-permute-start.10 = (bf16[128,2048]{1,0:T(8,128)(2,1)S(1)}, bf16[128,2048]{1,0:T(8,128)(2,1)S(1)}, u32[]{:S(2)}, u32[]{:S(2)}) collective-permute-start(bf16[128,2048]{1,0:T(8,128)(2,1)S(1)} %get-tuple-element.32), channel_id=1, source_target_pairs={{0,2},{2,0},{4,6},{6,4},{8,10},{10,8},{12,14},{14,12},{1,3},{3,1},... | collective-permute-start | bytes 1572872 | tf_op jit(solution)/shard_map/ppermute | solution.py:247
  45.4 0.1 collective-permute-start.5
  45.5 4.0 %collective-permute-done.6.refs_2_ = bf16[32,64,128]{2,1,0:T(8,128)(2,1)S(1)} collective-permute-done((bf16[32,64,128]{2,1,0:T(8,128)(2,1)S(1)}, bf16[32,64,128]{2,1,0:T(8,128)(2,1)S(1)}, u32[]{:S(2)}, u32[]{:S(2)}) %collective-permute-start.6) | collective-permute-done | bytes 524320 | tf_op jit(solution)/shard_map/ppermute | solution.py:239
  49.5 2.3 %collective-permute-start.7 = (bf16[32,64,128]{2,1,0:T(8,128)(2,1)S(1)}, bf16[32,64,128]{2,1,0:T(8,128)(2,1)S(1)}, u32[]{:S(2)}, u32[]{:S(2)}) collective-permute-start(bf16[32,64,128]{2,1,0:T(8,128)(2,1)S(1)} %collective-permute-done.6.refs_2_), channel_id=1, source_target_pairs={{0,2},{2,0},{4,6},{6,4},{8,10},{10,8},{12,14},{14,12},{1,3},{3,1},... | collective-permute-start | bytes 1572872 | tf_op jit(solution)/shard_map/ppermute | solution.py:247
  51.8 0.0 collective-permute-done.8.refs_3_
  51.8 0.0 collective-permute-start.9
  51.8 0.0 collective-permute-done.refs_0_
  51.8 0.0 copy-done
  51.8 1.0 %choose.1 = (bf16[16,128,256]{2,1,0:T(8,128)(2,1)S(1)}, f32[16,128,128]{2,1,0:T(8,128)S(1)}) custom-call(bf16[32,8,128]{2,1,0:T(8,128)(2,1)S(1)} %slice.32.lists_near, bf16[32,8,128]{2,1,0:T(8,128)(2,1)S(1)} %slice.33.lists_far, bf16[64,128]{1,0:T(8,128)(2,1)S(1)} %copy-done), custom_call_target="tpu_custom_call" | custom-call | flops 40000000 | bytes 2300000 | tf_op jit(solution)/shard_map/choose/pallas_call | solution.py:107
  52.9 0.8 %select_near.1.refs_8_ = f32[2,16,128,128]{3,2,1,0:T(8,128)S(1)} custom-call(bf16[32,72,128]{2,1,0:T(8,128)(2,1)S(1)} %all-to-all-done.refs_0_, bf16[32,64,128]{2,1,0:T(8,128)(2,1)S(1)} %collective-permute-done.4.refs_1_, bf16[32,64,128]{2,1,0:T(8,128)(2,1)S(1)} %collective-permute-done.6.refs_2_, bf16[32,64,128]{2,1,0:T(8,128)(2,1)S(1)} %collective-permute-done.8.refs_3_, ...), custom_call_target="tpu_custom_call" | custom-call | flops 270000000 | bytes 5300000 | tf_op jit(solution)/shard_map/select_near/pallas_call | solution.py:160
  53.7 0.0 collective-permute-done.10.refs_5_
  53.7 0.0 collective-permute-done.5.refs_1_
  53.7 0.0 collective-permute-done.7.refs_2_
  53.7 0.3 collective-permute-done.9.refs_3_
  54.0 1.8 %update.1 = (bf16[128,2048]{1,0:T(8,128)(2,1)S(1)}, bf16[128,2048]{1,0:T(8,128)(2,1)S(1)}) custom-call(bf16[32,72,128]{2,1,0:T(8,128)(2,1)S(1)} %collective-permute-done.refs_0_, bf16[32,64,128]{2,1,0:T(8,128)(2,1)S(1)} %collective-permute-done.5.refs_1_, bf16[32,64,128]{2,1,0:T(8,128)(2,1)S(1)} %collective-permute-done.7.refs_2_, ...), custom_call_target="tpu_custom_call" | custom-call | flops 800000000 | bytes 6500000 | tf_op jit(solution)/shard_map/update/pallas_call | solution.py:202
  55.8 0.6 collective-permute-start.11
  56.5 2.1 %collective-permute-start.12 = (bf16[32,2048]{1,0:T(8,128)(2,1)S(1)}, bf16[32,2048]{1,0:T(8,128)(2,1)S(1)}, u32[]{:S(2)}, u32[]{:S(2)}) collective-permute-start(bf16[32,2048]{1,0:T(8,128)(2,1)S(1)} %slice.28), channel_id=1, source_target_pairs={{0,8},{2,10},{4,12},{6,14},{8,0},{10,2},{12,4},{14,6},{1,9},{3,11}... | collective-permute-start | bytes 393224 | tf_op jit(solution)/shard_map/ppermute | solution.py:235
  58.5 0.0 collective-permute-done.11
  58.5 0.1 broadcast_select_fusion.1
  58.6 0.1 broadcast_in_dim.3
  58.7 0.1 pad_maximum_fusion
  58.8 1.4 %collective-permute-start.13 = (bf16[32,4096]{1,0:T(8,128)(2,1)S(1)}, bf16[32,4096]{1,0:T(8,128)(2,1)S(1)}, u32[]{:S(2)}, u32[]{:S(2)}) collective-permute-start(bf16[32,4096]{1,0:T(8,128)(2,1)S(1)} %get-tuple-element.28), channel_id=1, source_target_pairs={{0,12},{2,14},{4,0},{6,2},{8,4},{10,6},{12,8},{14,10},{1,13},{3,15... | collective-permute-start | bytes 786440 | tf_op jit(solution)/shard_map/ppermute | solution.py:235
  60.1 0.2 collective-permute-start.14
  60.3 1.9 %collective-permute-start.15 = (bf16[32,2048]{1,0:T(8,128)(2,1)S(1)}, bf16[32,2048]{1,0:T(8,128)(2,1)S(1)}, u32[]{:S(2)}, u32[]{:S(2)}) collective-permute-start(bf16[32,2048]{1,0:T(8,128)(2,1)S(1)} %slice.34), channel_id=1, source_target_pairs={{0,8},{2,10},{4,12},{6,14},{8,0},{10,2},{12,4},{14,6},{1,9},{3,11}... | collective-permute-start | bytes 393224 | tf_op jit(solution)/shard_map/ppermute | solution.py:235
  62.2 0.8 %collective-permute-done.12 = bf16[32,2048]{1,0:T(8,128)(2,1)S(1)} collective-permute-done((bf16[32,2048]{1,0:T(8,128)(2,1)S(1)}, bf16[32,2048]{1,0:T(8,128)(2,1)S(1)}, u32[]{:S(2)}, u32[]{:S(2)}) %collective-permute-start.12) | collective-permute-done | bytes 131104 | tf_op jit(solution)/shard_map/ppermute | solution.py:235
  63.0 4.3 %collective-permute-done.13 = bf16[32,4096]{1,0:T(8,128)(2,1)S(1)} collective-permute-done((bf16[32,4096]{1,0:T(8,128)(2,1)S(1)}, bf16[32,4096]{1,0:T(8,128)(2,1)S(1)}, u32[]{:S(2)}, u32[]{:S(2)}) %collective-permute-start.13) | collective-permute-done | bytes 262176 | tf_op jit(solution)/shard_map/ppermute | solution.py:235
  67.4 0.7 %collective-permute-done.14 = bf16[32,4096]{1,0:T(8,128)(2,1)S(1)} collective-permute-done((bf16[32,4096]{1,0:T(8,128)(2,1)S(1)}, bf16[32,4096]{1,0:T(8,128)(2,1)S(1)}, u32[]{:S(2)}, u32[]{:S(2)}) %collective-permute-start.14) | collective-permute-done | bytes 262176 | tf_op jit(solution)/shard_map/ppermute | solution.py:235
  68.2 0.0 copy-start.1
  68.2 3.3 %collective-permute-done.15 = bf16[32,2048]{1,0:T(8,128)(2,1)S(1)} collective-permute-done((bf16[32,2048]{1,0:T(8,128)(2,1)S(1)}, bf16[32,2048]{1,0:T(8,128)(2,1)S(1)}, u32[]{:S(2)}, u32[]{:S(2)}) %collective-permute-start.15) | collective-permute-done | bytes 131104 | tf_op jit(solution)/shard_map/ppermute | solution.py:235
  71.4 0.7 constant_dynamic-update-slice_fusion.4
  (12 shorter events, 0.2 us)
Async XLA Ops:
  2.0 31.0 %all-to-all-start = ((bf16[32,72,128]{2,1,0:T(8,128)(2,1)}), bf16[32,72,128]{2,1,0:T(8,128)(2,1)S(1)}, u32[]{:S(2)}, u32[]{:S(2)}) async-start(bf16[32,72,128]{2,1,0:T(8,128)(2,1)} %prepare.1), calls=%async_computation | async-start | bytes 1179648 | tf_op jit(solution)/shard_map/all_to_all | solution.py:259
  15.3 10.2 %collective-permute-start.1 = (bf16[32,4096]{1,0:T(8,128)(2,1)S(1)}, bf16[32,4096]{1,0:T(8,128)(2,1)S(1)}, u32[]{:S(2)}, u32[]{:S(2)}) collective-permute-start(bf16[32,4096]{1,0:T(8,128)(2,1)S(1)} %get-tuple-element.25), channel_id=1, source_target_pairs={{0,4},{2,6},{4,8},{6,10},{8,12},{10,14},{12,0},{14,2},{1,5},{3,7},... | collective-permute-start | bytes 786440 | tf_op jit(solution)/shard_map/ppermute | solution.py:235
  16.6 16.4 %collective-permute-start.2 = (bf16[32,4096]{1,0:T(8,128)(2,1)S(1)}, bf16[32,4096]{1,0:T(8,128)(2,1)S(1)}, u32[]{:S(2)}, u32[]{:S(2)}) collective-permute-start(bf16[32,4096]{1,0:T(8,128)(2,1)S(1)} %get-tuple-element.24), channel_id=1, source_target_pairs={{0,8},{2,10},{4,12},{6,14},{8,0},{10,2},{12,4},{14,6},{1,9},{3,11}... | collective-permute-start | bytes 786440 | tf_op jit(solution)/shard_map/ppermute | solution.py:235
  19.0 13.9 %collective-permute-start.3 = (bf16[32,4096]{1,0:T(8,128)(2,1)S(1)}, bf16[32,4096]{1,0:T(8,128)(2,1)S(1)}, u32[]{:S(2)}, u32[]{:S(2)}) collective-permute-start(bf16[32,4096]{1,0:T(8,128)(2,1)S(1)} %get-tuple-element.26), channel_id=1, source_target_pairs={{0,12},{2,14},{4,0},{6,2},{8,4},{10,6},{12,8},{14,10},{1,13},{3,15... | collective-permute-start | bytes 786440 | tf_op jit(solution)/shard_map/ppermute | solution.py:235
  33.1 9.7 %collective-permute-start.4 = (bf16[32,64,128]{2,1,0:T(8,128)(2,1)S(1)}, bf16[32,64,128]{2,1,0:T(8,128)(2,1)S(1)}, u32[]{:S(2)}, u32[]{:S(2)}) collective-permute-start(bf16[32,64,128]{2,1,0:T(8,128)(2,1)S(1)} %slice.24), channel_id=1, source_target_pairs={{0,4},{1,5},{16,20},{17,21},{32,36},{33,37},{48,52},{49,53},{64,68... | collective-permute-start | bytes 1572872 | tf_op jit(solution)/shard_map/ppermute | solution.py:239
  34.2 15.3 %collective-permute-start.6 = (bf16[32,64,128]{2,1,0:T(8,128)(2,1)S(1)}, bf16[32,64,128]{2,1,0:T(8,128)(2,1)S(1)}, u32[]{:S(2)}, u32[]{:S(2)}) collective-permute-start(bf16[32,64,128]{2,1,0:T(8,128)(2,1)S(1)} %slice.24), channel_id=1, source_target_pairs={{0,8},{1,9},{16,24},{17,25},{32,40},{33,41},{48,56},{49,57},{64,72... | collective-permute-start | bytes 1572872 | tf_op jit(solution)/shard_map/ppermute | solution.py:239
  37.0 14.7 %collective-permute-start.8 = (bf16[32,64,128]{2,1,0:T(8,128)(2,1)S(1)}, bf16[32,64,128]{2,1,0:T(8,128)(2,1)S(1)}, u32[]{:S(2)}, u32[]{:S(2)}) collective-permute-start(bf16[32,64,128]{2,1,0:T(8,128)(2,1)S(1)} %slice.24), channel_id=1, source_target_pairs={{0,12},{1,13},{16,28},{17,29},{32,44},{33,45},{48,60},{49,61},{64,... | collective-permute-start | bytes 1572872 | tf_op jit(solution)/shard_map/ppermute | solution.py:239
  38.0 13.8 %collective-permute-start = (bf16[32,72,128]{2,1,0:T(8,128)(2,1)S(1)}, bf16[32,72,128]{2,1,0:T(8,128)(2,1)S(1)}, u32[]{:S(2)}, u32[]{:S(2)}) collective-permute-start(bf16[32,72,128]{2,1,0:T(8,128)(2,1)S(1)} %all-to-all-done.refs_0_), channel_id=1, source_target_pairs={{0,2},{2,0},{4,6},{6,4},{8,10},{10,8},{12,14},{14,12},{1,3},{3,1},... | collective-permute-start | bytes 1769480 | tf_op jit(solution)/shard_map/ppermute | solution.py:247
  42.7 9.1 %copy-start = (bf16[64,128]{1,0:T(8,128)(2,1)S(1)}, bf16[64,128]{1,0:T(8,128)(2,1)}, u32[]{:S(2)}) copy-start(bf16[64,128]{1,0:T(8,128)(2,1)} %table_ref.1) | copy-start | bytes 49156
  42.9 10.7 %collective-permute-start.10 = (bf16[128,2048]{1,0:T(8,128)(2,1)S(1)}, bf16[128,2048]{1,0:T(8,128)(2,1)S(1)}, u32[]{:S(2)}, u32[]{:S(2)}) collective-permute-start(bf16[128,2048]{1,0:T(8,128)(2,1)S(1)} %get-tuple-element.32), channel_id=1, source_target_pairs={{0,2},{2,0},{4,6},{6,4},{8,10},{10,8},{12,14},{14,12},{1,3},{3,1},... | collective-permute-start | bytes 1572872 | tf_op jit(solution)/shard_map/ppermute | solution.py:247
  45.4 8.3 %collective-permute-start.5 = (bf16[32,64,128]{2,1,0:T(8,128)(2,1)S(1)}, bf16[32,64,128]{2,1,0:T(8,128)(2,1)S(1)}, u32[]{:S(2)}, u32[]{:S(2)}) collective-permute-start(bf16[32,64,128]{2,1,0:T(8,128)(2,1)S(1)} %collective-permute-done.4.refs_1_), channel_id=1, source_target_pairs={{0,2},{2,0},{4,6},{6,4},{8,10},{10,8},{12,14},{14,12},{1,3},{3,1},... | collective-permute-start | bytes 1572872 | tf_op jit(solution)/shard_map/ppermute | solution.py:247
  49.5 4.2 %collective-permute-start.7 = (bf16[32,64,128]{2,1,0:T(8,128)(2,1)S(1)}, bf16[32,64,128]{2,1,0:T(8,128)(2,1)S(1)}, u32[]{:S(2)}, u32[]{:S(2)}) collective-permute-start(bf16[32,64,128]{2,1,0:T(8,128)(2,1)S(1)} %collective-permute-done.6.refs_2_), channel_id=1, source_target_pairs={{0,2},{2,0},{4,6},{6,4},{8,10},{10,8},{12,14},{14,12},{1,3},{3,1},... | collective-permute-start | bytes 1572872 | tf_op jit(solution)/shard_map/ppermute | solution.py:247
  51.8 2.3 %collective-permute-start.9 = (bf16[32,64,128]{2,1,0:T(8,128)(2,1)S(1)}, bf16[32,64,128]{2,1,0:T(8,128)(2,1)S(1)}, u32[]{:S(2)}, u32[]{:S(2)}) collective-permute-start(bf16[32,64,128]{2,1,0:T(8,128)(2,1)S(1)} %collective-permute-done.8.refs_3_), channel_id=1, source_target_pairs={{0,2},{2,0},{4,6},{6,4},{8,10},{10,8},{12,14},{14,12},{1,3},{3,1},... | collective-permute-start | bytes 1572872 | tf_op jit(solution)/shard_map/ppermute | solution.py:247
  55.8 2.7 %collective-permute-start.11 = (bf16[128,2048]{1,0:T(8,128)(2,1)S(1)}, bf16[128,2048]{1,0:T(8,128)(2,1)S(1)}, u32[]{:S(2)}, u32[]{:S(2)}) collective-permute-start(bf16[128,2048]{1,0:T(8,128)(2,1)S(1)} %get-tuple-element.22), channel_id=1, source_target_pairs={{0,2},{2,0},{4,6},{6,4},{8,10},{10,8},{12,14},{14,12},{1,3},{3,1},... | collective-permute-start | bytes 1572872 | tf_op jit(solution)/shard_map/ppermute | solution.py:247
  56.5 6.5 %collective-permute-start.12 = (bf16[32,2048]{1,0:T(8,128)(2,1)S(1)}, bf16[32,2048]{1,0:T(8,128)(2,1)S(1)}, u32[]{:S(2)}, u32[]{:S(2)}) collective-permute-start(bf16[32,2048]{1,0:T(8,128)(2,1)S(1)} %slice.28), channel_id=1, source_target_pairs={{0,8},{2,10},{4,12},{6,14},{8,0},{10,2},{12,4},{14,6},{1,9},{3,11}... | collective-permute-start | bytes 393224 | tf_op jit(solution)/shard_map/ppermute | solution.py:235
  58.8 8.6 %collective-permute-start.13 = (bf16[32,4096]{1,0:T(8,128)(2,1)S(1)}, bf16[32,4096]{1,0:T(8,128)(2,1)S(1)}, u32[]{:S(2)}, u32[]{:S(2)}) collective-permute-start(bf16[32,4096]{1,0:T(8,128)(2,1)S(1)} %get-tuple-element.28), channel_id=1, source_target_pairs={{0,12},{2,14},{4,0},{6,2},{8,4},{10,6},{12,8},{14,10},{1,13},{3,15... | collective-permute-start | bytes 786440 | tf_op jit(solution)/shard_map/ppermute | solution.py:235
  60.1 8.0 %collective-permute-start.14 = (bf16[32,4096]{1,0:T(8,128)(2,1)S(1)}, bf16[32,4096]{1,0:T(8,128)(2,1)S(1)}, u32[]{:S(2)}, u32[]{:S(2)}) collective-permute-start(bf16[32,4096]{1,0:T(8,128)(2,1)S(1)} %get-tuple-element.27), channel_id=1, source_target_pairs={{0,4},{2,6},{4,8},{6,10},{8,12},{10,14},{12,0},{14,2},{1,5},{3,7},... | collective-permute-start | bytes 786440 | tf_op jit(solution)/shard_map/ppermute | solution.py:235
  60.3 11.1 %collective-permute-start.15 = (bf16[32,2048]{1,0:T(8,128)(2,1)S(1)}, bf16[32,2048]{1,0:T(8,128)(2,1)S(1)}, u32[]{:S(2)}, u32[]{:S(2)}) collective-permute-start(bf16[32,2048]{1,0:T(8,128)(2,1)S(1)} %slice.34), channel_id=1, source_target_pairs={{0,8},{2,10},{4,12},{6,14},{8,0},{10,2},{12,4},{14,6},{1,9},{3,11}... | collective-permute-start | bytes 393224 | tf_op jit(solution)/shard_map/ppermute | solution.py:235
  68.2 3.3 %copy-start.1 = (bf16[32,16384]{1,0:T(8,128)(2,1)}, bf16[32,16384]{1,0:T(8,128)(2,1)S(1)}, u32[]{:S(2)}) copy-start(bf16[32,16384]{1,0:T(8,128)(2,1)S(1)} %constant_dynamic-update-slice_fusion.5) | copy-start | bytes 3145732
